TPU v7x, 32 devices: a whole 2x2x4 slice. The times are simulated.
32 devices in a mesh: dp: 8 (over z, core), expert: 4 (over y, x).
Axes of the slice: x: 2, y: 2, z: 4, core: 2. Of those that a mesh axis runs over, the one named last changes fastest.
Arguments:
- tokens: bfloat16 [4096, 4096], P(('dp', 'expert')), may hold values from -6 to 6
- expert_ids: int32 [4096, 2], P(('dp', 'expert')), may hold values from 0 to 3, all different within a row; in each aligned block of 128 rows (0 to 127, 128 to 255, ...) at most 80 rows name the same one
- gate_probs: float32 [4096, 2], P(('dp', 'expert')), may hold values from 0.2 to 1
- gate_weight: bfloat16 [4, 4096, 1536], P('expert', 'dp'), may hold values from -0.09375 to 0.09375
- up_weight: bfloat16 [4, 4096, 1536], P('expert', 'dp'), may hold values from -0.09375 to 0.09375
- down_weight: bfloat16 [4, 1536, 4096], P('expert', None, 'dp'), may hold values from -0.15625 to 0.15625
Outputs:
- mixed: bfloat16 [4096, 4096], P(('dp', 'expert'))
Inputs may be any that keep to these rules, and one draw needn't show every extreme that they name: `expert_ids`: each token names 2 different experts. Among the 128 tokens of one device (aligned blocks of rows), no expert is named by more than 80 tokens, and in every draw some expert is named by exactly 80 tokens of some device.
All inputs are finite; a program needn't handle non-finite values.
Results may differ from a plain program's by a relative error of at most 0.0057.
Values may be sent and summed in bfloat16 or wider, within the bound.
No kernel may reach another device: no remote copies, remote signals or barrier semaphores. Data moves between devices by JAX's collectives and lax.ppermute only.
A program may use at most 128 MiB of HBM per device.

v0:
```python
import jax
import jax.numpy as jnp
from jax import lax
from jax.sharding import PartitionSpec as P

CAP = 80


def on_device(tokens, expert_ids, gate_probs, gate_weight, up_weight, down_weight):
    tok_count, model_width = tokens.shape
    top_count = expert_ids.shape[1]
    groups = lax.axis_size("expert")
    total_rows = groups * CAP
    flat_ids = expert_ids.reshape(-1)
    onehot = (flat_ids[:, None] == jnp.arange(groups, dtype=jnp.int32)[None, :]).astype(jnp.int32)
    ranks = jnp.cumsum(onehot, axis=0) - 1
    rank_own = jnp.sum(ranks * onehot, axis=1)
    slot_index = flat_ids * CAP + rank_own
    counts = jnp.sum(onehot, axis=0)
    source_rows = jnp.arange(tok_count * top_count, dtype=jnp.int32) // top_count
    table = jnp.full((total_rows,), tok_count, jnp.int32).at[slot_index].set(source_rows)
    padded_tokens = jnp.concatenate([tokens, jnp.zeros((1, model_width), tokens.dtype)], axis=0)
    send_rows = padded_tokens[table]
    received, arrived = (
        lax.all_to_all(send_rows, "expert", split_axis=0, concat_axis=0, tiled=True),
        lax.all_to_all(counts[:, None], "expert", split_axis=0, concat_axis=0, tiled=True),
    )
    arrived = arrived[:, 0]
    gate_local = gate_weight[0]
    up_local = up_weight[0]
    down_local = down_weight[0]
    gate = jnp.dot(
        received,
        lax.all_gather(gate_local, "dp", axis=0, tiled=True),
        preferred_element_type=jnp.float32,
    )
    upper = jnp.dot(
        received,
        lax.all_gather(up_local, "dp", axis=0, tiled=True),
        preferred_element_type=jnp.float32,
    )
    hidden = (jax.nn.silu(gate) * upper).astype(jnp.bfloat16)
    outputs = jnp.dot(
        hidden,
        lax.all_gather(down_local, "dp", axis=1, tiled=True),
        preferred_element_type=jnp.float32,
    ).astype(jnp.bfloat16)
    returned = lax.all_to_all(outputs, "expert", split_axis=0, concat_axis=0, tiled=True)
    picked = returned[slot_index].astype(jnp.float32)
    weighted = picked * gate_probs.reshape(-1)[:, None]
    mixed = jnp.sum(weighted.reshape(tok_count, top_count, model_width), axis=1)
    return mixed.astype(jnp.bfloat16)


def solution(mesh):
    placed = (
        P(("dp", "expert"), None),
        P(("dp", "expert"), None),
        P(("dp", "expert"), None),
        P("expert", "dp", None),
        P("expert", "dp", None),
        P("expert", None, "dp"),
    )
    return jax.shard_map(
        on_device, mesh=mesh, in_specs=placed, out_specs=P(("dp", "expert"), None), check_vma=False
    )
```

profile of v0, /device:TPU:0, one launch (start us, length us, event | category | flops | bytes accessed | tf_op | source)
XLA Modules:
  0.0 440.1 jit_solution(6647712758904265105)
XLA Ops:
  6.5 0.0 all-gather.7.cloned.1.call-start
  6.5 0.7 all-gather.7.cloned.1.call-update
  7.3 0.0 all-gather.11.cloned.1.call-start
  7.3 0.7 all-gather.11.cloned.1.call-update
  8.0 0.0 all-gather.9.cloned.1.call-start
  8.1 0.7 all-gather.9.cloned.1.call-update
  8.7 0.0 copy-done.1
  8.8 0.1 copy.11
  8.9 0.1 eq.29
  9.0 0.1 eq.25
  9.2 1.2 reduce-window.6
  10.4 0.1 slice.12
  10.5 0.1 copy.13
  10.6 0.1 copy.14
  10.7 0.1 copy.10
  10.8 0.1 mul.37
  11.0 0.1 concatenate.3
  11.1 0.1 add_bitcast_fusion
  11.2 1.4 scatter_custom_fusion
  12.6 3.9 gather_fusion
  16.5 36.2 %all_to_all.24 = bf16[4,80,4096]{2,1,0:T(8,128)(2,1)S(1)} all-to-all(bf16[4,80,4096]{2,1,0:T(8,128)(2,1)} %bitcast.41), channel_id=1, replica_groups=mesh['dp'=8,'expert'=4] {'expert'}, dimensions={0} | all-to-all | bytes 5242880 | tf_op jit(solution)/shard_map/all_to_all | solution.py:25
  52.8 75.7 %all-gather.7.cloned.1.call-done = bf16[1,4096,1536]{2,1,0:T(8,128)(2,1)} async-done(((bf16[1,512,1536]{2,1,0:T(8,128)(2,1)}), bf16[1,4096,1536]{2,1,0:T(8,128)(2,1)}) %all-gather.7.cloned.1.call-update) | async-done | bytes 12582928 | tf_op jit(solution)/shard_map/all_gather | solution.py:34
  128.5 8.4 %fusion.4 = f32[320,1536]{1,0:T(8,128)} fusion(bf16[320,4096]{1,0:T(8,128)(2,1)S(1)} %bitcast.42, bf16[1,4096,1536]{2,1,0:T(8,128)(2,1)} %all-gather.7.cloned.1.call-done), kind=kOutput, calls=%fused_computation.7 | convolution fusion | flops 4026531840 | bytes 17170432 | tf_op jit(solution)/shard_map/dot_general | solution.py:32
  136.9 108.2 %all-gather.11.cloned.1.call-done = bf16[1,1536,4096]{2,1,0:T(8,128)(2,1)} async-done(((bf16[1,1536,512]{2,1,0:T(8,128)(2,1)}), bf16[1,1536,4096]{2,1,0:T(8,128)(2,1)}) %all-gather.11.cloned.1.call-update) | async-done | bytes 12582928 | tf_op jit(solution)/shard_map/all_gather | solution.py:45
  245.1 116.6 %all-gather.9.cloned.1.call-done = bf16[1,4096,1536]{2,1,0:T(8,128)(2,1)} async-done(((bf16[1,512,1536]{2,1,0:T(8,128)(2,1)}), bf16[1,4096,1536]{2,1,0:T(8,128)(2,1)}) %all-gather.9.cloned.1.call-update) | async-done | bytes 12582928 | tf_op jit(solution)/shard_map/all_gather | solution.py:39
  361.7 18.7 %fusion.6 = bf16[320,4096]{1,0:T(8,128)(2,1)} fusion(bf16[1,1536,4096]{2,1,0:T(8,128)(2,1)} %all-gather.11.cloned.1.call-done, bf16[320,4096]{1,0:T(8,128)(2,1)S(1)} %bitcast.43, bf16[1,4096,1536]{2,1,0:T(8,128)(2,1)} %all-gather.9.cloned.1.call-done, f32[320,1536]{1,0:T(8,128)} %fusion.4), kind=kOutput, calls=%fused_computation.9 | convolution fusion | flops 8057323520 | bytes 32374784 | tf_op jit(solution)/shard_map/dot_general | solution.py:43
  380.4 4.0 all-to-all-start.1
  384.4 0.1 copy.15
  384.5 30.8 %all-to-all-done.1 = bf16[4,80,4096]{2,1,0:T(8,128)(2,1)S(1)} async-done(((bf16[4,80,4096]{2,1,0:T(8,128)(2,1)}), bf16[4,80,4096]{2,1,0:T(8,128)(2,1)S(1)}, u32[]{:S(2)}, u32[]{:S(2)}) %all-to-all-start.1) | async-done | bytes 2621472 | tf_op jit(solution)/shard_map/all_to_all | solution.py:48
  415.3 3.2 gather_fusion.1
  418.5 5.4 %reshape.63 = f32[128,2,4096]{2,1,0:T(2,128)} reshape(bf16[256,4096]{1,0:T(8,128)(2,1)} %gather_fusion.1) | data formatting | bytes 6291456 | tf_op jit(solution)/shard_map/convert_element_type | solution.py:49
  423.9 9.6 %multiply_reduce_fusion = bf16[128,4096]{1,0:T(8,128)(2,1)} fusion(f32[128,2,4096]{2,1,0:T(2,128)} %reshape.63, f32[128,2]{1,0:T(8,128)S(1)} %copy.15), kind=kLoop, calls=%fused_computation.10 | loop fusion | flops 1572864 | bytes 5243904 | tf_op jit(solution)/shard_map/reduce_sum | solution.py:51
  (15 shorter events, 0.1 us)
Async XLA Ops:
  6.5 2.2 copy-start.1
  6.5 4.4 %copy-start = (bf16[128,4096]{1,0:T(8,128)(2,1)S(1)}, bf16[128,4096]{1,0:T(8,128)(2,1)}, u32[]{:S(2)}) copy-start(bf16[128,4096]{1,0:T(8,128)(2,1)} %param.6) | copy-start | bytes 3145732
  6.5 121.9 %all-gather.7.cloned.1.call-start = ((), (), s32[]{:S(2)}) async-start(), calls=%async_computation.2 | async-start | bytes 14155776 | tf_op jit(solution)/shard_map/all_gather | solution.py:34
  7.3 237.8 %all-gather.11.cloned.1.call-start = ((), (), s32[]{:S(2)}) async-start(), calls=%async_computation.4 | async-start | bytes 14155776 | tf_op jit(solution)/shard_map/all_gather | solution.py:45
  8.0 353.7 %all-gather.9.cloned.1.call-start = ((), (), s32[]{:S(2)}) async-start(), calls=%async_computation.3 | async-start | bytes 14155776 | tf_op jit(solution)/shard_map/all_gather | solution.py:39
  380.4 4.0 copy-start.2
  380.4 34.9 %all-to-all-start.1 = ((bf16[4,80,4096]{2,1,0:T(8,128)(2,1)}), bf16[4,80,4096]{2,1,0:T(8,128)(2,1)S(1)}, u32[]{:S(2)}, u32[]{:S(2)}) async-start(bf16[4,80,4096]{2,1,0:T(8,128)(2,1)} %bitcast.44), calls=%async_computation.1 | async-start | bytes 5242880 | tf_op jit(solution)/shard_map/all_to_all | solution.py:48
Sparse Core Ops, SparseCore 0:
  9.0 119.4 all-gather.6
  130.1 114.9 all-gather.10
  246.7 114.9 all-gather.8
where the time goes:
time: 440 us
  waiting for transfers between devices  333 us (76%)
  blocking collectives  36.2 us (8%)
  matrix products  27.1 us (6%)
  local copies, waits for them, and re-layouts  15 us (3%)
  between operations  13.2 us (3%)
  other arithmetic  11 us (2%)
    all_gather x1, waiting for transfers between devices, on_device(): lax.all_gather(up_local, 'dp', axis=0, tiled=True)  117 us
    all_gather x1, waiting for transfers between devices, on_device(): lax.all_gather(down_local, 'dp', axis=1, tiled=True)  108 us
    all_gather x1, waiting for transfers between devices, on_device(): lax.all_gather(gate_local, 'dp', axis=0, tiled=True)  75.7 us
    all_to_all x1, blocking collectives, on_device(): lax.all_to_all(send_rows, 'expert', split_axis=0, concat_axis=0, tiled=True)  36.2 us
    all_to_all x1, waiting for transfers between devices, on_device(): lax.all_to_all(outputs, 'expert', split_axis=0, concat_axis=0, tiled=True)  30.8 us
    dot_general x1, matrix products, on_device(): jnp.dot(hidden, lax.all_gather(down_local, 'dp', axis=1, tiled=True), pre...  18.7 us
    reduce_sum x1, other arithmetic, on_device(): mixed = jnp.sum(weighted.reshape(tok_count, top_count, model_width), axis=1)  9.64 us
  transfers between devices with their start and end apart: 4, of which 4 were waited for; matrix products, arithmetic and copies ran while one was open for 4% of the time, Pallas kernels for 0%

commit v1 on v0

v1 whole, which is shorter than its diff:
```python
import jax
import jax.numpy as jnp
from jax import lax
from jax.sharding import PartitionSpec as P

CAP = 80
F32 = jnp.float32
BF16 = jnp.bfloat16
NOTE_ROWS = 8


def ranks_of(ids, groups):
    flat = ids.reshape(-1)
    count = flat.shape[0]
    onehot = (flat[:, None] == jnp.arange(groups, dtype=jnp.int32)).astype(BF16)
    before = (jnp.arange(count)[:, None] > jnp.arange(count)[None, :]).astype(BF16)
    ranks = jnp.dot(before, onehot, preferred_element_type=F32)
    return jnp.sum(ranks * onehot.astype(F32), axis=1).reshape(ids.shape)


def take(array, index):
    return lax.dynamic_index_in_dim(array, index, 0, keepdims=False)


def on_device(tokens, expert_ids, gate_probs, gate_weight, up_weight, down_weight):
    tok_count, model_width = tokens.shape
    top = expert_ids.shape[1]
    n_dp, groups = lax.axis_size("dp"), lax.axis_size("expert")
    planes = n_dp // 2
    place = lax.axis_index("dp")
    plane, core = place // 2, place % 2
    width = model_width // n_dp
    hidden_width = gate_weight.shape[2]
    half = hidden_width // 2
    slots = groups * CAP
    swap = [(i, i ^ 1) for i in range(n_dp)]

    def other(array):
        return lax.ppermute(array, "dp", swap)

    def columns(array, which):
        return lax.dynamic_slice_in_dim(array, which * half, half, 1)

    def split(array):
        return [take(array, which) for which in range(array.shape[0])]

    notes = jnp.concatenate([expert_ids.astype(F32).T, ranks_of(expert_ids, groups).T], axis=0)
    notes = jnp.pad(notes, ((0, NOTE_ROWS - 2 * top), (0, width - tok_count))).astype(BF16)
    sent = jnp.concatenate([tokens, jnp.tile(notes, (1, n_dp))], axis=0)
    arrived = lax.all_to_all(sent, "dp", split_axis=1, concat_axis=0, tiled=True)
    arrived = arrived.reshape(n_dp, tok_count + NOTE_ROWS, width)

    gate_local, up_local, down_local = gate_weight[0], up_weight[0], down_weight[0]
    keep = jnp.concatenate([columns(gate_local, core), columns(up_local, core)], axis=1)
    give = jnp.concatenate([columns(gate_local, 1 - core), columns(up_local, 1 - core)], axis=1)
    in_weight = jnp.concatenate([keep, other(give)], axis=0)
    other_probs = other(gate_probs)
    probs = jnp.where(core == 0, jnp.stack([gate_probs, other_probs]), jnp.stack([other_probs, gate_probs]))
    arrived, in_weight, probs, down_local = lax.optimization_barrier((arrived, in_weight, probs, down_local))

    told = arrived[:, tok_count : tok_count + 2 * top, :tok_count].astype(jnp.int32)
    slot = (told[:, :top] ^ lax.axis_index("expert")) * CAP + told[:, top:]
    slot_range = jnp.arange(slots, dtype=jnp.int32)[:, None]

    def across(blocks):
        return [blocks[0]] + [
            lax.ppermute(blocks[k], "expert", [(i, i ^ k) for i in range(groups)]) for k in range(1, groups)
        ]

    def routed(first, count):
        tokens_there = lax.dynamic_slice_in_dim(arrived[:, :tok_count], 2 * first, 2 * count, 0)
        slot_there = lax.dynamic_slice_in_dim(slot, 2 * first, 2 * count, 0)
        chosen = sum((slot_there[:, k, None, :] == slot_range).astype(BF16) for k in range(top))
        sending = jnp.einsum("dst,dtc->dsc", chosen, tokens_there, preferred_element_type=F32).astype(BF16)
        sending = sending.reshape(2 * count, groups, CAP, width)
        rows = jnp.concatenate(across([sending[:, k] for k in range(groups)]), axis=1)
        rows = rows.reshape(2 * count * slots, width)
        return jnp.concatenate([rows, other(rows)], axis=1).reshape(count, 2, slots, 2 * width)

    mid = planes // 2
    rising = plane < mid
    far_first = jnp.where(rising, mid, 0)
    near_first = mid - far_first
    far_rows = routed(far_first, planes - mid)

    def pass_on(below, above, step):
        upward = [(2 * i + c, 2 * i + 2 + c) for i in range(step - 1, planes - 1) for c in (0, 1)]
        downward = [(2 * i + 2 + c, 2 * i + c) for i in range(planes - step) for c in (0, 1)]
        return lax.ppermute(below, "dp", upward), lax.ppermute(above, "dp", downward)

    def product(rows):
        return jnp.dot(rows, in_weight, preferred_element_type=F32)

    def rows_for(far, near, target, side):
        there = (target >= mid) == rising
        return jnp.where(there, take(far[:, side], target % mid), take(near[:, side], target % mid))

    def add_on(far, near, side, below, above, step):
        upward = [(2 * i + c, 2 * i + 2 + c) for i in range(step) for c in (0, 1)]
        downward = [(2 * (planes - 1 - i) + c, 2 * (planes - 2 - i) + c) for i in range(step) for c in (0, 1)]
        if step <= mid:
            target = jnp.where(rising, plane - step, plane + step) % planes
            send = product(take(far[:, side], target % mid))
            if below is not None:
                send = send + jnp.where(rising, below, above).astype(F32)
            going_up = going_down = send.astype(BF16)
        else:
            going_up = product(rows_for(far, near, (plane - step) % planes, side))
            going_down = product(rows_for(far, near, (plane + step) % planes, side))
            going_up = (going_up + below.astype(F32)).astype(BF16)
            going_down = (going_down + above.astype(F32)).astype(BF16)
        return lax.ppermute(going_up, "dp", upward), lax.ppermute(going_down, "dp", downward)

    passed = [(down_local, down_local)]
    passed.append(pass_on(*passed[0], 1))
    near_rows = routed(near_first, mid)
    sums = [(None, None), (None, None)]
    for step in range(1, planes):
        sums[0] = add_on(far_rows, near_rows, 0, *sums[0], step)
        far_rows, sums[1], passed[step] = lax.optimization_barrier((far_rows, sums[1], passed[step]))
        if step == mid:
            far_rows, near_rows = lax.optimization_barrier((far_rows, near_rows))
        if step + 1 < planes:
            passed.append(pass_on(*passed[step], step + 1))
        sums[1] = add_on(far_rows, near_rows, 1, *sums[1], step)
    pieces = [down_local] + [
        jnp.where(plane >= step, passed[step][0], passed[planes - step][1]) for step in range(1, planes)
    ]
    pieces = jnp.stack(pieces)
    out_weight = jnp.concatenate([take(pieces, (plane - p) % planes) for p in range(planes)], axis=1)
    out_weight, near_rows = lax.optimization_barrier((out_weight, near_rows))

    def returned(side):
        below, above = sums[side]
        total = product(take(near_rows[:, side], plane % mid)) + below.astype(F32) + above.astype(F32)
        hidden = (jax.nn.silu(total[:, :half]) * total[:, half:]).astype(BF16)
        apart = other(hidden)
        hidden = jnp.concatenate(
            [jnp.where(core == 0, hidden, apart), jnp.where(core == 0, apart, hidden)], axis=1
        )
        return jnp.dot(hidden, out_weight, preferred_element_type=F32).astype(BF16).reshape(groups, CAP, -1)

    def combined(side, blocks):
        back = jnp.concatenate(across(split(blocks)), axis=0)
        side_slot = take(slot, 2 * plane + side)
        coarse = lax.reduce_precision(probs[side], 8, 7)
        weights = [
            sum(jnp.where(side_slot[k, :, None] == slot_range[:, 0], part[:, k, None], 0.0) for k in range(top)).astype(BF16)
            for part in (coarse, probs[side] - coarse)
        ]
        both = jnp.dot(jnp.concatenate(weights, axis=0), back, preferred_element_type=F32)
        return (both[:tok_count] + both[tok_count:]).astype(BF16)

    first = returned(0)
    first, sums[1] = lax.optimization_barrier((first, sums[1]))
    mixed = [combined(0, first), combined(1, returned(1))]
    mine = jnp.where(core == 0, mixed[0], mixed[1])
    theirs = other(jnp.where(core == 0, mixed[1], mixed[0]))
    sides = [jnp.where(core == 0, mine, theirs), jnp.where(core == 0, theirs, mine)]
    sides = [side.reshape(tok_count, planes, width) for side in sides]
    return jnp.stack(sides, axis=2).reshape(tok_count, model_width)


def solution(mesh):
    placed = (
        P(("dp", "expert"), None),
        P(("dp", "expert"), None),
        P(("dp", "expert"), None),
        P("expert", "dp", None),
        P("expert", "dp", None),
        P("expert", None, "dp"),
    )
    return jax.shard_map(
        on_device, mesh=mesh, in_specs=placed, out_specs=P(("dp", "expert"), None), check_vma=False
    )
```

time: 440 us -> 276 us (0.63)
  waiting for transfers between devices: 333 us -> 139 us
  starting transfers between devices: 4.04 us -> 88.1 us
  blocking collectives: 36.2 us -> 0 us
  between operations: 13.2 us -> 0.76 us
  matrix products: 27.1 us -> 19.2 us
  other arithmetic: 11 us -> 16.2 us
    all_gather x3 -> x0, waiting for transfers between devices: 300 us -> none  [the longest x1 117 us: on_device(): lax.all_gather(up_local, 'dp', axis=0, tiled=True)]
    ppermute x0 -> x37, waiting for transfers between devices: none -> 121 us  [the longest x12 51.7 us: across(): lax.ppermute(blocks[k], 'expert', [(i, i ^ k) for i in range(groups)])]
    ppermute x0 -> x37, starting transfers between devices: none -> 81.8 us  [the longest x6 50.9 us: add_on(): lax.ppermute(going_up, 'dp', upward)]
    all_to_all x1 -> x0, blocking collectives: 36.2 us -> none  [on_device(): lax.all_to_all(send_rows, 'expert', split_axis=0, concat_axis=0, tiled=True)]
    all_to_all x1, waiting for transfers between devices: 30.8 us -> 17.5 us  [on_device(): lax.all_to_all(sent, 'dp', split_axis=1, concat_axis=0, tiled=True)]
    concatenate x0 -> x9, other arithmetic: none -> 10.4 us  [the longest x1 3.25 us: on_device(): in_weight = jnp.concatenate([keep, other(give)], axis=0)]
    reduce_sum x2 -> x0, other arithmetic: 9.66 us -> none  [the longest x1 9.64 us: on_device(): mixed = jnp.sum(weighted.reshape(tok_count, top_count, model_width), axis=1)]
    dot_general x2 -> x17, matrix products: 27.1 us -> 19.2 us  [the longest x10 12.1 us: product(): return jnp.dot(rows, in_weight, preferred_element_type=F32)]
  transfers between devices with their start and end apart: 4 -> 38, of which waited for: 4 -> 22; matrix products, arithmetic and copies ran while one was open for 4% -> 12% of each run, Pallas kernels for 0% -> 0%
where the time goes in v1:
time: 276 us
  waiting for transfers between devices  139 us (50%)
  starting transfers between devices  88.1 us (32%)
  matrix products  19.2 us (7%)
  other arithmetic  16.2 us (6%)
  local copies, waits for them, and re-layouts  12.8 us (5%)
    ppermute x12, waiting for transfers between devices, across(): lax.ppermute(blocks[k], 'expert', [(i, i ^ k) for i in range(groups)])  51.7 us
    ppermute x6, starting transfers between devices, add_on(): lax.ppermute(going_up, 'dp', upward)  50.9 us
    ppermute x6, waiting for transfers between devices, add_on(): lax.ppermute(going_up, 'dp', upward)  44.4 us
    ppermute x6, waiting for transfers between devices, add_on(): lax.ppermute(going_down, 'dp', downward)  19.8 us
    all_to_all x1, waiting for transfers between devices, on_device(): lax.all_to_all(sent, 'dp', split_axis=1, concat_axis=0, tiled=True)  17.5 us
    ppermute x12, starting transfers between devices, across(): lax.ppermute(blocks[k], 'expert', [(i, i ^ k) for i in range(groups)])  14.1 us
    dot_general x10, matrix products, product(): return jnp.dot(rows, in_weight, preferred_element_type=F32)  12.1 us
    all_to_all x1, starting transfers between devices, on_device(): lax.all_to_all(sent, 'dp', split_axis=1, concat_axis=0, tiled=True)  6.33 us
  transfers between devices with their start and end apart: 38, of which 22 were waited for; matrix products, arithmetic and copies ran while one was open for 12% of the time, Pallas kernels for 0%

profile of v1, /device:TPU:0, one launch (start us, length us, event | category | flops | bytes accessed | tf_op | source)
XLA Modules:
  0.0 275.7 jit_solution(6203732600134210934)
XLA Ops:
  2.1 1.6 copy.26
  5.4 6.3 %all-to-all-start = ((bf16[136,8,512]{2,0,1:T(8,128)(2,1)}), bf16[136,8,512]{2,0,1:T(8,128)(2,1)S(1)}, u32[]{:S(2)}, u32[]{:S(2)}) async-start(bf16[136,8,512]{2,0,1:T(8,128)(2,1)} %pad_maximum_fusion.8), calls=%async_computation | async-start | bytes 2228224 | tf_op jit(solution)/shard_map/all_to_all | solution.py:50
  11.7 2.0 dynamic-slice_bitcast_fusion.6
  15.6 2.9 %collective-permute-done.1 = f32[128,2]{0,1:T(2,128)S(1)} collective-permute-done((f32[128,2]{0,1:T(2,128)S(1)}, f32[128,2]{0,1:T(2,128)S(1)}, u32[]{:S(2)}, u32[]{:S(2)}) %collective-permute-start.1) | collective-permute-done | bytes 1056 | tf_op jit(solution)/shard_map/ppermute | solution.py:39
  19.0 3.2 %pad_maximum_fusion.2 = bf16[1024,1536]{1,0:T(8,128)(2,1)} fusion(bf16[512,1536]{1,0:T(8,128)(2,1)} %collective-permute-done, bf16[512,768]{1,0:T(8,128)(2,1)S(1)} %get-tuple-element.72, bf16[512,768]{1,0:T(8,128)(2,1)S(1)} %get-tuple-element.123), kind=kLoop, calls=%fused_computation.2 | loop fusion | flops 9437184 | bytes 6291456 | tf_op jit(solution)/shard_map/concatenate | solution.py:56
  22.2 17.5 %all-to-all-done = bf16[136,8,512]{2,0,1:T(8,128)(2,1)S(1)} async-done(((bf16[136,8,512]{2,0,1:T(8,128)(2,1)}), bf16[136,8,512]{2,0,1:T(8,128)(2,1)S(1)}, u32[]{:S(2)}, u32[]{:S(2)}) %all-to-all-start) | async-done | bytes 1114144 | tf_op jit(solution)/shard_map/all_to_all | solution.py:50
  46.4 4.6 %collective-permute-start.6 = (bf16[1536,512]{1,0:T(8,128)(2,1)S(1)}, bf16[1536,512]{1,0:T(8,128)(2,1)S(1)}, u32[]{:S(2)}, u32[]{:S(2)}) collective-permute-start(bf16[1536,512]{1,0:T(8,128)(2,1)S(1)} %bitcast.182), channel_id=1, source_target_pairs={{0,8},{4,12},{8,16},{12,20},{16,24},{20,28},{1,9},{5,13},{9,17},{1... | collective-permute-start | bytes 4718600 | tf_op jit(solution)/shard_map/ppermute | solution.py:89
  52.4 6.7 %collective-permute-done.4 = bf16[4,80,512]{2,1,0:T(8,128)(2,1)S(1)} collective-permute-done((bf16[4,80,512]{2,1,0:T(8,128)(2,1)}, bf16[4,80,512]{2,1,0:T(8,128)(2,1)S(1)}, u32[]{:S(2)}, u32[]{:S(2)}) %collective-permute-start.4) | collective-permute-done | bytes 327712 | tf_op jit(solution)/shard_map/ppermute | solution.py:67
  64.6 8.5 %collective-permute-done.12 = bf16[4,80,512]{2,1,0:T(8,128)(2,1)S(1)} collective-permute-done((bf16[4,80,512]{2,1,0:T(8,128)(2,1)S(1)}, bf16[4,80,512]{2,1,0:T(8,128)(2,1)S(1)}, u32[]{:S(2)}, u32[]{:S(2)}) %collective-permute-start.12) | collective-permute-done | bytes 327712 | tf_op jit(solution)/shard_map/ppermute | solution.py:67
  73.6 6.2 %collective-permute-done.14 = bf16[4,80,512]{2,1,0:T(8,128)(2,1)S(1)} collective-permute-done((bf16[4,80,512]{2,1,0:T(8,128)(2,1)S(1)}, bf16[4,80,512]{2,1,0:T(8,128)(2,1)S(1)}, u32[]{:S(2)}, u32[]{:S(2)}) %collective-permute-start.14) | collective-permute-done | bytes 327712 | tf_op jit(solution)/shard_map/ppermute | solution.py:67
  79.8 6.9 %collective-permute-done.13 = bf16[4,80,512]{2,1,0:T(8,128)(2,1)S(1)} collective-permute-done((bf16[4,80,512]{2,1,0:T(8,128)(2,1)S(1)}, bf16[4,80,512]{2,1,0:T(8,128)(2,1)S(1)}, u32[]{:S(2)}, u32[]{:S(2)}) %collective-permute-start.13) | collective-permute-done | bytes 327712 | tf_op jit(solution)/shard_map/ppermute | solution.py:67
  86.9 2.1 pad_maximum_fusion.3
  96.8 4.6 %collective-permute-start.8 = (bf16[320,1536]{1,0:T(8,128)(2,1)S(1)}, bf16[320,1536]{1,0:T(8,128)(2,1)S(1)}, u32[]{:S(2)}, u32[]{:S(2)}) collective-permute-start(bf16[320,1536]{1,0:T(8,128)(2,1)S(1)} %convolution_convert_fusion.3), channel_id=1, source_target_pairs={{0,8},{4,12},{1,9},{5,13},{2,10},{6,14},{3,11},{7,15}} | collective-permute-start | bytes 2949128 | tf_op jit(solution)/shard_map/ppermute | solution.py:112
  102.1 12.5 %collective-permute-done.20 = bf16[320,1536]{1,0:T(8,128)(2,1)S(1)} collective-permute-done((bf16[320,1536]{1,0:T(8,128)(2,1)S(1)}, bf16[320,1536]{1,0:T(8,128)(2,1)S(1)}, u32[]{:S(2)}, u32[]{:S(2)}) %collective-permute-start.20) | collective-permute-done | bytes 983072 | tf_op jit(solution)/shard_map/ppermute | solution.py:112
  116.6 5.0 %collective-permute-start.22 = (bf16[320,1536]{1,0:T(8,128)(2,1)S(1)}, bf16[320,1536]{1,0:T(8,128)(2,1)S(1)}, u32[]{:S(2)}, u32[]{:S(2)}) collective-permute-start(bf16[320,1536]{1,0:T(8,128)(2,1)S(1)} %add_convert_fusion.4), channel_id=1, source_target_pairs={{0,8},{4,12},{8,16},{12,20},{1,9},{5,13},{9,17},{13,21},{2,10},{6,... | collective-permute-start | bytes 2949128 | tf_op jit(solution)/shard_map/ppermute | solution.py:112
  121.6 14.1 %collective-permute-done.8 = bf16[320,1536]{1,0:T(8,128)(2,1)S(1)} collective-permute-done((bf16[320,1536]{1,0:T(8,128)(2,1)S(1)}, bf16[320,1536]{1,0:T(8,128)(2,1)S(1)}, u32[]{:S(2)}, u32[]{:S(2)}) %collective-permute-start.8) | collective-permute-done | bytes 983072 | tf_op jit(solution)/shard_map/ppermute | solution.py:112
  140.3 16.5 %collective-permute-start.16 = (bf16[320,1536]{1,0:T(8,128)(2,1)S(1)}, bf16[320,1536]{1,0:T(8,128)(2,1)S(1)}, u32[]{:S(2)}, u32[]{:S(2)}) collective-permute-start(bf16[320,1536]{1,0:T(8,128)(2,1)S(1)} %add_convert_fusion.5), channel_id=1, source_target_pairs={{0,8},{4,12},{8,16},{12,20},{1,9},{5,13},{9,17},{13,21},{2,10},{6,... | collective-permute-start | bytes 2949128 | tf_op jit(solution)/shard_map/ppermute | solution.py:112
  160.8 17.1 %collective-permute-start.23 = (bf16[320,1536]{1,0:T(8,128)(2,1)S(1)}, bf16[320,1536]{1,0:T(8,128)(2,1)S(1)}, u32[]{:S(2)}, u32[]{:S(2)}) collective-permute-start(bf16[320,1536]{1,0:T(8,128)(2,1)S(1)} %add_convert_fusion.3), channel_id=1, source_target_pairs={{0,8},{4,12},{8,16},{12,20},{16,24},{20,28},{1,9},{5,13},{9,17},{1... | collective-permute-start | bytes 2949128 | tf_op jit(solution)/shard_map/ppermute | solution.py:112
  182.2 15.0 %collective-permute-done.25 = bf16[320,1536]{1,0:T(8,128)(2,1)S(1)} collective-permute-done((bf16[320,1536]{1,0:T(8,128)(2,1)S(1)}, bf16[320,1536]{1,0:T(8,128)(2,1)S(1)}, u32[]{:S(2)}, u32[]{:S(2)}) %collective-permute-start.25) | collective-permute-done | bytes 983072 | tf_op jit(solution)/shard_map/ppermute | solution.py:112
  201.8 6.3 %collective-permute-start.27 = (bf16[320,1536]{1,0:T(8,128)(2,1)S(1)}, bf16[320,1536]{1,0:T(8,128)(2,1)S(1)}, u32[]{:S(2)}, u32[]{:S(2)}) collective-permute-start(bf16[320,1536]{1,0:T(8,128)(2,1)S(1)} %add_convert_fusion.1), channel_id=1, source_target_pairs={{0,8},{4,12},{8,16},{12,20},{16,24},{20,28},{1,9},{5,13},{9,17},{1... | collective-permute-start | bytes 2949128 | tf_op jit(solution)/shard_map/ppermute | solution.py:112
  211.3 2.2 convolution_convert_fusion.1
  213.6 16.2 %collective-permute-done.27 = bf16[320,1536]{1,0:T(8,128)(2,1)S(1)} collective-permute-done((bf16[320,1536]{1,0:T(8,128)(2,1)S(1)}, bf16[320,1536]{1,0:T(8,128)(2,1)S(1)}, u32[]{:S(2)}, u32[]{:S(2)}) %collective-permute-start.27) | collective-permute-done | bytes 983072 | tf_op jit(solution)/shard_map/ppermute | solution.py:112
  229.7 4.9 %collective-permute-done.28 = bf16[320,1536]{1,0:T(8,128)(2,1)S(1)} collective-permute-done((bf16[320,1536]{1,0:T(8,128)(2,1)S(1)}, bf16[320,1536]{1,0:T(8,128)(2,1)S(1)}, u32[]{:S(2)}, u32[]{:S(2)}) %collective-permute-start.28) | collective-permute-done | bytes 983072 | tf_op jit(solution)/shard_map/ppermute | solution.py:112
  235.4 2.5 collective-permute-start.31
  239.5 2.3 convolution_convert_fusion
  241.8 2.5 collective-permute-start.35
  244.9 2.1 collective-permute-done.31
  248.6 5.4 %collective-permute-done.30 = bf16[80,2048]{1,0:T(8,128)(2,1)S(1)} collective-permute-done((bf16[80,2048]{1,0:T(8,128)(2,1)S(1)}, bf16[80,2048]{1,0:T(8,128)(2,1)S(1)}, u32[]{:S(2)}, u32[]{:S(2)}) %collective-permute-start.30) | collective-permute-done | bytes 327712 | tf_op jit(solution)/shard_map/ppermute | solution.py:67
  254.8 6.3 %collective-permute-done.35 = bf16[80,2048]{1,0:T(8,128)(2,1)S(1)} collective-permute-done((bf16[80,2048]{1,0:T(8,128)(2,1)S(1)}, bf16[80,2048]{1,0:T(8,128)(2,1)S(1)}, u32[]{:S(2)}, u32[]{:S(2)}) %collective-permute-start.35) | collective-permute-done | bytes 327712 | tf_op jit(solution)/shard_map/ppermute | solution.py:67
  261.1 6.5 %collective-permute-done.34 = bf16[80,2048]{1,0:T(8,128)(2,1)S(1)} collective-permute-done((bf16[80,2048]{1,0:T(8,128)(2,1)S(1)}, bf16[80,2048]{1,0:T(8,128)(2,1)S(1)}, u32[]{:S(2)}, u32[]{:S(2)}) %collective-permute-start.34) | collective-permute-done | bytes 327712 | tf_op jit(solution)/shard_map/ppermute | solution.py:67
  268.9 1.9 collective-permute-done.36
  272.4 1.6 copy.36
  (130 shorter events, 60.7 us)
Async XLA Ops:
  5.4 34.3 %all-to-all-start = ((bf16[136,8,512]{2,0,1:T(8,128)(2,1)}), bf16[136,8,512]{2,0,1:T(8,128)(2,1)S(1)}, u32[]{:S(2)}, u32[]{:S(2)}) async-start(bf16[136,8,512]{2,0,1:T(8,128)(2,1)} %pad_maximum_fusion.8), calls=%async_computation | async-start | bytes 2228224 | tf_op jit(solution)/shard_map/all_to_all | solution.py:50
  41.6 10.8 %collective-permute-start.2 = (bf16[4,80,512]{2,1,0:T(8,128)(2,1)}, bf16[4,80,512]{2,1,0:T(8,128)(2,1)S(1)}, u32[]{:S(2)}, u32[]{:S(2)}) collective-permute-start(bf16[4,80,512]{2,1,0:T(8,128)(2,1)} %get-tuple-element.89), channel_id=1, source_target_pairs={{0,1},{1,0},{2,3},{3,2},{4,5},{5,4},{6,7},{7,6},{8,9},{9,8},{10,11... | collective-permute-start | bytes 983048 | tf_op jit(solution)/shard_map/ppermute | solution.py:67
  43.1 16.1 %collective-permute-start.4 = (bf16[4,80,512]{2,1,0:T(8,128)(2,1)}, bf16[4,80,512]{2,1,0:T(8,128)(2,1)S(1)}, u32[]{:S(2)}, u32[]{:S(2)}) collective-permute-start(bf16[4,80,512]{2,1,0:T(8,128)(2,1)} %get-tuple-element.90), channel_id=1, source_target_pairs={{0,3},{1,2},{2,1},{3,0},{4,7},{5,6},{6,5},{7,4},{8,11},{9,10},{10,... | collective-permute-start | bytes 983048 | tf_op jit(solution)/shard_map/ppermute | solution.py:67
  44.6 16.0 %collective-permute-start.3 = (bf16[4,80,512]{2,1,0:T(8,128)(2,1)}, bf16[4,80,512]{2,1,0:T(8,128)(2,1)}, u32[]{:S(2)}, u32[]{:S(2)}) collective-permute-start(bf16[4,80,512]{2,1,0:T(8,128)(2,1)} %get-tuple-element.91), channel_id=1, source_target_pairs={{0,2},{1,3},{2,0},{3,1},{4,6},{5,7},{6,4},{7,5},{8,10},{9,11},{10,... | collective-permute-start | bytes 983048 | tf_op jit(solution)/shard_map/ppermute | solution.py:67
  45.1 47.4 %collective-permute-start.7 = (bf16[1536,512]{1,0:T(8,128)(2,1)S(1)}, bf16[1536,512]{1,0:T(8,128)(2,1)S(1)}, u32[]{:S(2)}, u32[]{:S(2)}) collective-permute-start(bf16[1536,512]{1,0:T(8,128)(2,1)S(1)} %bitcast.181), channel_id=1, source_target_pairs={{8,0},{12,4},{16,8},{20,12},{24,16},{28,20},{9,1},{13,5},{17,9},{2... | collective-permute-start | bytes 4718600 | tf_op jit(solution)/shard_map/ppermute | solution.py:89
  46.4 46.1 %collective-permute-start.6 = (bf16[1536,512]{1,0:T(8,128)(2,1)S(1)}, bf16[1536,512]{1,0:T(8,128)(2,1)S(1)}, u32[]{:S(2)}, u32[]{:S(2)}) collective-permute-start(bf16[1536,512]{1,0:T(8,128)(2,1)S(1)} %bitcast.182), channel_id=1, source_target_pairs={{0,8},{4,12},{8,16},{12,20},{16,24},{20,28},{1,9},{5,13},{9,17},{1... | collective-permute-start | bytes 4718600 | tf_op jit(solution)/shard_map/ppermute | solution.py:89
  61.8 25.1 %collective-permute-start.5 = (bf16[1280,512]{1,0:T(8,128)(2,1)S(1)}, bf16[1280,512]{1,0:T(8,128)(2,1)S(1)}, u32[]{:S(2)}, u32[]{:S(2)}) collective-permute-start(bf16[1280,512]{1,0:T(8,128)(2,1)S(1)} %bitcast.192), channel_id=1, source_target_pairs={{0,4},{4,0},{8,12},{12,8},{16,20},{20,16},{24,28},{28,24},{1,5},{5... | collective-permute-start | bytes 3932168 | tf_op jit(solution)/shard_map/ppermute | solution.py:39
  62.5 10.6 %collective-permute-start.12 = (bf16[4,80,512]{2,1,0:T(8,128)(2,1)S(1)}, bf16[4,80,512]{2,1,0:T(8,128)(2,1)S(1)}, u32[]{:S(2)}, u32[]{:S(2)}) collective-permute-start(bf16[4,80,512]{2,1,0:T(8,128)(2,1)S(1)} %get-tuple-element.84), channel_id=1, source_target_pairs={{0,1},{1,0},{2,3},{3,2},{4,5},{5,4},{6,7},{7,6},{8,9},{9,8},{10,11... | collective-permute-start | bytes 983048 | tf_op jit(solution)/shard_map/ppermute | solution.py:67
  64.1 15.7 %collective-permute-start.14 = (bf16[4,80,512]{2,1,0:T(8,128)(2,1)S(1)}, bf16[4,80,512]{2,1,0:T(8,128)(2,1)S(1)}, u32[]{:S(2)}, u32[]{:S(2)}) collective-permute-start(bf16[4,80,512]{2,1,0:T(8,128)(2,1)S(1)} %get-tuple-element.85), channel_id=1, source_target_pairs={{0,3},{1,2},{2,1},{3,0},{4,7},{5,6},{6,5},{7,4},{8,11},{9,10},{10,... | collective-permute-start | bytes 983048 | tf_op jit(solution)/shard_map/ppermute | solution.py:67
  73.1 13.6 %collective-permute-start.13 = (bf16[4,80,512]{2,1,0:T(8,128)(2,1)S(1)}, bf16[4,80,512]{2,1,0:T(8,128)(2,1)S(1)}, u32[]{:S(2)}, u32[]{:S(2)}) collective-permute-start(bf16[4,80,512]{2,1,0:T(8,128)(2,1)S(1)} %get-tuple-element.86), channel_id=1, source_target_pairs={{0,2},{1,3},{2,0},{3,1},{4,6},{5,7},{6,4},{7,5},{8,10},{9,11},{10,... | collective-permute-start | bytes 983048 | tf_op jit(solution)/shard_map/ppermute | solution.py:67
  91.2 23.4 %collective-permute-start.20 = (bf16[320,1536]{1,0:T(8,128)(2,1)S(1)}, bf16[320,1536]{1,0:T(8,128)(2,1)S(1)}, u32[]{:S(2)}, u32[]{:S(2)}) collective-permute-start(bf16[320,1536]{1,0:T(8,128)(2,1)S(1)} %convolution_convert_fusion.2), channel_id=1, source_target_pairs={{0,8},{4,12},{1,9},{5,13},{2,10},{6,14},{3,11},{7,15}} | collective-permute-start | bytes 2949128 | tf_op jit(solution)/shard_map/ppermute | solution.py:112
  92.5 43.1 %collective-permute-start.10 = (bf16[1536,512]{1,0:T(8,128)(2,1)S(1)}, bf16[1536,512]{1,0:T(8,128)(2,1)S(1)}, u32[]{:S(2)}, u32[]{:S(2)}) collective-permute-start(bf16[1536,512]{1,0:T(8,128)(2,1)S(1)} %collective-permute-done.6), channel_id=1, source_target_pairs={{8,16},{12,20},{16,24},{20,28},{9,17},{13,21},{17,25},{21,29},{10,... | collective-permute-start | bytes 4718600 | tf_op jit(solution)/shard_map/ppermute | solution.py:89
  93.3 42.3 %collective-permute-start.11 = (bf16[1536,512]{1,0:T(8,128)(2,1)S(1)}, bf16[1536,512]{1,0:T(8,128)(2,1)S(1)}, u32[]{:S(2)}, u32[]{:S(2)}) collective-permute-start(bf16[1536,512]{1,0:T(8,128)(2,1)S(1)} %collective-permute-done.7), channel_id=1, source_target_pairs={{8,0},{12,4},{16,8},{20,12},{9,1},{13,5},{17,9},{21,13},{10,2},{14... | collective-permute-start | bytes 4718600 | tf_op jit(solution)/shard_map/ppermute | solution.py:89
  96.1 20.5 %collective-permute-start.9 = (bf16[320,1536]{1,0:T(8,128)(2,1)S(1)}, bf16[320,1536]{1,0:T(8,128)(2,1)S(1)}, u32[]{:S(2)}, u32[]{:S(2)}) collective-permute-start(bf16[320,1536]{1,0:T(8,128)(2,1)S(1)} %convolution_convert_fusion.3), channel_id=1, source_target_pairs={{24,16},{28,20},{25,17},{29,21},{26,18},{30,22},{27,19},{31,23}} | collective-permute-start | bytes 2949128 | tf_op jit(solution)/shard_map/ppermute | solution.py:112
  96.8 38.8 %collective-permute-start.8 = (bf16[320,1536]{1,0:T(8,128)(2,1)S(1)}, bf16[320,1536]{1,0:T(8,128)(2,1)S(1)}, u32[]{:S(2)}, u32[]{:S(2)}) collective-permute-start(bf16[320,1536]{1,0:T(8,128)(2,1)S(1)} %convolution_convert_fusion.3), channel_id=1, source_target_pairs={{0,8},{4,12},{1,9},{5,13},{2,10},{6,14},{3,11},{7,15}} | collective-permute-start | bytes 2949128 | tf_op jit(solution)/shard_map/ppermute | solution.py:112
  115.8 24.5 %collective-permute-start.24 = (bf16[320,1536]{1,0:T(8,128)(2,1)S(1)}, bf16[320,1536]{1,0:T(8,128)(2,1)S(1)}, u32[]{:S(2)}, u32[]{:S(2)}) collective-permute-start(bf16[320,1536]{1,0:T(8,128)(2,1)S(1)} %add_convert_fusion.4), channel_id=1, source_target_pairs={{24,16},{28,20},{16,8},{20,12},{25,17},{29,21},{17,9},{21,13},{26,... | collective-permute-start | bytes 2949128 | tf_op jit(solution)/shard_map/ppermute | solution.py:112
  116.6 41.7 %collective-permute-start.22 = (bf16[320,1536]{1,0:T(8,128)(2,1)S(1)}, bf16[320,1536]{1,0:T(8,128)(2,1)S(1)}, u32[]{:S(2)}, u32[]{:S(2)}) collective-permute-start(bf16[320,1536]{1,0:T(8,128)(2,1)S(1)} %add_convert_fusion.4), channel_id=1, source_target_pairs={{0,8},{4,12},{8,16},{12,20},{1,9},{5,13},{9,17},{13,21},{2,10},{6,... | collective-permute-start | bytes 2949128 | tf_op jit(solution)/shard_map/ppermute | solution.py:112
  135.7 42.4 %collective-permute-start.18 = (bf16[1536,512]{1,0:T(8,128)(2,1)S(1)}, bf16[1536,512]{1,0:T(8,128)(2,1)S(1)}, u32[]{:S(2)}, u32[]{:S(2)}) collective-permute-start(bf16[1536,512]{1,0:T(8,128)(2,1)S(1)} %collective-permute-done.10), channel_id=1, source_target_pairs={{16,24},{20,28},{17,25},{21,29},{18,26},{22,30},{19,27},{23,31}} | collective-permute-start | bytes 4718600 | tf_op jit(solution)/shard_map/ppermute | solution.py:89
  136.4 41.6 %collective-permute-start.19 = (bf16[1536,512]{1,0:T(8,128)(2,1)S(1)}, bf16[1536,512]{1,0:T(8,128)(2,1)S(1)}, u32[]{:S(2)}, u32[]{:S(2)}) collective-permute-start(bf16[1536,512]{1,0:T(8,128)(2,1)S(1)} %collective-permute-done.11), channel_id=1, source_target_pairs={{8,0},{12,4},{9,1},{13,5},{10,2},{14,6},{11,3},{15,7}} | collective-permute-start | bytes 4718600 | tf_op jit(solution)/shard_map/ppermute | solution.py:89
  139.6 21.2 %collective-permute-start.17 = (bf16[320,1536]{1,0:T(8,128)(2,1)S(1)}, bf16[320,1536]{1,0:T(8,128)(2,1)S(1)}, u32[]{:S(2)}, u32[]{:S(2)}) collective-permute-start(bf16[320,1536]{1,0:T(8,128)(2,1)S(1)} %add_convert_fusion.5), channel_id=1, source_target_pairs={{24,16},{28,20},{16,8},{20,12},{25,17},{29,21},{17,9},{21,13},{26,... | collective-permute-start | bytes 2949128 | tf_op jit(solution)/shard_map/ppermute | solution.py:112
  140.3 37.7 %collective-permute-start.16 = (bf16[320,1536]{1,0:T(8,128)(2,1)S(1)}, bf16[320,1536]{1,0:T(8,128)(2,1)S(1)}, u32[]{:S(2)}, u32[]{:S(2)}) collective-permute-start(bf16[320,1536]{1,0:T(8,128)(2,1)S(1)} %add_convert_fusion.5), channel_id=1, source_target_pairs={{0,8},{4,12},{8,16},{12,20},{1,9},{5,13},{9,17},{13,21},{2,10},{6,... | collective-permute-start | bytes 2949128 | tf_op jit(solution)/shard_map/ppermute | solution.py:112
  158.3 38.8 %collective-permute-start.25 = (bf16[320,1536]{1,0:T(8,128)(2,1)S(1)}, bf16[320,1536]{1,0:T(8,128)(2,1)S(1)}, u32[]{:S(2)}, u32[]{:S(2)}) collective-permute-start(bf16[320,1536]{1,0:T(8,128)(2,1)S(1)} %add_convert_fusion.2), channel_id=1, source_target_pairs={{24,16},{28,20},{16,8},{20,12},{8,0},{12,4},{25,17},{29,21},{17,9}... | collective-permute-start | bytes 2949128 | tf_op jit(solution)/shard_map/ppermute | solution.py:112
  160.8 37.8 %collective-permute-start.23 = (bf16[320,1536]{1,0:T(8,128)(2,1)S(1)}, bf16[320,1536]{1,0:T(8,128)(2,1)S(1)}, u32[]{:S(2)}, u32[]{:S(2)}) collective-permute-start(bf16[320,1536]{1,0:T(8,128)(2,1)S(1)} %add_convert_fusion.3), channel_id=1, source_target_pairs={{0,8},{4,12},{8,16},{12,20},{16,24},{20,28},{1,9},{5,13},{9,17},{1... | collective-permute-start | bytes 2949128 | tf_op jit(solution)/shard_map/ppermute | solution.py:112
  199.3 11.6 %collective-permute-start.26 = (bf16[320,768]{1,0:T(8,128)(2,1)S(1)}, bf16[320,768]{1,0:T(8,128)(2,1)S(1)}, u32[]{:S(2)}, u32[]{:S(2)}) collective-permute-start(bf16[320,768]{1,0:T(8,128)(2,1)S(1)} %fusion.20), channel_id=1, source_target_pairs={{0,4},{4,0},{8,12},{12,8},{16,20},{20,16},{24,28},{28,24},{1,5},{5... | collective-permute-start | bytes 1474568 | tf_op jit(solution)/shard_map/ppermute | solution.py:39
  201.8 27.9 %collective-permute-start.27 = (bf16[320,1536]{1,0:T(8,128)(2,1)S(1)}, bf16[320,1536]{1,0:T(8,128)(2,1)S(1)}, u32[]{:S(2)}, u32[]{:S(2)}) collective-permute-start(bf16[320,1536]{1,0:T(8,128)(2,1)S(1)} %add_convert_fusion.1), channel_id=1, source_target_pairs={{0,8},{4,12},{8,16},{12,20},{16,24},{20,28},{1,9},{5,13},{9,17},{1... | collective-permute-start | bytes 2949128 | tf_op jit(solution)/shard_map/ppermute | solution.py:112
  208.1 26.5 %collective-permute-start.28 = (bf16[320,1536]{1,0:T(8,128)(2,1)S(1)}, bf16[320,1536]{1,0:T(8,128)(2,1)S(1)}, u32[]{:S(2)}, u32[]{:S(2)}) collective-permute-start(bf16[320,1536]{1,0:T(8,128)(2,1)S(1)} %add_convert_fusion), channel_id=1, source_target_pairs={{24,16},{28,20},{16,8},{20,12},{8,0},{12,4},{25,17},{29,21},{17,9}... | collective-permute-start | bytes 2949128 | tf_op jit(solution)/shard_map/ppermute | solution.py:112
  235.4 11.5 %collective-permute-start.31 = (bf16[80,2048]{1,0:T(8,128)(2,1)S(1)}, bf16[80,2048]{1,0:T(8,128)(2,1)S(1)}, u32[]{:S(2)}, u32[]{:S(2)}) collective-permute-start(bf16[80,2048]{1,0:T(8,128)(2,1)S(1)} %get-tuple-element.79), channel_id=1, source_target_pairs={{0,3},{1,2},{2,1},{3,0},{4,7},{5,6},{6,5},{7,4},{8,11},{9,10},{10,... | collective-permute-start | bytes 983048 | tf_op jit(solution)/shard_map/ppermute | solution.py:67
  237.9 16.1 %collective-permute-start.30 = (bf16[80,2048]{1,0:T(8,128)(2,1)S(1)}, bf16[80,2048]{1,0:T(8,128)(2,1)S(1)}, u32[]{:S(2)}, u32[]{:S(2)}) collective-permute-start(bf16[80,2048]{1,0:T(8,128)(2,1)S(1)} %get-tuple-element.80), channel_id=1, source_target_pairs={{0,2},{1,3},{2,0},{3,1},{4,6},{5,7},{6,4},{7,5},{8,10},{9,11},{10,... | collective-permute-start | bytes 983048 | tf_op jit(solution)/shard_map/ppermute | solution.py:67
  238.5 15.6 %collective-permute-start.29 = (bf16[80,2048]{1,0:T(8,128)(2,1)S(1)}, bf16[80,2048]{1,0:T(8,128)(2,1)S(1)}, u32[]{:S(2)}, u32[]{:S(2)}) collective-permute-start(bf16[80,2048]{1,0:T(8,128)(2,1)S(1)} %get-tuple-element.81), channel_id=1, source_target_pairs={{0,1},{1,0},{2,3},{3,2},{4,5},{5,4},{6,7},{7,6},{8,9},{9,8},{10,11... | collective-permute-start | bytes 983048 | tf_op jit(solution)/shard_map/ppermute | solution.py:67
  241.8 19.2 %collective-permute-start.35 = (bf16[80,2048]{1,0:T(8,128)(2,1)S(1)}, bf16[80,2048]{1,0:T(8,128)(2,1)S(1)}, u32[]{:S(2)}, u32[]{:S(2)}) collective-permute-start(bf16[80,2048]{1,0:T(8,128)(2,1)S(1)} %get-tuple-element.75), channel_id=1, source_target_pairs={{0,3},{1,2},{2,1},{3,0},{4,7},{5,6},{6,5},{7,4},{8,11},{9,10},{10,... | collective-permute-start | bytes 983048 | tf_op jit(solution)/shard_map/ppermute | solution.py:67
  244.3 23.2 %collective-permute-start.34 = (bf16[80,2048]{1,0:T(8,128)(2,1)S(1)}, bf16[80,2048]{1,0:T(8,128)(2,1)S(1)}, u32[]{:S(2)}, u32[]{:S(2)}) collective-permute-start(bf16[80,2048]{1,0:T(8,128)(2,1)S(1)} %get-tuple-element.76), channel_id=1, source_target_pairs={{0,2},{1,3},{2,0},{3,1},{4,6},{5,7},{6,4},{7,5},{8,10},{9,11},{10,... | collective-permute-start | bytes 983048 | tf_op jit(solution)/shard_map/ppermute | solution.py:67
  247.0 20.8 %collective-permute-start.33 = (bf16[80,2048]{1,0:T(8,128)(2,1)S(1)}, bf16[80,2048]{1,0:T(8,128)(2,1)S(1)}, u32[]{:S(2)}, u32[]{:S(2)}) collective-permute-start(bf16[80,2048]{1,0:T(8,128)(2,1)S(1)} %get-tuple-element.77), channel_id=1, source_target_pairs={{0,1},{1,0},{2,3},{3,2},{4,5},{5,4},{6,7},{7,6},{8,9},{9,8},{10,11... | collective-permute-start | bytes 983048 | tf_op jit(solution)/shard_map/ppermute | solution.py:67
  (10 other events, 61.3 us)

commit v2 on v1

--- a/solution.py
+++ b/solution.py
@@ -67,81 +67,89 @@
             lax.ppermute(blocks[k], "expert", [(i, i ^ k) for i in range(groups)]) for k in range(1, groups)
         ]
 
-    def routed(first, count):
-        tokens_there = lax.dynamic_slice_in_dim(arrived[:, :tok_count], 2 * first, 2 * count, 0)
-        slot_there = lax.dynamic_slice_in_dim(slot, 2 * first, 2 * count, 0)
-        chosen = sum((slot_there[:, k, None, :] == slot_range).astype(BF16) for k in range(top))
-        sending = jnp.einsum("dst,dtc->dsc", chosen, tokens_there, preferred_element_type=F32).astype(BF16)
-        sending = sending.reshape(2 * count, groups, CAP, width)
-        rows = jnp.concatenate(across([sending[:, k] for k in range(groups)]), axis=1)
-        rows = rows.reshape(2 * count * slots, width)
-        return jnp.concatenate([rows, other(rows)], axis=1).reshape(count, 2, slots, 2 * width)
+    def pass_on(below, above, step):
+        upward = [(2 * i + c, 2 * i + 2 + c) for i in range(step - 1, planes - 1) for c in (0, 1)]
+        downward = [(2 * i + 2 + c, 2 * i + c) for i in range(planes - step) for c in (0, 1)]
+        return lax.ppermute(below, "dp", upward), lax.ppermute(above, "dp", downward)
+
+    passed = [(down_local, down_local)]
+    passed.append(pass_on(*passed[0], 1))
+
+    chosen = sum((slot[:, k, None, :] == slot_range).astype(BF16) for k in range(top))
+    sending = jnp.einsum("dst,dtc->dsc", chosen, arrived[:, :tok_count], preferred_element_type=F32).astype(BF16)
+    sending = sending.reshape(n_dp, groups, CAP, width)
+    rows = jnp.concatenate(across([sending[:, k] for k in range(groups)]), axis=1)
+    rows = rows.reshape(planes, 2 * slots, width)
+    rows, passed[1] = lax.optimization_barrier((rows, passed[1]))
+
+    def whole(first, count):
+        some = lax.dynamic_slice_in_dim(rows, first, count, 0)
+        return jnp.concatenate([some, other(some)], axis=2).reshape(count, 2, slots, 2 * width)
+
+    def together(*values):
+        return lax.optimization_barrier(values)
 
     mid = planes // 2
     rising = plane < mid
     far_first = jnp.where(rising, mid, 0)
     near_first = mid - far_first
-    far_rows = routed(far_first, planes - mid)
-
-    def pass_on(below, above, step):
-        upward = [(2 * i + c, 2 * i + 2 + c) for i in range(step - 1, planes - 1) for c in (0, 1)]
-        downward = [(2 * i + 2 + c, 2 * i + c) for i in range(planes - step) for c in (0, 1)]
-        return lax.ppermute(below, "dp", upward), lax.ppermute(above, "dp", downward)
+    far = whole(far_first, planes - mid)
 
     def product(rows):
         return jnp.dot(rows, in_weight, preferred_element_type=F32)
 
-    def rows_for(far, near, target, side):
-        there = (target >= mid) == rising
-        return jnp.where(there, take(far[:, side], target % mid), take(near[:, side], target % mid))
-
-    def add_on(far, near, side, below, above, step):
-        upward = [(2 * i + c, 2 * i + 2 + c) for i in range(step) for c in (0, 1)]
-        downward = [(2 * (planes - 1 - i) + c, 2 * (planes - 2 - i) + c) for i in range(step) for c in (0, 1)]
+    def add_on(side, below, above, step):
         if step <= mid:
             target = jnp.where(rising, plane - step, plane + step) % planes
             send = product(take(far[:, side], target % mid))
             if below is not None:
                 send = send + jnp.where(rising, below, above).astype(F32)
-            going_up = going_down = send.astype(BF16)
-        else:
-            going_up = product(rows_for(far, near, (plane - step) % planes, side))
-            going_down = product(rows_for(far, near, (plane + step) % planes, side))
-            going_up = (going_up + below.astype(F32)).astype(BF16)
-            going_down = (going_down + above.astype(F32)).astype(BF16)
-        return lax.ppermute(going_up, "dp", upward), lax.ppermute(going_down, "dp", downward)
+            return send.astype(BF16), send.astype(BF16)
+        sending = []
+        for target, so_far in (((plane - step) % planes, below), ((plane + step) % planes, above)):
+            there = (target >= mid) == rising
+            rows = jnp.where(there, take(far[:, side], target % mid), take(near[:, side], target % mid))
+            sending.append((product(rows) + so_far.astype(F32)).astype(BF16))
+        return tuple(sending)
 
-    passed = [(down_local, down_local)]
-    passed.append(pass_on(*passed[0], 1))
-    near_rows = routed(near_first, mid)
+    def send_on(sending, step):
+        upward = [(2 * i + c, 2 * i + 2 + c) for i in range(step) for c in (0, 1)]
+        downward = [(2 * (planes - 1 - i) + c, 2 * (planes - 2 - i) + c) for i in range(step) for c in (0, 1)]
+        if step == 1:
+            both = lax.ppermute(sending[0], "dp", upward + downward)
+            return both, both
+        return lax.ppermute(sending[0], "dp", upward), lax.ppermute(sending[1], "dp", downward)
+
+    near = whole(near_first, mid)
     sums = [(None, None), (None, None)]
     for step in range(1, planes):
-        sums[0] = add_on(far_rows, near_rows, 0, *sums[0], step)
-        far_rows, sums[1], passed[step] = lax.optimization_barrier((far_rows, sums[1], passed[step]))
-        if step == mid:
-            far_rows, near_rows = lax.optimization_barrier((far_rows, near_rows))
+        sums[0] = send_on(add_on(0, *sums[0], step), step)
+        if step > 1:
+            far, sums[1], passed[step] = together(far, sums[1], passed[step])
         if step + 1 < planes:
             passed.append(pass_on(*passed[step], step + 1))
-        sums[1] = add_on(far_rows, near_rows, 1, *sums[1], step)
+        sending = add_on(1, *sums[1], step)
+        _, sums[0] = together(sending, sums[0])
+        sums[1] = send_on(sending, step)
     pieces = [down_local] + [
         jnp.where(plane >= step, passed[step][0], passed[planes - step][1]) for step in range(1, planes)
     ]
     pieces = jnp.stack(pieces)
     out_weight = jnp.concatenate([take(pieces, (plane - p) % planes) for p in range(planes)], axis=1)
-    out_weight, near_rows = lax.optimization_barrier((out_weight, near_rows))
 
     def returned(side):
+        total = product(take(near[:, side], plane % mid))
         below, above = sums[side]
-        total = product(take(near_rows[:, side], plane % mid)) + below.astype(F32) + above.astype(F32)
+        total = total + below.astype(F32) + above.astype(F32)
         hidden = (jax.nn.silu(total[:, :half]) * total[:, half:]).astype(BF16)
         apart = other(hidden)
         hidden = jnp.concatenate(
             [jnp.where(core == 0, hidden, apart), jnp.where(core == 0, apart, hidden)], axis=1
         )
-        return jnp.dot(hidden, out_weight, preferred_element_type=F32).astype(BF16).reshape(groups, CAP, -1)
+        outputs = jnp.dot(hidden, out_weight, preferred_element_type=F32).astype(BF16).reshape(groups, CAP, -1)
+        return jnp.concatenate(across(split(outputs)), axis=0)
 
-    def combined(side, blocks):
-        back = jnp.concatenate(across(split(blocks)), axis=0)
+    def combined(side, back):
         side_slot = take(slot, 2 * plane + side)
         coarse = lax.reduce_precision(probs[side], 8, 7)
         weights = [
@@ -152,13 +160,14 @@
         return (both[:tok_count] + both[tok_count:]).astype(BF16)
 
     first = returned(0)
-    first, sums[1] = lax.optimization_barrier((first, sums[1]))
+    first, sums[1] = together(first, sums[1])
     mixed = [combined(0, first), combined(1, returned(1))]
     mine = jnp.where(core == 0, mixed[0], mixed[1])
     theirs = other(jnp.where(core == 0, mixed[1], mixed[0]))
     sides = [jnp.where(core == 0, mine, theirs), jnp.where(core == 0, theirs, mine)]
-    sides = [side.reshape(tok_count, planes, width) for side in sides]
-    return jnp.stack(sides, axis=2).reshape(tok_count, model_width)
+    return jnp.concatenate(
+        [side[:, p * width : (p + 1) * width] for p in range(planes) for side in sides], axis=1
+    )
 
 
 def solution(mesh):

time: 276 us -> 255 us (0.924)
  starting transfers between devices: 88.1 us -> 58.4 us
  waiting for transfers between devices: 139 us -> 147 us
    ppermute x12 -> x10, starting transfers between devices: 56.6 us -> 33.6 us  [the longest x4 20.5 us: send_on(): lax.ppermute(sending[0], 'dp', upward)]
    ppermute x3, waiting for transfers between devices: 0.01 us -> 10.8 us  [pass_on(): lax.ppermute(above, 'dp', downward)]
    ppermute x12 -> x10, waiting for transfers between devices: 64.2 us -> 55.2 us  [the longest x4 35.1 us: send_on(): lax.ppermute(sending[0], 'dp', upward)]
    ppermute x7, waiting for transfers between devices: 5.27 us -> 9.47 us  [other(): return lax.ppermute(array, 'dp', swap)]
    unnamed x10 -> x21, local copies, waits for them, and re-layouts: 2.45 us -> 6.07 us
    ppermute x12 -> x9, starting transfers between devices: 14.1 us -> 10.6 us  [across(): lax.ppermute(blocks[k], 'expert', [(i, i ^ k) for i in range(groups)])]
    ppermute x3, starting transfers between devices: 6.16 us -> 2.89 us  [pass_on(): lax.ppermute(below, 'dp', upward)]
    ppermute x12 -> x9, waiting for transfers between devices: 51.7 us -> 53.9 us  [across(): lax.ppermute(blocks[k], 'expert', [(i, i ^ k) for i in range(groups)])]
  transfers between devices with their start and end apart: 38 -> 33, of which waited for: 22 -> 21; matrix products, arithmetic and copies ran while one was open for 12% -> 13% of each run, Pallas kernels for 0% -> 0%
where the time goes in v2:
time: 255 us; the launch traced here: 254 us
  waiting for transfers between devices  147 us (58%)
  starting transfers between devices  58.4 us (23%)
  matrix products  18.9 us (7%)
  other arithmetic  16.1 us (6%)
  local copies, waits for them, and re-layouts  12.6 us (5%)
    ppermute x9, waiting for transfers between devices, across(): lax.ppermute(blocks[k], 'expert', [(i, i ^ k) for i in range(groups)])  53.9 us
    ppermute x4, waiting for transfers between devices, send_on(): lax.ppermute(sending[0], 'dp', upward)  35.1 us
    ppermute x4, starting transfers between devices, send_on(): lax.ppermute(sending[0], 'dp', upward)  20.5 us
    all_to_all x1, waiting for transfers between devices, on_device(): lax.all_to_all(sent, 'dp', split_axis=1, concat_axis=0, tiled=True)  17.5 us
    ppermute x2, waiting for transfers between devices, send_on(): both = lax.ppermute(sending[0], 'dp', upward + downward)  17.4 us
    dot_general x10, matrix products, product(): return jnp.dot(rows, in_weight, preferred_element_type=F32)  12 us
    ppermute x3, waiting for transfers between devices, pass_on(): lax.ppermute(above, 'dp', downward)  10.8 us
    ppermute x9, starting transfers between devices, across(): lax.ppermute(blocks[k], 'expert', [(i, i ^ k) for i in range(groups)])  10.6 us
  transfers between devices with their start and end apart: 33, of which 21 were waited for; matrix products, arithmetic and copies ran while one was open for 13% of the time, Pallas kernels for 0%

profile of v2, /device:TPU:0, one launch (start us, length us, event | category | flops | bytes accessed | tf_op | source)
XLA Modules:
  0.0 253.9 jit_solution(14391427605877794545)
XLA Ops:
  1.5 1.6 copy.18
  5.4 6.3 %all-to-all-start = ((bf16[136,8,512]{2,0,1:T(8,128)(2,1)}), bf16[136,8,512]{2,0,1:T(8,128)(2,1)S(1)}, u32[]{:S(2)}, u32[]{:S(2)}) async-start(bf16[136,8,512]{2,0,1:T(8,128)(2,1)} %pad_maximum_fusion.8), calls=%async_computation | async-start | bytes 2228224 | tf_op jit(solution)/shard_map/all_to_all | solution.py:50
  11.7 2.0 dynamic-slice_bitcast_fusion.6
  15.6 2.9 %collective-permute-done.1 = f32[128,2]{0,1:T(2,128)S(1)} collective-permute-done((f32[128,2]{0,1:T(2,128)S(1)}, f32[128,2]{0,1:T(2,128)S(1)}, u32[]{:S(2)}, u32[]{:S(2)}) %collective-permute-start.1) | collective-permute-done | bytes 1056 | tf_op jit(solution)/shard_map/ppermute | solution.py:39
  19.0 3.2 %pad_maximum_fusion.2 = bf16[1024,1536]{1,0:T(8,128)(2,1)} fusion(bf16[512,1536]{1,0:T(8,128)(2,1)} %collective-permute-done, bf16[512,768]{1,0:T(8,128)(2,1)S(1)} %get-tuple-element.80, bf16[512,768]{1,0:T(8,128)(2,1)S(1)} %get-tuple-element.119), kind=kLoop, calls=%fused_computation.2 | loop fusion | flops 9437184 | bytes 6291456 | tf_op jit(solution)/shard_map/concatenate | solution.py:56
  22.2 17.5 %all-to-all-done = bf16[136,8,512]{2,0,1:T(8,128)(2,1)S(1)} async-done(((bf16[136,8,512]{2,0,1:T(8,128)(2,1)}), bf16[136,8,512]{2,0,1:T(8,128)(2,1)S(1)}, u32[]{:S(2)}, u32[]{:S(2)}) %all-to-all-start) | async-done | bytes 1114144 | tf_op jit(solution)/shard_map/all_to_all | solution.py:50
  48.1 14.5 %collective-permute-done.2 = bf16[8,80,512]{2,1,0:T(8,128)(2,1)} collective-permute-done((bf16[8,80,512]{2,1,0:T(8,128)(2,1)}, bf16[8,80,512]{2,1,0:T(8,128)(2,1)}, u32[]{:S(2)}, u32[]{:S(2)}) %collective-permute-start.2) | collective-permute-done | bytes 655392 | tf_op jit(solution)/shard_map/ppermute | solution.py:67
  62.5 13.9 %collective-permute-done.3 = bf16[8,80,512]{2,1,0:T(8,128)(2,1)} collective-permute-done((bf16[8,80,512]{2,1,0:T(8,128)(2,1)}, bf16[8,80,512]{2,1,0:T(8,128)(2,1)}, u32[]{:S(2)}, u32[]{:S(2)}) %collective-permute-start.3) | collective-permute-done | bytes 655392 | tf_op jit(solution)/shard_map/ppermute | solution.py:67
  80.1 2.6 %collective-permute-done.8 = bf16[2,640,512]{2,1,0:T(8,128)(2,1)} collective-permute-done((bf16[2,640,512]{2,1,0:T(8,128)(2,1)S(1)}, bf16[2,640,512]{2,1,0:T(8,128)(2,1)}, u32[]{:S(2)}, u32[]{:S(2)}) %collective-permute-start.8) | collective-permute-done | bytes 1310752 | tf_op jit(solution)/shard_map/ppermute | solution.py:39
  82.7 1.7 pad_maximum_fusion.5
  87.4 4.3 %collective-permute-start.16 = (bf16[320,1536]{1,0:T(8,128)(2,1)S(1)}, bf16[320,1536]{1,0:T(8,128)(2,1)S(1)}, u32[]{:S(2)}, u32[]{:S(2)}) collective-permute-start(bf16[320,1536]{1,0:T(8,128)(2,1)S(1)} %convolution_convert_fusion.2), channel_id=1, source_target_pairs={{0,8},{4,12},{24,16},{28,20},{1,9},{5,13},{25,17},{29,21},{2,10},{... | collective-permute-start | bytes 2949128 | tf_op jit(solution)/shard_map/ppermute | solution.py:119
  95.0 4.6 %collective-permute-start.9 = (bf16[320,1536]{1,0:T(8,128)(2,1)S(1)}, bf16[320,1536]{1,0:T(8,128)(2,1)S(1)}, u32[]{:S(2)}, u32[]{:S(2)}) collective-permute-start(bf16[320,1536]{1,0:T(8,128)(2,1)S(1)} %convolution_convert_fusion.3), channel_id=1, source_target_pairs={{0,8},{4,12},{24,16},{28,20},{1,9},{5,13},{25,17},{29,21},{2,10},{... | collective-permute-start | bytes 2949128 | tf_op jit(solution)/shard_map/ppermute | solution.py:119
  100.3 13.5 %collective-permute-done.16 = bf16[320,1536]{1,0:T(8,128)(2,1)S(1)} collective-permute-done((bf16[320,1536]{1,0:T(8,128)(2,1)S(1)}, bf16[320,1536]{1,0:T(8,128)(2,1)S(1)}, u32[]{:S(2)}, u32[]{:S(2)}) %collective-permute-start.16) | collective-permute-done | bytes 983072 | tf_op jit(solution)/shard_map/ppermute | solution.py:119
  115.0 4.4 %collective-permute-start.17 = (bf16[320,1536]{1,0:T(8,128)(2,1)S(1)}, bf16[320,1536]{1,0:T(8,128)(2,1)S(1)}, u32[]{:S(2)}, u32[]{:S(2)}) collective-permute-start(bf16[320,1536]{1,0:T(8,128)(2,1)S(1)} %add_convert_fusion.2), channel_id=1, source_target_pairs={{0,8},{4,12},{8,16},{12,20},{1,9},{5,13},{9,17},{13,21},{2,10},{6,... | collective-permute-start | bytes 2949128 | tf_op jit(solution)/shard_map/ppermute | solution.py:121
  121.4 9.5 %collective-permute-done.11 = bf16[1536,512]{1,0:T(8,128)(2,1)S(1)} collective-permute-done((bf16[1536,512]{1,0:T(8,128)(2,1)}, bf16[1536,512]{1,0:T(8,128)(2,1)S(1)}, u32[]{:S(2)}, u32[]{:S(2)}) %collective-permute-start.11) | collective-permute-done | bytes 1572896 | tf_op jit(solution)/shard_map/ppermute | solution.py:73
  130.9 3.9 %collective-permute-done.9 = bf16[320,1536]{1,0:T(8,128)(2,1)S(1)} collective-permute-done((bf16[320,1536]{1,0:T(8,128)(2,1)S(1)}, bf16[320,1536]{1,0:T(8,128)(2,1)S(1)}, u32[]{:S(2)}, u32[]{:S(2)}) %collective-permute-start.9) | collective-permute-done | bytes 983072 | tf_op jit(solution)/shard_map/ppermute | solution.py:119
  138.3 4.7 %collective-permute-start.12 = (bf16[320,1536]{1,0:T(8,128)(2,1)S(1)}, bf16[320,1536]{1,0:T(8,128)(2,1)S(1)}, u32[]{:S(2)}, u32[]{:S(2)}) collective-permute-start(bf16[320,1536]{1,0:T(8,128)(2,1)S(1)} %add_convert_fusion.5), channel_id=1, source_target_pairs={{0,8},{4,12},{8,16},{12,20},{1,9},{5,13},{9,17},{13,21},{2,10},{6,... | collective-permute-start | bytes 2949128 | tf_op jit(solution)/shard_map/ppermute | solution.py:121
  143.1 12.8 %collective-permute-done.17 = bf16[320,1536]{1,0:T(8,128)(2,1)S(1)} collective-permute-done((bf16[320,1536]{1,0:T(8,128)(2,1)S(1)}, bf16[320,1536]{1,0:T(8,128)(2,1)S(1)}, u32[]{:S(2)}, u32[]{:S(2)}) %collective-permute-start.17) | collective-permute-done | bytes 983072 | tf_op jit(solution)/shard_map/ppermute | solution.py:121
  160.7 15.4 %collective-permute-done.12 = bf16[320,1536]{1,0:T(8,128)(2,1)S(1)} collective-permute-done((bf16[320,1536]{1,0:T(8,128)(2,1)S(1)}, bf16[320,1536]{1,0:T(8,128)(2,1)S(1)}, u32[]{:S(2)}, u32[]{:S(2)}) %collective-permute-start.12) | collective-permute-done | bytes 983072 | tf_op jit(solution)/shard_map/ppermute | solution.py:121
  176.2 4.4 %collective-permute-start.19 = (bf16[320,1536]{1,0:T(8,128)(2,1)S(1)}, bf16[320,1536]{1,0:T(8,128)(2,1)S(1)}, u32[]{:S(2)}, u32[]{:S(2)}) collective-permute-start(bf16[320,1536]{1,0:T(8,128)(2,1)S(1)} %add_convert_fusion.1), channel_id=1, source_target_pairs={{0,8},{4,12},{8,16},{12,20},{16,24},{20,28},{1,9},{5,13},{9,17},{1... | collective-permute-start | bytes 2949128 | tf_op jit(solution)/shard_map/ppermute | solution.py:121
  184.5 6.9 %collective-permute-start.25 = (bf16[320,1536]{1,0:T(8,128)(2,1)S(1)}, bf16[320,1536]{1,0:T(8,128)(2,1)S(1)}, u32[]{:S(2)}, u32[]{:S(2)}) collective-permute-start(bf16[320,1536]{1,0:T(8,128)(2,1)S(1)} %add_convert_fusion.4), channel_id=1, source_target_pairs={{0,8},{4,12},{8,16},{12,20},{16,24},{20,28},{1,9},{5,13},{9,17},{1... | collective-permute-start | bytes 2949128 | tf_op jit(solution)/shard_map/ppermute | solution.py:121
  193.2 2.7 %collective-permute-done.20 = bf16[320,1536]{1,0:T(8,128)(2,1)S(1)} collective-permute-done((bf16[320,1536]{1,0:T(8,128)(2,1)S(1)}, bf16[320,1536]{1,0:T(8,128)(2,1)S(1)}, u32[]{:S(2)}, u32[]{:S(2)}) %collective-permute-start.20) | collective-permute-done | bytes 983072 | tf_op jit(solution)/shard_map/ppermute | solution.py:121
  195.9 6.8 %collective-permute-done.19 = bf16[320,1536]{1,0:T(8,128)(2,1)S(1)} collective-permute-done((bf16[320,1536]{1,0:T(8,128)(2,1)S(1)}, bf16[320,1536]{1,0:T(8,128)(2,1)S(1)}, u32[]{:S(2)}, u32[]{:S(2)}) %collective-permute-start.19) | collective-permute-done | bytes 983072 | tf_op jit(solution)/shard_map/ppermute | solution.py:121
  206.3 2.2 convolution_convert_fusion.1
  213.4 5.9 %collective-permute-done.22 = bf16[80,2048]{1,0:T(8,128)(2,1)S(1)} collective-permute-done((bf16[80,2048]{1,0:T(8,128)(2,1)S(1)}, bf16[80,2048]{1,0:T(8,128)(2,1)S(1)}, u32[]{:S(2)}, u32[]{:S(2)}) %collective-permute-start.22) | collective-permute-done | bytes 327712 | tf_op jit(solution)/shard_map/ppermute | solution.py:67
  219.3 5.1 %collective-permute-done.23 = bf16[80,2048]{1,0:T(8,128)(2,1)S(1)} collective-permute-done((bf16[80,2048]{1,0:T(8,128)(2,1)S(1)}, bf16[80,2048]{1,0:T(8,128)(2,1)S(1)}, u32[]{:S(2)}, u32[]{:S(2)}) %collective-permute-start.23) | collective-permute-done | bytes 327712 | tf_op jit(solution)/shard_map/ppermute | solution.py:67
  224.3 1.6 collective-permute-done.24
  227.1 1.6 collective-permute-done.27
  229.2 2.2 convolution_convert_fusion
  236.0 6.2 %collective-permute-done.28 = bf16[80,2048]{1,0:T(8,128)(2,1)S(1)} collective-permute-done((bf16[80,2048]{1,0:T(8,128)(2,1)S(1)}, bf16[80,2048]{1,0:T(8,128)(2,1)S(1)}, u32[]{:S(2)}, u32[]{:S(2)}) %collective-permute-start.28) | collective-permute-done | bytes 327712 | tf_op jit(solution)/shard_map/ppermute | solution.py:67
  242.2 6.7 %collective-permute-done.29 = bf16[80,2048]{1,0:T(8,128)(2,1)S(1)} collective-permute-done((bf16[80,2048]{1,0:T(8,128)(2,1)S(1)}, bf16[80,2048]{1,0:T(8,128)(2,1)S(1)}, u32[]{:S(2)}, u32[]{:S(2)}) %collective-permute-start.29) | collective-permute-done | bytes 327712 | tf_op jit(solution)/shard_map/ppermute | solution.py:67
  250.1 1.9 collective-permute-done.31
  (122 shorter events, 59.1 us)
Async XLA Ops:
  5.4 34.3 %all-to-all-start = ((bf16[136,8,512]{2,0,1:T(8,128)(2,1)}), bf16[136,8,512]{2,0,1:T(8,128)(2,1)S(1)}, u32[]{:S(2)}, u32[]{:S(2)}) async-start(bf16[136,8,512]{2,0,1:T(8,128)(2,1)} %pad_maximum_fusion.8), calls=%async_computation | async-start | bytes 2228224 | tf_op jit(solution)/shard_map/all_to_all | solution.py:50
  15.1 3.9 %collective-permute-start = (bf16[512,1536]{1,0:T(8,128)(2,1)}, bf16[512,1536]{1,0:T(8,128)(2,1)}, u32[]{:S(2)}, u32[]{:S(2)}) collective-permute-start(bf16[512,1536]{1,0:T(8,128)(2,1)} %pad_maximum_fusion.6), channel_id=1, source_target_pairs={{0,4},{4,0},{8,12},{12,8},{16,20},{20,16},{24,28},{28,24},{1,5},{5... | collective-permute-start | bytes 4718600 | tf_op jit(solution)/shard_map/ppermute | solution.py:39
  15.6 2.9 %collective-permute-start.1 = (f32[128,2]{0,1:T(2,128)S(1)}, f32[128,2]{0,1:T(2,128)S(1)}, u32[]{:S(2)}, u32[]{:S(2)}) collective-permute-start(f32[128,2]{0,1:T(2,128)S(1)} %copy-done.5), channel_id=1, source_target_pairs={{0,4},{4,0},{8,12},{12,8},{16,20},{20,16},{24,28},{28,24},{1,5},{5... | collective-permute-start | bytes 3080 | tf_op jit(solution)/shard_map/ppermute | solution.py:39
  39.7 38.3 %collective-permute-start.5 = (bf16[1536,512]{1,0:T(8,128)(2,1)}, bf16[1536,512]{1,0:T(8,128)(2,1)S(1)}, u32[]{:S(2)}, u32[]{:S(2)}) collective-permute-start(bf16[1536,512]{1,0:T(8,128)(2,1)} %bitcast.147), channel_id=1, source_target_pairs={{0,8},{4,12},{8,16},{12,20},{16,24},{20,28},{1,9},{5,13},{9,17},{1... | collective-permute-start | bytes 4718600 | tf_op jit(solution)/shard_map/ppermute | solution.py:73
  41.1 38.2 %collective-permute-start.6 = (bf16[1536,512]{1,0:T(8,128)(2,1)}, bf16[1536,512]{1,0:T(8,128)(2,1)}, u32[]{:S(2)}, u32[]{:S(2)}) collective-permute-start(bf16[1536,512]{1,0:T(8,128)(2,1)} %bitcast.148), channel_id=1, source_target_pairs={{8,0},{12,4},{16,8},{20,12},{24,16},{28,20},{9,1},{13,5},{17,9},{2... | collective-permute-start | bytes 4718600 | tf_op jit(solution)/shard_map/ppermute | solution.py:73
  44.6 18.0 %collective-permute-start.2 = (bf16[8,80,512]{2,1,0:T(8,128)(2,1)}, bf16[8,80,512]{2,1,0:T(8,128)(2,1)}, u32[]{:S(2)}, u32[]{:S(2)}) collective-permute-start(bf16[8,80,512]{2,1,0:T(8,128)(2,1)} %get-tuple-element.73), channel_id=1, source_target_pairs={{0,1},{1,0},{2,3},{3,2},{4,5},{5,4},{6,7},{7,6},{8,9},{9,8},{10,11... | collective-permute-start | bytes 1966088 | tf_op jit(solution)/shard_map/ppermute | solution.py:67
  46.1 30.4 %collective-permute-start.3 = (bf16[8,80,512]{2,1,0:T(8,128)(2,1)}, bf16[8,80,512]{2,1,0:T(8,128)(2,1)}, u32[]{:S(2)}, u32[]{:S(2)}) collective-permute-start(bf16[8,80,512]{2,1,0:T(8,128)(2,1)} %get-tuple-element.75), channel_id=1, source_target_pairs={{0,2},{1,3},{2,0},{3,1},{4,6},{5,7},{6,4},{7,5},{8,10},{9,11},{10,... | collective-permute-start | bytes 1966088 | tf_op jit(solution)/shard_map/ppermute | solution.py:67
  47.6 28.8 %collective-permute-start.4 = (bf16[8,80,512]{2,1,0:T(8,128)(2,1)S(1)}, bf16[8,80,512]{2,1,0:T(8,128)(2,1)}, u32[]{:S(2)}, u32[]{:S(2)}) collective-permute-start(bf16[8,80,512]{2,1,0:T(8,128)(2,1)S(1)} %get-tuple-element.74), channel_id=1, source_target_pairs={{0,3},{1,2},{2,1},{3,0},{4,7},{5,6},{6,5},{7,4},{8,11},{9,10},{10,... | collective-permute-start | bytes 1966088 | tf_op jit(solution)/shard_map/ppermute | solution.py:67
  79.4 3.2 %collective-permute-start.8 = (bf16[2,640,512]{2,1,0:T(8,128)(2,1)S(1)}, bf16[2,640,512]{2,1,0:T(8,128)(2,1)}, u32[]{:S(2)}, u32[]{:S(2)}) collective-permute-start(bf16[2,640,512]{2,1,0:T(8,128)(2,1)S(1)} %get-tuple-element.71), channel_id=1, source_target_pairs={{0,4},{4,0},{8,12},{12,8},{16,20},{20,16},{24,28},{28,24},{1,5},{5... | collective-permute-start | bytes 3932168 | tf_op jit(solution)/shard_map/ppermute | solution.py:39
  79.8 19.8 %collective-permute-start.7 = (bf16[2,640,512]{2,1,0:T(8,128)(2,1)S(1)}, bf16[2,640,512]{2,1,0:T(8,128)(2,1)S(1)}, u32[]{:S(2)}, u32[]{:S(2)}) collective-permute-start(bf16[2,640,512]{2,1,0:T(8,128)(2,1)S(1)} %get-tuple-element.70), channel_id=1, source_target_pairs={{0,4},{4,0},{8,12},{12,8},{16,20},{20,16},{24,28},{28,24},{1,5},{5... | collective-permute-start | bytes 3932168 | tf_op jit(solution)/shard_map/ppermute | solution.py:39
  87.4 26.3 %collective-permute-start.16 = (bf16[320,1536]{1,0:T(8,128)(2,1)S(1)}, bf16[320,1536]{1,0:T(8,128)(2,1)S(1)}, u32[]{:S(2)}, u32[]{:S(2)}) collective-permute-start(bf16[320,1536]{1,0:T(8,128)(2,1)S(1)} %convolution_convert_fusion.2), channel_id=1, source_target_pairs={{0,8},{4,12},{24,16},{28,20},{1,9},{5,13},{25,17},{29,21},{2,10},{... | collective-permute-start | bytes 2949128 | tf_op jit(solution)/shard_map/ppermute | solution.py:119
  91.8 29.6 %collective-permute-start.10 = (bf16[1536,512]{1,0:T(8,128)(2,1)S(1)}, bf16[1536,512]{1,0:T(8,128)(2,1)S(1)}, u32[]{:S(2)}, u32[]{:S(2)}) collective-permute-start(bf16[1536,512]{1,0:T(8,128)(2,1)S(1)} %copy-done.3), channel_id=1, source_target_pairs={{8,16},{12,20},{16,24},{20,28},{9,17},{13,21},{17,25},{21,29},{10,... | collective-permute-start | bytes 4718600 | tf_op jit(solution)/shard_map/ppermute | solution.py:73
  92.5 38.4 %collective-permute-start.11 = (bf16[1536,512]{1,0:T(8,128)(2,1)}, bf16[1536,512]{1,0:T(8,128)(2,1)S(1)}, u32[]{:S(2)}, u32[]{:S(2)}) collective-permute-start(bf16[1536,512]{1,0:T(8,128)(2,1)} %collective-permute-done.6), channel_id=1, source_target_pairs={{8,0},{12,4},{16,8},{20,12},{9,1},{13,5},{17,9},{21,13},{10,2},{14... | collective-permute-start | bytes 4718600 | tf_op jit(solution)/shard_map/ppermute | solution.py:73
  95.0 39.8 %collective-permute-start.9 = (bf16[320,1536]{1,0:T(8,128)(2,1)S(1)}, bf16[320,1536]{1,0:T(8,128)(2,1)S(1)}, u32[]{:S(2)}, u32[]{:S(2)}) collective-permute-start(bf16[320,1536]{1,0:T(8,128)(2,1)S(1)} %convolution_convert_fusion.3), channel_id=1, source_target_pairs={{0,8},{4,12},{24,16},{28,20},{1,9},{5,13},{25,17},{29,21},{2,10},{... | collective-permute-start | bytes 2949128 | tf_op jit(solution)/shard_map/ppermute | solution.py:119
  115.0 40.9 %collective-permute-start.17 = (bf16[320,1536]{1,0:T(8,128)(2,1)S(1)}, bf16[320,1536]{1,0:T(8,128)(2,1)S(1)}, u32[]{:S(2)}, u32[]{:S(2)}) collective-permute-start(bf16[320,1536]{1,0:T(8,128)(2,1)S(1)} %add_convert_fusion.2), channel_id=1, source_target_pairs={{0,8},{4,12},{8,16},{12,20},{1,9},{5,13},{9,17},{13,21},{2,10},{6,... | collective-permute-start | bytes 2949128 | tf_op jit(solution)/shard_map/ppermute | solution.py:121
  120.6 36.3 %collective-permute-start.18 = (bf16[320,1536]{1,0:T(8,128)(2,1)S(1)}, bf16[320,1536]{1,0:T(8,128)(2,1)S(1)}, u32[]{:S(2)}, u32[]{:S(2)}) collective-permute-start(bf16[320,1536]{1,0:T(8,128)(2,1)S(1)} %add_convert_fusion.2), channel_id=1, source_target_pairs={{24,16},{28,20},{16,8},{20,12},{25,17},{29,21},{17,9},{21,13},{26,... | collective-permute-start | bytes 2949128 | tf_op jit(solution)/shard_map/ppermute | solution.py:121
  134.8 45.8 %collective-permute-start.14 = (bf16[1536,512]{1,0:T(8,128)(2,1)S(1)}, bf16[1536,512]{1,0:T(8,128)(2,1)S(1)}, u32[]{:S(2)}, u32[]{:S(2)}) collective-permute-start(bf16[1536,512]{1,0:T(8,128)(2,1)S(1)} %collective-permute-done.10), channel_id=1, source_target_pairs={{16,24},{20,28},{17,25},{21,29},{18,26},{22,30},{19,27},{23,31}} | collective-permute-start | bytes 4718600 | tf_op jit(solution)/shard_map/ppermute | solution.py:73
  135.6 45.0 %collective-permute-start.15 = (bf16[1536,512]{1,0:T(8,128)(2,1)S(1)}, bf16[1536,512]{1,0:T(8,128)(2,1)S(1)}, u32[]{:S(2)}, u32[]{:S(2)}) collective-permute-start(bf16[1536,512]{1,0:T(8,128)(2,1)S(1)} %collective-permute-done.11), channel_id=1, source_target_pairs={{8,0},{12,4},{9,1},{13,5},{10,2},{14,6},{11,3},{15,7}} | collective-permute-start | bytes 4718600 | tf_op jit(solution)/shard_map/ppermute | solution.py:73
  138.3 37.8 %collective-permute-start.12 = (bf16[320,1536]{1,0:T(8,128)(2,1)S(1)}, bf16[320,1536]{1,0:T(8,128)(2,1)S(1)}, u32[]{:S(2)}, u32[]{:S(2)}) collective-permute-start(bf16[320,1536]{1,0:T(8,128)(2,1)S(1)} %add_convert_fusion.5), channel_id=1, source_target_pairs={{0,8},{4,12},{8,16},{12,20},{1,9},{5,13},{9,17},{13,21},{2,10},{6,... | collective-permute-start | bytes 2949128 | tf_op jit(solution)/shard_map/ppermute | solution.py:121
  155.9 24.7 %collective-permute-start.13 = (bf16[320,1536]{1,0:T(8,128)(2,1)S(1)}, bf16[320,1536]{1,0:T(8,128)(2,1)S(1)}, u32[]{:S(2)}, u32[]{:S(2)}) collective-permute-start(bf16[320,1536]{1,0:T(8,128)(2,1)S(1)} %add_convert_fusion.5), channel_id=1, source_target_pairs={{24,16},{28,20},{16,8},{20,12},{25,17},{29,21},{17,9},{21,13},{26,... | collective-permute-start | bytes 2949128 | tf_op jit(solution)/shard_map/ppermute | solution.py:121
  158.2 37.7 %collective-permute-start.20 = (bf16[320,1536]{1,0:T(8,128)(2,1)S(1)}, bf16[320,1536]{1,0:T(8,128)(2,1)S(1)}, u32[]{:S(2)}, u32[]{:S(2)}) collective-permute-start(bf16[320,1536]{1,0:T(8,128)(2,1)S(1)} %add_convert_fusion), channel_id=1, source_target_pairs={{24,16},{28,20},{16,8},{20,12},{8,0},{12,4},{25,17},{29,21},{17,9}... | collective-permute-start | bytes 2949128 | tf_op jit(solution)/shard_map/ppermute | solution.py:121
  176.2 26.6 %collective-permute-start.19 = (bf16[320,1536]{1,0:T(8,128)(2,1)S(1)}, bf16[320,1536]{1,0:T(8,128)(2,1)S(1)}, u32[]{:S(2)}, u32[]{:S(2)}) collective-permute-start(bf16[320,1536]{1,0:T(8,128)(2,1)S(1)} %add_convert_fusion.1), channel_id=1, source_target_pairs={{0,8},{4,12},{8,16},{12,20},{16,24},{20,28},{1,9},{5,13},{9,17},{1... | collective-permute-start | bytes 2949128 | tf_op jit(solution)/shard_map/ppermute | solution.py:121
  183.2 42.9 %collective-permute-start.26 = (bf16[320,1536]{1,0:T(8,128)(2,1)S(1)}, bf16[320,1536]{1,0:T(8,128)(2,1)S(1)}, u32[]{:S(2)}, u32[]{:S(2)}) collective-permute-start(bf16[320,1536]{1,0:T(8,128)(2,1)S(1)} %add_convert_fusion.3), channel_id=1, source_target_pairs={{24,16},{28,20},{16,8},{20,12},{8,0},{12,4},{25,17},{29,21},{17,9}... | collective-permute-start | bytes 2949128 | tf_op jit(solution)/shard_map/ppermute | solution.py:121
  184.5 41.6 %collective-permute-start.25 = (bf16[320,1536]{1,0:T(8,128)(2,1)S(1)}, bf16[320,1536]{1,0:T(8,128)(2,1)S(1)}, u32[]{:S(2)}, u32[]{:S(2)}) collective-permute-start(bf16[320,1536]{1,0:T(8,128)(2,1)S(1)} %add_convert_fusion.4), channel_id=1, source_target_pairs={{0,8},{4,12},{8,16},{12,20},{16,24},{20,28},{1,9},{5,13},{9,17},{1... | collective-permute-start | bytes 2949128 | tf_op jit(solution)/shard_map/ppermute | solution.py:121
  203.5 2.4 collective-permute-start.21
  208.6 10.7 %collective-permute-start.22 = (bf16[80,2048]{1,0:T(8,128)(2,1)S(1)}, bf16[80,2048]{1,0:T(8,128)(2,1)S(1)}, u32[]{:S(2)}, u32[]{:S(2)}) collective-permute-start(bf16[80,2048]{1,0:T(8,128)(2,1)S(1)} %get-tuple-element.89), channel_id=1, source_target_pairs={{0,1},{1,0},{2,3},{3,2},{4,5},{5,4},{6,7},{7,6},{8,9},{9,8},{10,11... | collective-permute-start | bytes 983048 | tf_op jit(solution)/shard_map/ppermute | solution.py:67
  209.9 14.4 %collective-permute-start.23 = (bf16[80,2048]{1,0:T(8,128)(2,1)S(1)}, bf16[80,2048]{1,0:T(8,128)(2,1)S(1)}, u32[]{:S(2)}, u32[]{:S(2)}) collective-permute-start(bf16[80,2048]{1,0:T(8,128)(2,1)S(1)} %get-tuple-element.88), channel_id=1, source_target_pairs={{0,2},{1,3},{2,0},{3,1},{4,6},{5,7},{6,4},{7,5},{8,10},{9,11},{10,... | collective-permute-start | bytes 983048 | tf_op jit(solution)/shard_map/ppermute | solution.py:67
  210.7 15.2 %collective-permute-start.24 = (bf16[80,2048]{1,0:T(8,128)(2,1)S(1)}, bf16[80,2048]{1,0:T(8,128)(2,1)S(1)}, u32[]{:S(2)}, u32[]{:S(2)}) collective-permute-start(bf16[80,2048]{1,0:T(8,128)(2,1)S(1)} %get-tuple-element.87), channel_id=1, source_target_pairs={{0,3},{1,2},{2,1},{3,0},{4,7},{5,6},{6,5},{7,4},{8,11},{9,10},{10,... | collective-permute-start | bytes 983048 | tf_op jit(solution)/shard_map/ppermute | solution.py:67
  231.6 10.6 %collective-permute-start.28 = (bf16[80,2048]{1,0:T(8,128)(2,1)S(1)}, bf16[80,2048]{1,0:T(8,128)(2,1)S(1)}, u32[]{:S(2)}, u32[]{:S(2)}) collective-permute-start(bf16[80,2048]{1,0:T(8,128)(2,1)S(1)} %get-tuple-element.85), channel_id=1, source_target_pairs={{0,1},{1,0},{2,3},{3,2},{4,5},{5,4},{6,7},{7,6},{8,9},{9,8},{10,11... | collective-permute-start | bytes 983048 | tf_op jit(solution)/shard_map/ppermute | solution.py:67
  232.4 16.5 %collective-permute-start.29 = (bf16[80,2048]{1,0:T(8,128)(2,1)S(1)}, bf16[80,2048]{1,0:T(8,128)(2,1)S(1)}, u32[]{:S(2)}, u32[]{:S(2)}) collective-permute-start(bf16[80,2048]{1,0:T(8,128)(2,1)S(1)} %get-tuple-element.84), channel_id=1, source_target_pairs={{0,2},{1,3},{2,0},{3,1},{4,6},{5,7},{6,4},{7,5},{8,10},{9,11},{10,... | collective-permute-start | bytes 983048 | tf_op jit(solution)/shard_map/ppermute | solution.py:67
  233.9 15.0 %collective-permute-start.30 = (bf16[80,2048]{1,0:T(8,128)(2,1)S(1)}, bf16[80,2048]{1,0:T(8,128)(2,1)S(1)}, u32[]{:S(2)}, u32[]{:S(2)}) collective-permute-start(bf16[80,2048]{1,0:T(8,128)(2,1)S(1)} %get-tuple-element.83), channel_id=1, source_target_pairs={{0,3},{1,2},{2,1},{3,0},{4,7},{5,6},{6,5},{7,4},{8,11},{9,10},{10,... | collective-permute-start | bytes 983048 | tf_op jit(solution)/shard_map/ppermute | solution.py:67
  250.1 2.0 collective-permute-start.31
  (7 other events, 14.8 us)

commit v3 on v2

v3 whole, which is shorter than its diff:
```python
import jax
import jax.numpy as jnp
from jax import lax
from jax.sharding import PartitionSpec as P

CAP = 80
PARTS = ((0, 40), (40, 80))
F32 = jnp.float32
BF16 = jnp.bfloat16
NOTE_ROWS = 8


def ranks_of(ids, groups):
    flat = ids.reshape(-1)
    count = flat.shape[0]
    onehot = (flat[:, None] == jnp.arange(groups, dtype=jnp.int32)).astype(BF16)
    before = (jnp.arange(count)[:, None] > jnp.arange(count)[None, :]).astype(BF16)
    ranks = jnp.dot(before, onehot, preferred_element_type=F32)
    return jnp.sum(ranks * onehot.astype(F32), axis=1).reshape(ids.shape)


def take(array, index):
    return lax.dynamic_index_in_dim(array, index, 0, keepdims=False)


def on_device(tokens, expert_ids, gate_probs, gate_weight, up_weight, down_weight):
    tok_count, model_width = tokens.shape
    top = expert_ids.shape[1]
    n_dp, groups = lax.axis_size("dp"), lax.axis_size("expert")
    planes = n_dp // 2
    place = lax.axis_index("dp")
    plane, core = place // 2, place % 2
    width = model_width // n_dp
    hidden_width = gate_weight.shape[2]
    half = hidden_width // 2
    slots = groups * CAP
    swap = [(i, i ^ 1) for i in range(n_dp)]

    def other(array):
        return lax.ppermute(array, "dp", swap)

    def columns(array, which):
        return lax.dynamic_slice_in_dim(array, which * half, half, 1)

    def split(array):
        return [take(array, which) for which in range(array.shape[0])]

    notes = jnp.concatenate([expert_ids.astype(F32).T, ranks_of(expert_ids, groups).T], axis=0)
    notes = jnp.pad(notes, ((0, NOTE_ROWS - 2 * top), (0, width - tok_count))).astype(BF16)
    sent = jnp.concatenate([tokens, jnp.tile(notes, (1, n_dp))], axis=0)
    arrived = lax.all_to_all(sent, "dp", split_axis=1, concat_axis=0, tiled=True)
    arrived = arrived.reshape(n_dp, tok_count + NOTE_ROWS, width)

    gate_local, up_local, down_local = gate_weight[0], up_weight[0], down_weight[0]
    keep = jnp.concatenate([columns(gate_local, core), columns(up_local, core)], axis=1)
    give = jnp.concatenate([columns(gate_local, 1 - core), columns(up_local, 1 - core)], axis=1)
    in_weight = jnp.concatenate([keep, other(give)], axis=0)
    other_probs = other(gate_probs)
    probs = jnp.where(core == 0, jnp.stack([gate_probs, other_probs]), jnp.stack([other_probs, gate_probs]))
    arrived, in_weight, probs = lax.optimization_barrier((arrived, in_weight, probs))

    told = arrived[:, tok_count : tok_count + 2 * top, :tok_count].astype(jnp.int32)
    slot = (told[:, :top] ^ lax.axis_index("expert")) * CAP + told[:, top:]
    slot_range = jnp.arange(slots, dtype=jnp.int32)[:, None]

    def across(blocks):
        return [blocks[0]] + [
            lax.ppermute(blocks[k], "expert", [(i, i ^ k) for i in range(groups)]) for k in range(1, groups)
        ]

    def pass_on(below, above, step):
        upward = [(2 * i + c, 2 * i + 2 + c) for i in range(step - 1, planes - 1) for c in (0, 1)]
        downward = [(2 * i + 2 + c, 2 * i + c) for i in range(planes - step) for c in (0, 1)]
        return lax.ppermute(below, "dp", upward), lax.ppermute(above, "dp", downward)

    passed = [(down_local, down_local)]
    passed.append(pass_on(*passed[0], 1))

    def routed(k):
        at = jnp.arange(k * CAP, (k + 1) * CAP, dtype=jnp.int32)[:, None]
        chosen = sum((slot[:, i, None, :] == at).astype(BF16) for i in range(top))
        return jnp.einsum("dst,dtc->dsc", chosen, arrived[:, :tok_count], preferred_element_type=F32).astype(BF16)

    rows = jnp.concatenate(across([routed(k) for k in range(groups)]), axis=1)
    rows = rows.reshape(planes, 2 * slots, width)
    rows, passed[1] = lax.optimization_barrier((rows, passed[1]))

    rows = rows.reshape(planes, 2, groups, CAP, width)
    rows = [jnp.swapaxes(rows[:, :, :, low:high], 1, 2).reshape(planes, -1, width) for low, high in PARTS]
    rows = [jnp.concatenate([some, other(some)], axis=2) for some in rows]

    def together(*values):
        return lax.optimization_barrier(values)

    mid = planes // 2
    rising = plane < mid

    def product(part, target):
        return jnp.dot(take(rows[part], target % planes), in_weight, preferred_element_type=F32)

    def add_on(part, below, above, step):
        if step <= mid:
            send = product(part, jnp.where(rising, plane - step, plane + step))
            if below is not None:
                send = send + jnp.where(rising, below, above).astype(F32)
            return send.astype(BF16), send.astype(BF16)
        going_up = product(part, plane - step) + below.astype(F32)
        going_down = product(part, plane + step) + above.astype(F32)
        return going_up.astype(BF16), going_down.astype(BF16)

    def send_on(sending, step):
        upward = [(2 * i + c, 2 * i + 2 + c) for i in range(step) for c in (0, 1)]
        downward = [(2 * (planes - 1 - i) + c, 2 * (planes - 2 - i) + c) for i in range(step) for c in (0, 1)]
        if step == 1:
            both = lax.ppermute(sending[0], "dp", upward + downward)
            return both, both
        return lax.ppermute(sending[0], "dp", upward), lax.ppermute(sending[1], "dp", downward)

    sums = [(None, None) for part in PARTS]
    for step in range(1, planes):
        for part in range(len(PARTS)):
            if part == 1 and step > 1:
                rows[1], sums[1], passed[step] = together(rows[1], sums[1], passed[step])
            if part == 1 and step + 1 < planes:
                passed.append(pass_on(*passed[step], step + 1))
            sending = add_on(part, *sums[part], step)
            if part > 0:
                _, sums[part - 1] = together(sending, sums[part - 1])
            sums[part] = send_on(sending, step)
    pieces = [down_local] + [
        jnp.where(plane >= step, passed[step][0], passed[planes - step][1]) for step in range(1, planes)
    ]
    pieces = jnp.stack(pieces)
    pieces = jnp.concatenate([take(pieces, (plane - p) % planes) for p in range(planes)], axis=1)
    out_weight = [lax.dynamic_slice_in_dim(pieces, which * half, half, 0) for which in (core, 1 - core)]

    def outputs_of(part):
        below, above = sums[part]
        total = product(part, plane) + below.astype(F32) + above.astype(F32)
        hidden = (jax.nn.silu(total[:, :half]) * total[:, half:]).astype(BF16)
        ours = jnp.dot(hidden, out_weight[0], preferred_element_type=F32)
        return (ours + jnp.dot(other(hidden), out_weight[1], preferred_element_type=F32)).astype(BF16)

    coarse = lax.reduce_precision(probs, 8, 7)

    def combined(part, blocks, side):
        low, high = PARTS[part]
        size = high - low
        back = jnp.concatenate([lax.dynamic_slice_in_dim(some, side * size, size, 0) for some in blocks], axis=0)
        side_slot, side_probs, side_coarse = take(slot, 2 * plane + side), take(probs, side), take(coarse, side)
        here = jnp.concatenate([jnp.arange(k * CAP + low, k * CAP + high, dtype=jnp.int32) for k in range(groups)])
        weights = [
            sum(jnp.where(side_slot[k, :, None] == here, some[:, k, None], 0.0) for k in range(top)).astype(BF16)
            for some in (side_coarse, side_probs - side_coarse)
        ]
        both = jnp.dot(jnp.concatenate(weights, axis=0), back, preferred_element_type=F32)
        return both[:tok_count] + both[tok_count:]

    mixed = [0.0, 0.0]
    for part in range(len(PARTS)):
        outputs = outputs_of(part)
        blocks = across(split(outputs.reshape(groups, -1, outputs.shape[1])))
        if part + 1 < len(PARTS):
            blocks, sums[part + 1] = together(blocks, sums[part + 1])
        mixed = [mixed[away] + combined(part, blocks, core ^ away) for away in range(2)]
    mine, theirs = mixed[0].astype(BF16), other(mixed[1].astype(BF16))
    sides = [jnp.where(core == 0, mine, theirs), jnp.where(core == 0, theirs, mine)]
    return jnp.concatenate(
        [side[:, p * width : (p + 1) * width] for p in range(planes) for side in sides], axis=1
    )


def solution(mesh):
    placed = (
        P(("dp", "expert"), None),
        P(("dp", "expert"), None),
        P(("dp", "expert"), None),
        P("expert", "dp", None),
        P("expert", "dp", None),
        P("expert", None, "dp"),
    )
    return jax.shard_map(
        on_device, mesh=mesh, in_specs=placed, out_specs=P(("dp", "expert"), None), check_vma=False
    )
```

time: 255 us -> 243 us (0.953); the launches traced: 254 us -> 239 us
  waiting for transfers between devices: 147 us -> 106 us
  starting transfers between devices: 58.4 us -> 85.8 us
  local copies, waits for them, and re-layouts: 12.6 us -> 8.53 us
  matrix products: 18.9 us -> 21.9 us
    ppermute x4, waiting for transfers between devices: 35.1 us -> 7.41 us  [send_on(): lax.ppermute(sending[0], 'dp', upward)]
    ppermute x4, starting transfers between devices: 20.5 us -> 46.3 us  [send_on(): lax.ppermute(sending[0], 'dp', upward)]
    ppermute x9, waiting for transfers between devices: 53.9 us -> 45.1 us  [across(): lax.ppermute(blocks[k], 'expert', [(i, i ^ k) for i in range(groups)])]
    ppermute x4, waiting for transfers between devices: 2.68 us -> 7.94 us  [send_on(): lax.ppermute(sending[1], 'dp', downward)]
    ppermute x7, waiting for transfers between devices: 9.47 us -> 4.9 us  [other(): return lax.ppermute(array, 'dp', swap)]
    ppermute x3, starting transfers between devices: 2.89 us -> 7.23 us  [pass_on(): lax.ppermute(below, 'dp', upward)]
    all_to_all x1, waiting for transfers between devices: 17.5 us -> 13.2 us  [on_device(): lax.all_to_all(sent, 'dp', split_axis=1, concat_axis=0, tiled=True)]
    ppermute x2, starting transfers between devices: 8.9 us -> 5.96 us  [send_on(): both = lax.ppermute(sending[0], 'dp', upward + downward)]
  transfers between devices with their start and end apart: 33 -> 33, of which waited for: 21 -> 18; matrix products, arithmetic and copies ran while one was open for 13% -> 15% of each run, Pallas kernels for 0% -> 0%
where the time goes in v3:
time: 243 us; the launch traced here: 239 us
  waiting for transfers between devices  106 us (44%)
  starting transfers between devices  85.8 us (35%)
  matrix products  21.9 us (9%)
  other arithmetic  15.9 us (7%)
  local copies, waits for them, and re-layouts  8.53 us (4%)
    ppermute x4, starting transfers between devices, send_on(): lax.ppermute(sending[0], 'dp', upward)  46.3 us
    ppermute x9, waiting for transfers between devices, across(): lax.ppermute(blocks[k], 'expert', [(i, i ^ k) for i in range(groups)])  45.1 us
    ppermute x2, waiting for transfers between devices, send_on(): both = lax.ppermute(sending[0], 'dp', upward + downward)  17.8 us
    all_to_all x1, waiting for transfers between devices, on_device(): lax.all_to_all(sent, 'dp', split_axis=1, concat_axis=0, tiled=True)  13.2 us
    dot_general x10, matrix products, product(): jnp.dot(take(rows[part], target % planes), in_weight, preferred_element_t...  12.8 us
    ppermute x9, starting transfers between devices, across(): lax.ppermute(blocks[k], 'expert', [(i, i ^ k) for i in range(groups)])  10.7 us
    ppermute x3, waiting for transfers between devices, pass_on(): lax.ppermute(above, 'dp', downward)  9.77 us
    ppermute x4, waiting for transfers between devices, send_on(): lax.ppermute(sending[1], 'dp', downward)  7.94 us
  transfers between devices with their start and end apart: 33, of which 18 were waited for; matrix products, arithmetic and copies ran while one was open for 15% of the time, Pallas kernels for 0%

profile of v3, /device:TPU:0, one launch (start us, length us, event | category | flops | bytes accessed | tf_op | source)
XLA Modules:
  0.0 239.1 jit_solution(14509823916487826752)
XLA Ops:
  2.1 1.6 copy.19
  5.4 6.3 %all-to-all-start = ((bf16[136,8,512]{2,0,1:T(8,128)(2,1)}), bf16[136,8,512]{2,0,1:T(8,128)(2,1)S(1)}, u32[]{:S(2)}, u32[]{:S(2)}) async-start(bf16[136,8,512]{2,0,1:T(8,128)(2,1)} %pad_maximum_fusion.6), calls=%async_computation | async-start | bytes 2228224 | tf_op jit(solution)/shard_map/all_to_all | solution.py:51
  11.8 2.0 dynamic-slice_bitcast_fusion.6
  16.9 5.7 %collective-permute-start.5 = (bf16[1536,512]{1,0:T(8,128)(2,1)}, bf16[1536,512]{1,0:T(8,128)(2,1)}, u32[]{:S(2)}, u32[]{:S(2)}) collective-permute-start(bf16[1536,512]{1,0:T(8,128)(2,1)} %bitcast.21), channel_id=1, source_target_pairs={{0,8},{4,12},{8,16},{12,20},{16,24},{20,28},{1,9},{5,13},{9,17},{1... | collective-permute-start | bytes 4718600 | tf_op jit(solution)/shard_map/ppermute | solution.py:74
  23.8 3.3 %pad_maximum_fusion.2 = bf16[1024,1536]{1,0:T(8,128)(2,1)} fusion(bf16[512,1536]{1,0:T(8,128)(2,1)} %collective-permute-done, bf16[512,768]{1,0:T(8,128)(2,1)S(1)} %get-tuple-element.75, bf16[512,768]{1,0:T(8,128)(2,1)S(1)} %get-tuple-element.134), kind=kLoop, calls=%fused_computation.12 | loop fusion | flops 9437184 | bytes 6291456 | tf_op jit(solution)/shard_map/concatenate | solution.py:57
  27.1 13.2 %all-to-all-done = bf16[136,8,512]{2,0,1:T(8,128)(2,1)S(1)} async-done(((bf16[136,8,512]{2,0,1:T(8,128)(2,1)}), bf16[136,8,512]{2,0,1:T(8,128)(2,1)S(1)}, u32[]{:S(2)}, u32[]{:S(2)}) %all-to-all-start) | async-done | bytes 1114144 | tf_op jit(solution)/shard_map/all_to_all | solution.py:51
  42.3 2.4 %collective-permute-start.4 = (bf16[8,80,512]{2,1,0:T(8,128)(2,1)}, bf16[8,80,512]{2,1,0:T(8,128)(2,1)S(1)}, u32[]{:S(2)}, u32[]{:S(2)}) collective-permute-start(bf16[8,80,512]{2,1,0:T(8,128)(2,1)} %convolution_convert_fusion.2), channel_id=1, source_target_pairs={{0,3},{1,2},{2,1},{3,0},{4,7},{5,6},{6,5},{7,4},{8,11},{9,10},{10,... | collective-permute-start | bytes 1966088 | tf_op jit(solution)/shard_map/ppermute | solution.py:68
  46.2 15.0 %collective-permute-done.4 = bf16[8,80,512]{2,1,0:T(8,128)(2,1)S(1)} collective-permute-done((bf16[8,80,512]{2,1,0:T(8,128)(2,1)}, bf16[8,80,512]{2,1,0:T(8,128)(2,1)S(1)}, u32[]{:S(2)}, u32[]{:S(2)}) %collective-permute-start.4) | collective-permute-done | bytes 655392 | tf_op jit(solution)/shard_map/ppermute | solution.py:68
  61.2 12.2 %collective-permute-done.3 = bf16[8,80,512]{2,1,0:T(8,128)(2,1)} collective-permute-done((bf16[8,80,512]{2,1,0:T(8,128)(2,1)S(1)}, bf16[8,80,512]{2,1,0:T(8,128)(2,1)}, u32[]{:S(2)}, u32[]{:S(2)}) %collective-permute-start.3) | collective-permute-done | bytes 655392 | tf_op jit(solution)/shard_map/ppermute | solution.py:68
  73.5 1.4 pad_maximum_fusion.4
  76.3 2.2 collective-permute-done.7
  79.6 1.4 collective-permute-start.16
  84.3 4.6 %collective-permute-start.9 = (bf16[320,1536]{1,0:T(8,128)(2,1)S(1)}, bf16[320,1536]{1,0:T(8,128)(2,1)S(1)}, u32[]{:S(2)}, u32[]{:S(2)}) collective-permute-start(bf16[320,1536]{1,0:T(8,128)(2,1)S(1)} %convolution_convert_fusion.1), channel_id=1, source_target_pairs={{0,8},{4,12},{24,16},{28,20},{1,9},{5,13},{25,17},{29,21},{2,10},{... | collective-permute-start | bytes 2949128 | tf_op jit(solution)/shard_map/ppermute | solution.py:115
  88.9 14.1 %collective-permute-done.16 = bf16[320,1536]{1,0:T(8,128)(2,1)S(1)} collective-permute-done((bf16[320,1536]{1,0:T(8,128)(2,1)S(1)}, bf16[320,1536]{1,0:T(8,128)(2,1)S(1)}, u32[]{:S(2)}, u32[]{:S(2)}) %collective-permute-start.16) | collective-permute-done | bytes 983072 | tf_op jit(solution)/shard_map/ppermute | solution.py:115
  105.5 5.0 %collective-permute-start.17 = (bf16[320,1536]{1,0:T(8,128)(2,1)S(1)}, bf16[320,1536]{1,0:T(8,128)(2,1)S(1)}, u32[]{:S(2)}, u32[]{:S(2)}) collective-permute-start(bf16[320,1536]{1,0:T(8,128)(2,1)S(1)} %fusion.14), channel_id=1, source_target_pairs={{0,8},{4,12},{8,16},{12,20},{1,9},{5,13},{9,17},{13,21},{2,10},{6,... | collective-permute-start | bytes 2949128 | tf_op jit(solution)/shard_map/ppermute | solution.py:117
  110.6 9.8 %collective-permute-done.11 = bf16[1536,512]{1,0:T(8,128)(2,1)S(1)} collective-permute-done((bf16[1536,512]{1,0:T(8,128)(2,1)}, bf16[1536,512]{1,0:T(8,128)(2,1)S(1)}, u32[]{:S(2)}, u32[]{:S(2)}) %collective-permute-start.11) | collective-permute-done | bytes 1572896 | tf_op jit(solution)/shard_map/ppermute | solution.py:74
  120.3 3.7 %collective-permute-done.9 = bf16[320,1536]{1,0:T(8,128)(2,1)S(1)} collective-permute-done((bf16[320,1536]{1,0:T(8,128)(2,1)S(1)}, bf16[320,1536]{1,0:T(8,128)(2,1)S(1)}, u32[]{:S(2)}, u32[]{:S(2)}) %collective-permute-start.9) | collective-permute-done | bytes 983072 | tf_op jit(solution)/shard_map/ppermute | solution.py:115
  128.1 17.5 %collective-permute-start.12 = (bf16[320,1536]{1,0:T(8,128)(2,1)S(1)}, bf16[320,1536]{1,0:T(8,128)(2,1)S(1)}, u32[]{:S(2)}, u32[]{:S(2)}) collective-permute-start(bf16[320,1536]{1,0:T(8,128)(2,1)S(1)} %add_convert_fusion.2), channel_id=1, source_target_pairs={{0,8},{4,12},{8,16},{12,20},{1,9},{5,13},{9,17},{13,21},{2,10},{6,... | collective-permute-start | bytes 2949128 | tf_op jit(solution)/shard_map/ppermute | solution.py:117
  148.2 2.1 fusion.13
  150.4 16.4 %collective-permute-start.19 = (bf16[320,1536]{1,0:T(8,128)(2,1)}, bf16[320,1536]{1,0:T(8,128)(2,1)S(1)}, u32[]{:S(2)}, u32[]{:S(2)}) collective-permute-start(bf16[320,1536]{1,0:T(8,128)(2,1)} %fusion.13), channel_id=1, source_target_pairs={{0,8},{4,12},{8,16},{12,20},{16,24},{20,28},{1,9},{5,13},{9,17},{1... | collective-permute-start | bytes 2949128 | tf_op jit(solution)/shard_map/ppermute | solution.py:117
  170.5 7.4 %collective-permute-start.25 = (bf16[320,1536]{1,0:T(8,128)(2,1)S(1)}, bf16[320,1536]{1,0:T(8,128)(2,1)S(1)}, u32[]{:S(2)}, u32[]{:S(2)}) collective-permute-start(bf16[320,1536]{1,0:T(8,128)(2,1)S(1)} %add_convert_fusion.1), channel_id=1, source_target_pairs={{0,8},{4,12},{8,16},{12,20},{16,24},{20,28},{1,9},{5,13},{9,17},{1... | collective-permute-start | bytes 2949128 | tf_op jit(solution)/shard_map/ppermute | solution.py:117
  177.9 1.6 select_bitcast_fusion
  179.8 2.6 %pad_maximum_fusion = bf16[4,1536,512]{2,1,0:T(8,128)(2,1)S(1)} fusion(bf16[1,1536,512]{2,1,0:T(8,128)(2,1)S(1)} %select_bitcast_fusion, bf16[1,1536,512]{2,1,0:T(8,128)(2,1)S(1)} %select_bitcast_fusion.1, bf16[1,1536,512]{2,1,0:T(8,128)(2,1)S(1)} %select_bitcast_fusion.2, bf16[1,1536,512]{2,1,0:T(8,128)(2,1)} %param.11), kind=kLoop, calls=%fused_computation | loop fusion | flops 9437184 | bytes 12582912 | tf_op jit(solution)/shard_map/stack | solution.py:133
  182.8 2.3 collective-permute-done.20
  185.1 4.0 %collective-permute-done.19 = bf16[320,1536]{1,0:T(8,128)(2,1)S(1)} collective-permute-done((bf16[320,1536]{1,0:T(8,128)(2,1)}, bf16[320,1536]{1,0:T(8,128)(2,1)S(1)}, u32[]{:S(2)}, u32[]{:S(2)}) %collective-permute-start.19) | collective-permute-done | bytes 983072 | tf_op jit(solution)/shard_map/ppermute | solution.py:117
  194.0 2.0 collective-permute-start.24
  198.7 5.7 %collective-permute-done.26 = bf16[320,1536]{1,0:T(8,128)(2,1)S(1)} collective-permute-done((bf16[320,1536]{1,0:T(8,128)(2,1)S(1)}, bf16[320,1536]{1,0:T(8,128)(2,1)S(1)}, u32[]{:S(2)}, u32[]{:S(2)}) %collective-permute-start.26) | collective-permute-done | bytes 983072 | tf_op jit(solution)/shard_map/ppermute | solution.py:117
  204.4 3.4 %collective-permute-done.25 = bf16[320,1536]{1,0:T(8,128)(2,1)S(1)} collective-permute-done((bf16[320,1536]{1,0:T(8,128)(2,1)S(1)}, bf16[320,1536]{1,0:T(8,128)(2,1)S(1)}, u32[]{:S(2)}, u32[]{:S(2)}) %collective-permute-start.25) | collective-permute-done | bytes 983072 | tf_op jit(solution)/shard_map/ppermute | solution.py:117
  207.8 4.2 %collective-permute-done.23 = bf16[80,2048]{1,0:T(8,128)(2,1)S(1)} collective-permute-done((bf16[80,2048]{1,0:T(8,128)(2,1)S(1)}, bf16[80,2048]{1,0:T(8,128)(2,1)S(1)}, u32[]{:S(2)}, u32[]{:S(2)}) %collective-permute-start.23) | collective-permute-done | bytes 327712 | tf_op jit(solution)/shard_map/ppermute | solution.py:68
  216.3 1.8 collective-permute-start.30
  220.4 7.4 %collective-permute-done.30 = bf16[80,2048]{1,0:T(8,128)(2,1)S(1)} collective-permute-done((bf16[80,2048]{1,0:T(8,128)(2,1)S(1)}, bf16[80,2048]{1,0:T(8,128)(2,1)S(1)}, u32[]{:S(2)}, u32[]{:S(2)}) %collective-permute-start.30) | collective-permute-done | bytes 327712 | tf_op jit(solution)/shard_map/ppermute | solution.py:68
  227.9 6.1 %collective-permute-done.29 = bf16[80,2048]{1,0:T(8,128)(2,1)S(1)} collective-permute-done((bf16[80,2048]{1,0:T(8,128)(2,1)S(1)}, bf16[80,2048]{1,0:T(8,128)(2,1)S(1)}, u32[]{:S(2)}, u32[]{:S(2)}) %collective-permute-start.29) | collective-permute-done | bytes 327712 | tf_op jit(solution)/shard_map/ppermute | solution.py:68
  (137 shorter events, 49.7 us)
Async XLA Ops:
  5.4 34.8 %all-to-all-start = ((bf16[136,8,512]{2,0,1:T(8,128)(2,1)}), bf16[136,8,512]{2,0,1:T(8,128)(2,1)S(1)}, u32[]{:S(2)}, u32[]{:S(2)}) async-start(bf16[136,8,512]{2,0,1:T(8,128)(2,1)} %pad_maximum_fusion.6), calls=%async_computation | async-start | bytes 2228224 | tf_op jit(solution)/shard_map/all_to_all | solution.py:51
  15.1 8.7 %collective-permute-start = (bf16[512,1536]{1,0:T(8,128)(2,1)}, bf16[512,1536]{1,0:T(8,128)(2,1)}, u32[]{:S(2)}, u32[]{:S(2)}) collective-permute-start(bf16[512,1536]{1,0:T(8,128)(2,1)} %pad_maximum_fusion.5), channel_id=1, source_target_pairs={{0,4},{4,0},{8,12},{12,8},{16,20},{20,16},{24,28},{28,24},{1,5},{5... | collective-permute-start | bytes 4718600 | tf_op jit(solution)/shard_map/ppermute | solution.py:40
  15.6 59.3 %collective-permute-start.6 = (bf16[1536,512]{1,0:T(8,128)(2,1)}, bf16[1536,512]{1,0:T(8,128)(2,1)}, u32[]{:S(2)}, u32[]{:S(2)}) collective-permute-start(bf16[1536,512]{1,0:T(8,128)(2,1)} %bitcast.21), channel_id=1, source_target_pairs={{8,0},{12,4},{16,8},{20,12},{24,16},{28,20},{9,1},{13,5},{17,9},{2... | collective-permute-start | bytes 4718600 | tf_op jit(solution)/shard_map/ppermute | solution.py:74
  16.9 58.0 %collective-permute-start.5 = (bf16[1536,512]{1,0:T(8,128)(2,1)}, bf16[1536,512]{1,0:T(8,128)(2,1)}, u32[]{:S(2)}, u32[]{:S(2)}) collective-permute-start(bf16[1536,512]{1,0:T(8,128)(2,1)} %bitcast.21), channel_id=1, source_target_pairs={{0,8},{4,12},{8,16},{12,20},{16,24},{20,28},{1,9},{5,13},{9,17},{1... | collective-permute-start | bytes 4718600 | tf_op jit(solution)/shard_map/ppermute | solution.py:74
  42.3 18.8 %collective-permute-start.4 = (bf16[8,80,512]{2,1,0:T(8,128)(2,1)}, bf16[8,80,512]{2,1,0:T(8,128)(2,1)S(1)}, u32[]{:S(2)}, u32[]{:S(2)}) collective-permute-start(bf16[8,80,512]{2,1,0:T(8,128)(2,1)} %convolution_convert_fusion.2), channel_id=1, source_target_pairs={{0,3},{1,2},{2,1},{3,0},{4,7},{5,6},{6,5},{7,4},{8,11},{9,10},{10,... | collective-permute-start | bytes 1966088 | tf_op jit(solution)/shard_map/ppermute | solution.py:68
  44.8 28.6 %collective-permute-start.3 = (bf16[8,80,512]{2,1,0:T(8,128)(2,1)S(1)}, bf16[8,80,512]{2,1,0:T(8,128)(2,1)}, u32[]{:S(2)}, u32[]{:S(2)}) collective-permute-start(bf16[8,80,512]{2,1,0:T(8,128)(2,1)S(1)} %convolution_convert_fusion.3), channel_id=1, source_target_pairs={{0,2},{1,3},{2,0},{3,1},{4,6},{5,7},{6,4},{7,5},{8,10},{9,11},{10,... | collective-permute-start | bytes 1966088 | tf_op jit(solution)/shard_map/ppermute | solution.py:68
  45.3 28.2 %collective-permute-start.2 = (bf16[8,80,512]{2,1,0:T(8,128)(2,1)S(1)}, bf16[8,80,512]{2,1,0:T(8,128)(2,1)}, u32[]{:S(2)}, u32[]{:S(2)}) collective-permute-start(bf16[8,80,512]{2,1,0:T(8,128)(2,1)S(1)} %convolution_convert_fusion.4), channel_id=1, source_target_pairs={{0,1},{1,0},{2,3},{3,2},{4,5},{5,4},{6,7},{7,6},{8,9},{9,8},{10,11... | collective-permute-start | bytes 1966088 | tf_op jit(solution)/shard_map/ppermute | solution.py:68
  75.3 3.1 %collective-permute-start.7 = (bf16[4,320,512]{2,1,0:T(8,128)(2,1)S(1)}, bf16[4,320,512]{2,1,0:T(8,128)(2,1)S(1)}, u32[]{:S(2)}, u32[]{:S(2)}) collective-permute-start(bf16[4,320,512]{2,1,0:T(8,128)(2,1)S(1)} %bitcast.137), channel_id=1, source_target_pairs={{0,4},{4,0},{8,12},{12,8},{16,20},{20,16},{24,28},{28,24},{1,5},{5... | collective-permute-start | bytes 3932168 | tf_op jit(solution)/shard_map/ppermute | solution.py:40
  75.7 7.4 %collective-permute-start.8 = (bf16[4,320,512]{2,1,0:T(8,128)(2,1)S(1)}, bf16[4,320,512]{2,1,0:T(8,128)(2,1)S(1)}, u32[]{:S(2)}, u32[]{:S(2)}) collective-permute-start(bf16[4,320,512]{2,1,0:T(8,128)(2,1)S(1)} %bitcast.134), channel_id=1, source_target_pairs={{0,4},{4,0},{8,12},{12,8},{16,20},{20,16},{24,28},{28,24},{1,5},{5... | collective-permute-start | bytes 3932168 | tf_op jit(solution)/shard_map/ppermute | solution.py:40
  79.6 23.4 %collective-permute-start.16 = (bf16[320,1536]{1,0:T(8,128)(2,1)S(1)}, bf16[320,1536]{1,0:T(8,128)(2,1)S(1)}, u32[]{:S(2)}, u32[]{:S(2)}) collective-permute-start(bf16[320,1536]{1,0:T(8,128)(2,1)S(1)} %convolution_convert_fusion), channel_id=1, source_target_pairs={{0,8},{4,12},{24,16},{28,20},{1,9},{5,13},{25,17},{29,21},{2,10},{... | collective-permute-start | bytes 2949128 | tf_op jit(solution)/shard_map/ppermute | solution.py:115
  81.0 29.5 %collective-permute-start.10 = (bf16[1536,512]{1,0:T(8,128)(2,1)}, bf16[1536,512]{1,0:T(8,128)(2,1)S(1)}, u32[]{:S(2)}, u32[]{:S(2)}) collective-permute-start(bf16[1536,512]{1,0:T(8,128)(2,1)} %collective-permute-done.5), channel_id=1, source_target_pairs={{8,16},{12,20},{16,24},{20,28},{9,17},{13,21},{17,25},{21,29},{10,... | collective-permute-start | bytes 4718600 | tf_op jit(solution)/shard_map/ppermute | solution.py:74
  81.8 38.5 %collective-permute-start.11 = (bf16[1536,512]{1,0:T(8,128)(2,1)}, bf16[1536,512]{1,0:T(8,128)(2,1)S(1)}, u32[]{:S(2)}, u32[]{:S(2)}) collective-permute-start(bf16[1536,512]{1,0:T(8,128)(2,1)} %collective-permute-done.6), channel_id=1, source_target_pairs={{8,0},{12,4},{16,8},{20,12},{9,1},{13,5},{17,9},{21,13},{10,2},{14... | collective-permute-start | bytes 4718600 | tf_op jit(solution)/shard_map/ppermute | solution.py:74
  84.3 39.8 %collective-permute-start.9 = (bf16[320,1536]{1,0:T(8,128)(2,1)S(1)}, bf16[320,1536]{1,0:T(8,128)(2,1)S(1)}, u32[]{:S(2)}, u32[]{:S(2)}) collective-permute-start(bf16[320,1536]{1,0:T(8,128)(2,1)S(1)} %convolution_convert_fusion.1), channel_id=1, source_target_pairs={{0,8},{4,12},{24,16},{28,20},{1,9},{5,13},{25,17},{29,21},{2,10},{... | collective-permute-start | bytes 2949128 | tf_op jit(solution)/shard_map/ppermute | solution.py:115
  104.2 23.9 %collective-permute-start.18 = (bf16[320,1536]{1,0:T(8,128)(2,1)S(1)}, bf16[320,1536]{1,0:T(8,128)(2,1)S(1)}, u32[]{:S(2)}, u32[]{:S(2)}) collective-permute-start(bf16[320,1536]{1,0:T(8,128)(2,1)S(1)} %fusion.14), channel_id=1, source_target_pairs={{24,16},{28,20},{16,8},{20,12},{25,17},{29,21},{17,9},{21,13},{26,... | collective-permute-start | bytes 2949128 | tf_op jit(solution)/shard_map/ppermute | solution.py:117
  105.5 40.2 %collective-permute-start.17 = (bf16[320,1536]{1,0:T(8,128)(2,1)S(1)}, bf16[320,1536]{1,0:T(8,128)(2,1)S(1)}, u32[]{:S(2)}, u32[]{:S(2)}) collective-permute-start(bf16[320,1536]{1,0:T(8,128)(2,1)S(1)} %fusion.14), channel_id=1, source_target_pairs={{0,8},{4,12},{8,16},{12,20},{1,9},{5,13},{9,17},{13,21},{2,10},{6,... | collective-permute-start | bytes 2949128 | tf_op jit(solution)/shard_map/ppermute | solution.py:117
  124.1 42.8 %collective-permute-start.14 = (bf16[1536,512]{1,0:T(8,128)(2,1)S(1)}, bf16[1536,512]{1,0:T(8,128)(2,1)S(1)}, u32[]{:S(2)}, u32[]{:S(2)}) collective-permute-start(bf16[1536,512]{1,0:T(8,128)(2,1)S(1)} %collective-permute-done.10), channel_id=1, source_target_pairs={{16,24},{20,28},{17,25},{21,29},{18,26},{22,30},{19,27},{23,31}} | collective-permute-start | bytes 4718600 | tf_op jit(solution)/shard_map/ppermute | solution.py:74
  124.8 42.0 %collective-permute-start.15 = (bf16[1536,512]{1,0:T(8,128)(2,1)S(1)}, bf16[1536,512]{1,0:T(8,128)(2,1)S(1)}, u32[]{:S(2)}, u32[]{:S(2)}) collective-permute-start(bf16[1536,512]{1,0:T(8,128)(2,1)S(1)} %collective-permute-done.11), channel_id=1, source_target_pairs={{8,0},{12,4},{9,1},{13,5},{10,2},{14,6},{11,3},{15,7}} | collective-permute-start | bytes 4718600 | tf_op jit(solution)/shard_map/ppermute | solution.py:74
  127.3 23.1 %collective-permute-start.13 = (bf16[320,1536]{1,0:T(8,128)(2,1)S(1)}, bf16[320,1536]{1,0:T(8,128)(2,1)S(1)}, u32[]{:S(2)}, u32[]{:S(2)}) collective-permute-start(bf16[320,1536]{1,0:T(8,128)(2,1)S(1)} %add_convert_fusion.2), channel_id=1, source_target_pairs={{24,16},{28,20},{16,8},{20,12},{25,17},{29,21},{17,9},{21,13},{26,... | collective-permute-start | bytes 2949128 | tf_op jit(solution)/shard_map/ppermute | solution.py:117
  128.1 38.8 %collective-permute-start.12 = (bf16[320,1536]{1,0:T(8,128)(2,1)S(1)}, bf16[320,1536]{1,0:T(8,128)(2,1)S(1)}, u32[]{:S(2)}, u32[]{:S(2)}) collective-permute-start(bf16[320,1536]{1,0:T(8,128)(2,1)S(1)} %add_convert_fusion.2), channel_id=1, source_target_pairs={{0,8},{4,12},{8,16},{12,20},{1,9},{5,13},{9,17},{13,21},{2,10},{6,... | collective-permute-start | bytes 2949128 | tf_op jit(solution)/shard_map/ppermute | solution.py:117
  146.9 38.2 %collective-permute-start.20 = (bf16[320,1536]{1,0:T(8,128)(2,1)S(1)}, bf16[320,1536]{1,0:T(8,128)(2,1)S(1)}, u32[]{:S(2)}, u32[]{:S(2)}) collective-permute-start(bf16[320,1536]{1,0:T(8,128)(2,1)S(1)} %fusion.15), channel_id=1, source_target_pairs={{24,16},{28,20},{16,8},{20,12},{8,0},{12,4},{25,17},{29,21},{17,9}... | collective-permute-start | bytes 2949128 | tf_op jit(solution)/shard_map/ppermute | solution.py:117
  150.4 38.7 %collective-permute-start.19 = (bf16[320,1536]{1,0:T(8,128)(2,1)}, bf16[320,1536]{1,0:T(8,128)(2,1)S(1)}, u32[]{:S(2)}, u32[]{:S(2)}) collective-permute-start(bf16[320,1536]{1,0:T(8,128)(2,1)} %fusion.13), channel_id=1, source_target_pairs={{0,8},{4,12},{8,16},{12,20},{16,24},{20,28},{1,9},{5,13},{9,17},{1... | collective-permute-start | bytes 2949128 | tf_op jit(solution)/shard_map/ppermute | solution.py:117
  169.2 35.2 %collective-permute-start.26 = (bf16[320,1536]{1,0:T(8,128)(2,1)S(1)}, bf16[320,1536]{1,0:T(8,128)(2,1)S(1)}, u32[]{:S(2)}, u32[]{:S(2)}) collective-permute-start(bf16[320,1536]{1,0:T(8,128)(2,1)S(1)} %add_convert_fusion), channel_id=1, source_target_pairs={{24,16},{28,20},{16,8},{20,12},{8,0},{12,4},{25,17},{29,21},{17,9}... | collective-permute-start | bytes 2949128 | tf_op jit(solution)/shard_map/ppermute | solution.py:117
  170.5 37.3 %collective-permute-start.25 = (bf16[320,1536]{1,0:T(8,128)(2,1)S(1)}, bf16[320,1536]{1,0:T(8,128)(2,1)S(1)}, u32[]{:S(2)}, u32[]{:S(2)}) collective-permute-start(bf16[320,1536]{1,0:T(8,128)(2,1)S(1)} %add_convert_fusion.1), channel_id=1, source_target_pairs={{0,8},{4,12},{8,16},{12,20},{16,24},{20,28},{1,9},{5,13},{9,17},{1... | collective-permute-start | bytes 2949128 | tf_op jit(solution)/shard_map/ppermute | solution.py:117
  190.6 2.1 collective-permute-start.21
  194.0 13.9 %collective-permute-start.24 = (bf16[80,2048]{1,0:T(8,128)(2,1)S(1)}, bf16[80,2048]{1,0:T(8,128)(2,1)S(1)}, u32[]{:S(2)}, u32[]{:S(2)}) collective-permute-start(bf16[80,2048]{1,0:T(8,128)(2,1)S(1)} %get-tuple-element.81), channel_id=1, source_target_pairs={{0,3},{1,2},{2,1},{3,0},{4,7},{5,6},{6,5},{7,4},{8,11},{9,10},{10,... | collective-permute-start | bytes 983048 | tf_op jit(solution)/shard_map/ppermute | solution.py:68
  195.9 16.1 %collective-permute-start.23 = (bf16[80,2048]{1,0:T(8,128)(2,1)S(1)}, bf16[80,2048]{1,0:T(8,128)(2,1)S(1)}, u32[]{:S(2)}, u32[]{:S(2)}) collective-permute-start(bf16[80,2048]{1,0:T(8,128)(2,1)S(1)} %get-tuple-element.82), channel_id=1, source_target_pairs={{0,2},{1,3},{2,0},{3,1},{4,6},{5,7},{6,4},{7,5},{8,10},{9,11},{10,... | collective-permute-start | bytes 983048 | tf_op jit(solution)/shard_map/ppermute | solution.py:68
  197.0 15.1 %collective-permute-start.22 = (bf16[80,2048]{1,0:T(8,128)(2,1)S(1)}, bf16[80,2048]{1,0:T(8,128)(2,1)S(1)}, u32[]{:S(2)}, u32[]{:S(2)}) collective-permute-start(bf16[80,2048]{1,0:T(8,128)(2,1)S(1)} %get-tuple-element.83), channel_id=1, source_target_pairs={{0,1},{1,0},{2,3},{3,2},{4,5},{5,4},{6,7},{7,6},{8,9},{9,8},{10,11... | collective-permute-start | bytes 983048 | tf_op jit(solution)/shard_map/ppermute | solution.py:68
  212.9 1.9 collective-permute-start.27
  216.3 11.6 %collective-permute-start.30 = (bf16[80,2048]{1,0:T(8,128)(2,1)S(1)}, bf16[80,2048]{1,0:T(8,128)(2,1)S(1)}, u32[]{:S(2)}, u32[]{:S(2)}) collective-permute-start(bf16[80,2048]{1,0:T(8,128)(2,1)S(1)} %get-tuple-element.78), channel_id=1, source_target_pairs={{0,3},{1,2},{2,1},{3,0},{4,7},{5,6},{6,5},{7,4},{8,11},{9,10},{10,... | collective-permute-start | bytes 983048 | tf_op jit(solution)/shard_map/ppermute | solution.py:68
  218.5 15.5 %collective-permute-start.29 = (bf16[80,2048]{1,0:T(8,128)(2,1)S(1)}, bf16[80,2048]{1,0:T(8,128)(2,1)S(1)}, u32[]{:S(2)}, u32[]{:S(2)}) collective-permute-start(bf16[80,2048]{1,0:T(8,128)(2,1)S(1)} %get-tuple-element.79), channel_id=1, source_target_pairs={{0,2},{1,3},{2,0},{3,1},{4,6},{5,7},{6,4},{7,5},{8,10},{9,11},{10,... | collective-permute-start | bytes 983048 | tf_op jit(solution)/shard_map/ppermute | solution.py:68
  219.8 14.2 %collective-permute-start.28 = (bf16[80,2048]{1,0:T(8,128)(2,1)S(1)}, bf16[80,2048]{1,0:T(8,128)(2,1)S(1)}, u32[]{:S(2)}, u32[]{:S(2)}) collective-permute-start(bf16[80,2048]{1,0:T(8,128)(2,1)S(1)} %get-tuple-element.80), channel_id=1, source_target_pairs={{0,1},{1,0},{2,3},{3,2},{4,5},{5,4},{6,7},{7,6},{8,9},{9,8},{10,11... | collective-permute-start | bytes 983048 | tf_op jit(solution)/shard_map/ppermute | solution.py:68
  234.8 2.0 collective-permute-start.31
  (4 other events, 14.2 us)

commit v4 on v3

--- a/solution.py
+++ b/solution.py
@@ -161,7 +161,7 @@
         outputs = outputs_of(part)
         blocks = across(split(outputs.reshape(groups, -1, outputs.shape[1])))
         if part + 1 < len(PARTS):
-            blocks, sums[part + 1] = together(blocks, sums[part + 1])
+            blocks[-1], sums[part + 1] = together(blocks[-1], sums[part + 1])
         mixed = [mixed[away] + combined(part, blocks, core ^ away) for away in range(2)]
     mine, theirs = mixed[0].astype(BF16), other(mixed[1].astype(BF16))
     sides = [jnp.where(core == 0, mine, theirs), jnp.where(core == 0, theirs, mine)]

time: 243 us -> 241 us (level)
  transfers between devices with their start and end apart: 33 -> 33, of which waited for: 18 -> 17; matrix products, arithmetic and copies ran while one was open for 15% -> 15% of each run, Pallas kernels for 0% -> 0%
where the time goes in v4:
time: 241 us; the launch traced here: 238 us
  waiting for transfers between devices  105 us (44%)
  starting transfers between devices  85.9 us (36%)
  matrix products  21.9 us (9%)
  other arithmetic  15.9 us (7%)
  local copies, waits for them, and re-layouts  8.54 us (4%)
    ppermute x4, starting transfers between devices, send_on(): lax.ppermute(sending[0], 'dp', upward)  46.3 us
    ppermute x9, waiting for transfers between devices, across(): lax.ppermute(blocks[k], 'expert', [(i, i ^ k) for i in range(groups)])  44.2 us
    ppermute x2, waiting for transfers between devices, send_on(): both = lax.ppermute(sending[0], 'dp', upward + downward)  17.8 us
    all_to_all x1, waiting for transfers between devices, on_device(): lax.all_to_all(sent, 'dp', split_axis=1, concat_axis=0, tiled=True)  13.2 us
    dot_general x10, matrix products, product(): jnp.dot(take(rows[part], target % planes), in_weight, preferred_element_t...  12.8 us
    ppermute x9, starting transfers between devices, across(): lax.ppermute(blocks[k], 'expert', [(i, i ^ k) for i in range(groups)])  10.8 us
    ppermute x3, waiting for transfers between devices, pass_on(): lax.ppermute(above, 'dp', downward)  9.77 us
    ppermute x4, waiting for transfers between devices, send_on(): lax.ppermute(sending[1], 'dp', downward)  7.84 us
  transfers between devices with their start and end apart: 33, of which 17 were waited for; matrix products, arithmetic and copies ran while one was open for 15% of the time, Pallas kernels for 0%

profile of v4, /device:TPU:0, one launch (start us, length us, event | category | flops | bytes accessed | tf_op | source)
XLA Modules:
  0.0 237.5 jit_solution(5805412021372961610)
XLA Ops:
  2.1 1.6 copy.19
  5.4 6.3 %all-to-all-start = ((bf16[136,8,512]{2,0,1:T(8,128)(2,1)}), bf16[136,8,512]{2,0,1:T(8,128)(2,1)S(1)}, u32[]{:S(2)}, u32[]{:S(2)}) async-start(bf16[136,8,512]{2,0,1:T(8,128)(2,1)} %pad_maximum_fusion.6), calls=%async_computation | async-start | bytes 2228224 | tf_op jit(solution)/shard_map/all_to_all | solution.py:51
  11.8 2.0 dynamic-slice_bitcast_fusion.6
  16.9 5.7 %collective-permute-start.5 = (bf16[1536,512]{1,0:T(8,128)(2,1)}, bf16[1536,512]{1,0:T(8,128)(2,1)}, u32[]{:S(2)}, u32[]{:S(2)}) collective-permute-start(bf16[1536,512]{1,0:T(8,128)(2,1)} %bitcast.21), channel_id=1, source_target_pairs={{0,8},{4,12},{8,16},{12,20},{16,24},{20,28},{1,9},{5,13},{9,17},{1... | collective-permute-start | bytes 4718600 | tf_op jit(solution)/shard_map/ppermute | solution.py:74
  23.8 3.3 %pad_maximum_fusion.2 = bf16[1024,1536]{1,0:T(8,128)(2,1)} fusion(bf16[512,1536]{1,0:T(8,128)(2,1)} %collective-permute-done, bf16[512,768]{1,0:T(8,128)(2,1)S(1)} %get-tuple-element.69, bf16[512,768]{1,0:T(8,128)(2,1)S(1)} %get-tuple-element.128), kind=kLoop, calls=%fused_computation.12 | loop fusion | flops 9437184 | bytes 6291456 | tf_op jit(solution)/shard_map/concatenate | solution.py:57
  27.1 13.2 %all-to-all-done = bf16[136,8,512]{2,0,1:T(8,128)(2,1)S(1)} async-done(((bf16[136,8,512]{2,0,1:T(8,128)(2,1)}), bf16[136,8,512]{2,0,1:T(8,128)(2,1)S(1)}, u32[]{:S(2)}, u32[]{:S(2)}) %all-to-all-start) | async-done | bytes 1114144 | tf_op jit(solution)/shard_map/all_to_all | solution.py:51
  42.3 2.4 %collective-permute-start.4 = (bf16[8,80,512]{2,1,0:T(8,128)(2,1)}, bf16[8,80,512]{2,1,0:T(8,128)(2,1)S(1)}, u32[]{:S(2)}, u32[]{:S(2)}) collective-permute-start(bf16[8,80,512]{2,1,0:T(8,128)(2,1)} %convolution_convert_fusion.2), channel_id=1, source_target_pairs={{0,3},{1,2},{2,1},{3,0},{4,7},{5,6},{6,5},{7,4},{8,11},{9,10},{10,... | collective-permute-start | bytes 1966088 | tf_op jit(solution)/shard_map/ppermute | solution.py:68
  46.2 15.0 %collective-permute-done.4 = bf16[8,80,512]{2,1,0:T(8,128)(2,1)S(1)} collective-permute-done((bf16[8,80,512]{2,1,0:T(8,128)(2,1)}, bf16[8,80,512]{2,1,0:T(8,128)(2,1)S(1)}, u32[]{:S(2)}, u32[]{:S(2)}) %collective-permute-start.4) | collective-permute-done | bytes 655392 | tf_op jit(solution)/shard_map/ppermute | solution.py:68
  61.2 12.2 %collective-permute-done.3 = bf16[8,80,512]{2,1,0:T(8,128)(2,1)} collective-permute-done((bf16[8,80,512]{2,1,0:T(8,128)(2,1)S(1)}, bf16[8,80,512]{2,1,0:T(8,128)(2,1)}, u32[]{:S(2)}, u32[]{:S(2)}) %collective-permute-start.3) | collective-permute-done | bytes 655392 | tf_op jit(solution)/shard_map/ppermute | solution.py:68
  73.5 1.4 pad_maximum_fusion.4
  76.3 2.2 collective-permute-done.7
  79.6 1.4 collective-permute-start.16
  84.3 4.6 %collective-permute-start.9 = (bf16[320,1536]{1,0:T(8,128)(2,1)S(1)}, bf16[320,1536]{1,0:T(8,128)(2,1)S(1)}, u32[]{:S(2)}, u32[]{:S(2)}) collective-permute-start(bf16[320,1536]{1,0:T(8,128)(2,1)S(1)} %convolution_convert_fusion.1), channel_id=1, source_target_pairs={{0,8},{4,12},{24,16},{28,20},{1,9},{5,13},{25,17},{29,21},{2,10},{... | collective-permute-start | bytes 2949128 | tf_op jit(solution)/shard_map/ppermute | solution.py:115
  88.9 14.1 %collective-permute-done.16 = bf16[320,1536]{1,0:T(8,128)(2,1)S(1)} collective-permute-done((bf16[320,1536]{1,0:T(8,128)(2,1)S(1)}, bf16[320,1536]{1,0:T(8,128)(2,1)S(1)}, u32[]{:S(2)}, u32[]{:S(2)}) %collective-permute-start.16) | collective-permute-done | bytes 983072 | tf_op jit(solution)/shard_map/ppermute | solution.py:115
  105.5 5.0 %collective-permute-start.17 = (bf16[320,1536]{1,0:T(8,128)(2,1)S(1)}, bf16[320,1536]{1,0:T(8,128)(2,1)S(1)}, u32[]{:S(2)}, u32[]{:S(2)}) collective-permute-start(bf16[320,1536]{1,0:T(8,128)(2,1)S(1)} %fusion.14), channel_id=1, source_target_pairs={{0,8},{4,12},{8,16},{12,20},{1,9},{5,13},{9,17},{13,21},{2,10},{6,... | collective-permute-start | bytes 2949128 | tf_op jit(solution)/shard_map/ppermute | solution.py:117
  110.6 9.8 %collective-permute-done.11 = bf16[1536,512]{1,0:T(8,128)(2,1)S(1)} collective-permute-done((bf16[1536,512]{1,0:T(8,128)(2,1)}, bf16[1536,512]{1,0:T(8,128)(2,1)S(1)}, u32[]{:S(2)}, u32[]{:S(2)}) %collective-permute-start.11) | collective-permute-done | bytes 1572896 | tf_op jit(solution)/shard_map/ppermute | solution.py:74
  120.3 3.7 %collective-permute-done.9 = bf16[320,1536]{1,0:T(8,128)(2,1)S(1)} collective-permute-done((bf16[320,1536]{1,0:T(8,128)(2,1)S(1)}, bf16[320,1536]{1,0:T(8,128)(2,1)S(1)}, u32[]{:S(2)}, u32[]{:S(2)}) %collective-permute-start.9) | collective-permute-done | bytes 983072 | tf_op jit(solution)/shard_map/ppermute | solution.py:115
  128.1 17.5 %collective-permute-start.12 = (bf16[320,1536]{1,0:T(8,128)(2,1)S(1)}, bf16[320,1536]{1,0:T(8,128)(2,1)S(1)}, u32[]{:S(2)}, u32[]{:S(2)}) collective-permute-start(bf16[320,1536]{1,0:T(8,128)(2,1)S(1)} %add_convert_fusion.2), channel_id=1, source_target_pairs={{0,8},{4,12},{8,16},{12,20},{1,9},{5,13},{9,17},{13,21},{2,10},{6,... | collective-permute-start | bytes 2949128 | tf_op jit(solution)/shard_map/ppermute | solution.py:117
  148.2 2.1 fusion.13
  150.4 16.4 %collective-permute-start.19 = (bf16[320,1536]{1,0:T(8,128)(2,1)}, bf16[320,1536]{1,0:T(8,128)(2,1)S(1)}, u32[]{:S(2)}, u32[]{:S(2)}) collective-permute-start(bf16[320,1536]{1,0:T(8,128)(2,1)} %fusion.13), channel_id=1, source_target_pairs={{0,8},{4,12},{8,16},{12,20},{16,24},{20,28},{1,9},{5,13},{9,17},{1... | collective-permute-start | bytes 2949128 | tf_op jit(solution)/shard_map/ppermute | solution.py:117
  170.5 7.4 %collective-permute-start.25 = (bf16[320,1536]{1,0:T(8,128)(2,1)S(1)}, bf16[320,1536]{1,0:T(8,128)(2,1)S(1)}, u32[]{:S(2)}, u32[]{:S(2)}) collective-permute-start(bf16[320,1536]{1,0:T(8,128)(2,1)S(1)} %add_convert_fusion.1), channel_id=1, source_target_pairs={{0,8},{4,12},{8,16},{12,20},{16,24},{20,28},{1,9},{5,13},{9,17},{1... | collective-permute-start | bytes 2949128 | tf_op jit(solution)/shard_map/ppermute | solution.py:117
  177.9 1.6 select_bitcast_fusion
  179.8 2.6 %pad_maximum_fusion = bf16[4,1536,512]{2,1,0:T(8,128)(2,1)S(1)} fusion(bf16[1,1536,512]{2,1,0:T(8,128)(2,1)S(1)} %select_bitcast_fusion, bf16[1,1536,512]{2,1,0:T(8,128)(2,1)S(1)} %select_bitcast_fusion.1, bf16[1,1536,512]{2,1,0:T(8,128)(2,1)S(1)} %select_bitcast_fusion.2, bf16[1,1536,512]{2,1,0:T(8,128)(2,1)} %param.11), kind=kLoop, calls=%fused_computation | loop fusion | flops 9437184 | bytes 12582912 | tf_op jit(solution)/shard_map/stack | solution.py:133
  182.8 2.3 collective-permute-done.20
  185.1 4.0 %collective-permute-done.19 = bf16[320,1536]{1,0:T(8,128)(2,1)S(1)} collective-permute-done((bf16[320,1536]{1,0:T(8,128)(2,1)}, bf16[320,1536]{1,0:T(8,128)(2,1)S(1)}, u32[]{:S(2)}, u32[]{:S(2)}) %collective-permute-start.19) | collective-permute-done | bytes 983072 | tf_op jit(solution)/shard_map/ppermute | solution.py:117
  194.0 2.0 collective-permute-start.24
  198.8 5.6 %collective-permute-done.26 = bf16[320,1536]{1,0:T(8,128)(2,1)S(1)} collective-permute-done((bf16[320,1536]{1,0:T(8,128)(2,1)S(1)}, bf16[320,1536]{1,0:T(8,128)(2,1)S(1)}, u32[]{:S(2)}, u32[]{:S(2)}) %collective-permute-start.26) | collective-permute-done | bytes 983072 | tf_op jit(solution)/shard_map/ppermute | solution.py:117
  204.4 3.4 %collective-permute-done.25 = bf16[320,1536]{1,0:T(8,128)(2,1)S(1)} collective-permute-done((bf16[320,1536]{1,0:T(8,128)(2,1)S(1)}, bf16[320,1536]{1,0:T(8,128)(2,1)S(1)}, u32[]{:S(2)}, u32[]{:S(2)}) %collective-permute-start.25) | collective-permute-done | bytes 983072 | tf_op jit(solution)/shard_map/ppermute | solution.py:117
  208.7 3.4 %collective-permute-done.23 = bf16[80,2048]{1,0:T(8,128)(2,1)S(1)} collective-permute-done((bf16[80,2048]{1,0:T(8,128)(2,1)S(1)}, bf16[80,2048]{1,0:T(8,128)(2,1)S(1)}, u32[]{:S(2)}, u32[]{:S(2)}) %collective-permute-start.23) | collective-permute-done | bytes 327712 | tf_op jit(solution)/shard_map/ppermute | solution.py:68
  214.8 2.0 collective-permute-start.30
  218.9 7.4 %collective-permute-done.30 = bf16[80,2048]{1,0:T(8,128)(2,1)S(1)} collective-permute-done((bf16[80,2048]{1,0:T(8,128)(2,1)S(1)}, bf16[80,2048]{1,0:T(8,128)(2,1)S(1)}, u32[]{:S(2)}, u32[]{:S(2)}) %collective-permute-start.30) | collective-permute-done | bytes 327712 | tf_op jit(solution)/shard_map/ppermute | solution.py:68
  226.4 6.0 %collective-permute-done.29 = bf16[80,2048]{1,0:T(8,128)(2,1)S(1)} collective-permute-done((bf16[80,2048]{1,0:T(8,128)(2,1)S(1)}, bf16[80,2048]{1,0:T(8,128)(2,1)S(1)}, u32[]{:S(2)}, u32[]{:S(2)}) %collective-permute-start.29) | collective-permute-done | bytes 327712 | tf_op jit(solution)/shard_map/ppermute | solution.py:68
  (137 shorter events, 49.0 us)
Async XLA Ops:
  5.4 34.8 %all-to-all-start = ((bf16[136,8,512]{2,0,1:T(8,128)(2,1)}), bf16[136,8,512]{2,0,1:T(8,128)(2,1)S(1)}, u32[]{:S(2)}, u32[]{:S(2)}) async-start(bf16[136,8,512]{2,0,1:T(8,128)(2,1)} %pad_maximum_fusion.6), calls=%async_computation | async-start | bytes 2228224 | tf_op jit(solution)/shard_map/all_to_all | solution.py:51
  15.1 8.7 %collective-permute-start = (bf16[512,1536]{1,0:T(8,128)(2,1)}, bf16[512,1536]{1,0:T(8,128)(2,1)}, u32[]{:S(2)}, u32[]{:S(2)}) collective-permute-start(bf16[512,1536]{1,0:T(8,128)(2,1)} %pad_maximum_fusion.5), channel_id=1, source_target_pairs={{0,4},{4,0},{8,12},{12,8},{16,20},{20,16},{24,28},{28,24},{1,5},{5... | collective-permute-start | bytes 4718600 | tf_op jit(solution)/shard_map/ppermute | solution.py:40
  15.6 59.3 %collective-permute-start.6 = (bf16[1536,512]{1,0:T(8,128)(2,1)}, bf16[1536,512]{1,0:T(8,128)(2,1)}, u32[]{:S(2)}, u32[]{:S(2)}) collective-permute-start(bf16[1536,512]{1,0:T(8,128)(2,1)} %bitcast.21), channel_id=1, source_target_pairs={{8,0},{12,4},{16,8},{20,12},{24,16},{28,20},{9,1},{13,5},{17,9},{2... | collective-permute-start | bytes 4718600 | tf_op jit(solution)/shard_map/ppermute | solution.py:74
  16.9 58.0 %collective-permute-start.5 = (bf16[1536,512]{1,0:T(8,128)(2,1)}, bf16[1536,512]{1,0:T(8,128)(2,1)}, u32[]{:S(2)}, u32[]{:S(2)}) collective-permute-start(bf16[1536,512]{1,0:T(8,128)(2,1)} %bitcast.21), channel_id=1, source_target_pairs={{0,8},{4,12},{8,16},{12,20},{16,24},{20,28},{1,9},{5,13},{9,17},{1... | collective-permute-start | bytes 4718600 | tf_op jit(solution)/shard_map/ppermute | solution.py:74
  42.3 18.8 %collective-permute-start.4 = (bf16[8,80,512]{2,1,0:T(8,128)(2,1)}, bf16[8,80,512]{2,1,0:T(8,128)(2,1)S(1)}, u32[]{:S(2)}, u32[]{:S(2)}) collective-permute-start(bf16[8,80,512]{2,1,0:T(8,128)(2,1)} %convolution_convert_fusion.2), channel_id=1, source_target_pairs={{0,3},{1,2},{2,1},{3,0},{4,7},{5,6},{6,5},{7,4},{8,11},{9,10},{10,... | collective-permute-start | bytes 1966088 | tf_op jit(solution)/shard_map/ppermute | solution.py:68
  44.8 28.6 %collective-permute-start.3 = (bf16[8,80,512]{2,1,0:T(8,128)(2,1)S(1)}, bf16[8,80,512]{2,1,0:T(8,128)(2,1)}, u32[]{:S(2)}, u32[]{:S(2)}) collective-permute-start(bf16[8,80,512]{2,1,0:T(8,128)(2,1)S(1)} %convolution_convert_fusion.3), channel_id=1, source_target_pairs={{0,2},{1,3},{2,0},{3,1},{4,6},{5,7},{6,4},{7,5},{8,10},{9,11},{10,... | collective-permute-start | bytes 1966088 | tf_op jit(solution)/shard_map/ppermute | solution.py:68
  45.3 28.2 %collective-permute-start.2 = (bf16[8,80,512]{2,1,0:T(8,128)(2,1)S(1)}, bf16[8,80,512]{2,1,0:T(8,128)(2,1)}, u32[]{:S(2)}, u32[]{:S(2)}) collective-permute-start(bf16[8,80,512]{2,1,0:T(8,128)(2,1)S(1)} %convolution_convert_fusion.4), channel_id=1, source_target_pairs={{0,1},{1,0},{2,3},{3,2},{4,5},{5,4},{6,7},{7,6},{8,9},{9,8},{10,11... | collective-permute-start | bytes 1966088 | tf_op jit(solution)/shard_map/ppermute | solution.py:68
  75.3 3.1 %collective-permute-start.7 = (bf16[4,320,512]{2,1,0:T(8,128)(2,1)S(1)}, bf16[4,320,512]{2,1,0:T(8,128)(2,1)S(1)}, u32[]{:S(2)}, u32[]{:S(2)}) collective-permute-start(bf16[4,320,512]{2,1,0:T(8,128)(2,1)S(1)} %bitcast.137), channel_id=1, source_target_pairs={{0,4},{4,0},{8,12},{12,8},{16,20},{20,16},{24,28},{28,24},{1,5},{5... | collective-permute-start | bytes 3932168 | tf_op jit(solution)/shard_map/ppermute | solution.py:40
  75.7 7.4 %collective-permute-start.8 = (bf16[4,320,512]{2,1,0:T(8,128)(2,1)S(1)}, bf16[4,320,512]{2,1,0:T(8,128)(2,1)S(1)}, u32[]{:S(2)}, u32[]{:S(2)}) collective-permute-start(bf16[4,320,512]{2,1,0:T(8,128)(2,1)S(1)} %bitcast.134), channel_id=1, source_target_pairs={{0,4},{4,0},{8,12},{12,8},{16,20},{20,16},{24,28},{28,24},{1,5},{5... | collective-permute-start | bytes 3932168 | tf_op jit(solution)/shard_map/ppermute | solution.py:40
  79.6 23.4 %collective-permute-start.16 = (bf16[320,1536]{1,0:T(8,128)(2,1)S(1)}, bf16[320,1536]{1,0:T(8,128)(2,1)S(1)}, u32[]{:S(2)}, u32[]{:S(2)}) collective-permute-start(bf16[320,1536]{1,0:T(8,128)(2,1)S(1)} %convolution_convert_fusion), channel_id=1, source_target_pairs={{0,8},{4,12},{24,16},{28,20},{1,9},{5,13},{25,17},{29,21},{2,10},{... | collective-permute-start | bytes 2949128 | tf_op jit(solution)/shard_map/ppermute | solution.py:115
  81.0 29.5 %collective-permute-start.10 = (bf16[1536,512]{1,0:T(8,128)(2,1)}, bf16[1536,512]{1,0:T(8,128)(2,1)S(1)}, u32[]{:S(2)}, u32[]{:S(2)}) collective-permute-start(bf16[1536,512]{1,0:T(8,128)(2,1)} %collective-permute-done.5), channel_id=1, source_target_pairs={{8,16},{12,20},{16,24},{20,28},{9,17},{13,21},{17,25},{21,29},{10,... | collective-permute-start | bytes 4718600 | tf_op jit(solution)/shard_map/ppermute | solution.py:74
  81.8 38.5 %collective-permute-start.11 = (bf16[1536,512]{1,0:T(8,128)(2,1)}, bf16[1536,512]{1,0:T(8,128)(2,1)S(1)}, u32[]{:S(2)}, u32[]{:S(2)}) collective-permute-start(bf16[1536,512]{1,0:T(8,128)(2,1)} %collective-permute-done.6), channel_id=1, source_target_pairs={{8,0},{12,4},{16,8},{20,12},{9,1},{13,5},{17,9},{21,13},{10,2},{14... | collective-permute-start | bytes 4718600 | tf_op jit(solution)/shard_map/ppermute | solution.py:74
  84.3 39.8 %collective-permute-start.9 = (bf16[320,1536]{1,0:T(8,128)(2,1)S(1)}, bf16[320,1536]{1,0:T(8,128)(2,1)S(1)}, u32[]{:S(2)}, u32[]{:S(2)}) collective-permute-start(bf16[320,1536]{1,0:T(8,128)(2,1)S(1)} %convolution_convert_fusion.1), channel_id=1, source_target_pairs={{0,8},{4,12},{24,16},{28,20},{1,9},{5,13},{25,17},{29,21},{2,10},{... | collective-permute-start | bytes 2949128 | tf_op jit(solution)/shard_map/ppermute | solution.py:115
  104.2 23.9 %collective-permute-start.18 = (bf16[320,1536]{1,0:T(8,128)(2,1)S(1)}, bf16[320,1536]{1,0:T(8,128)(2,1)S(1)}, u32[]{:S(2)}, u32[]{:S(2)}) collective-permute-start(bf16[320,1536]{1,0:T(8,128)(2,1)S(1)} %fusion.14), channel_id=1, source_target_pairs={{24,16},{28,20},{16,8},{20,12},{25,17},{29,21},{17,9},{21,13},{26,... | collective-permute-start | bytes 2949128 | tf_op jit(solution)/shard_map/ppermute | solution.py:117
  105.5 40.2 %collective-permute-start.17 = (bf16[320,1536]{1,0:T(8,128)(2,1)S(1)}, bf16[320,1536]{1,0:T(8,128)(2,1)S(1)}, u32[]{:S(2)}, u32[]{:S(2)}) collective-permute-start(bf16[320,1536]{1,0:T(8,128)(2,1)S(1)} %fusion.14), channel_id=1, source_target_pairs={{0,8},{4,12},{8,16},{12,20},{1,9},{5,13},{9,17},{13,21},{2,10},{6,... | collective-permute-start | bytes 2949128 | tf_op jit(solution)/shard_map/ppermute | solution.py:117
  124.1 42.8 %collective-permute-start.14 = (bf16[1536,512]{1,0:T(8,128)(2,1)S(1)}, bf16[1536,512]{1,0:T(8,128)(2,1)S(1)}, u32[]{:S(2)}, u32[]{:S(2)}) collective-permute-start(bf16[1536,512]{1,0:T(8,128)(2,1)S(1)} %collective-permute-done.10), channel_id=1, source_target_pairs={{16,24},{20,28},{17,25},{21,29},{18,26},{22,30},{19,27},{23,31}} | collective-permute-start | bytes 4718600 | tf_op jit(solution)/shard_map/ppermute | solution.py:74
  124.8 42.0 %collective-permute-start.15 = (bf16[1536,512]{1,0:T(8,128)(2,1)S(1)}, bf16[1536,512]{1,0:T(8,128)(2,1)S(1)}, u32[]{:S(2)}, u32[]{:S(2)}) collective-permute-start(bf16[1536,512]{1,0:T(8,128)(2,1)S(1)} %collective-permute-done.11), channel_id=1, source_target_pairs={{8,0},{12,4},{9,1},{13,5},{10,2},{14,6},{11,3},{15,7}} | collective-permute-start | bytes 4718600 | tf_op jit(solution)/shard_map/ppermute | solution.py:74
  127.3 23.1 %collective-permute-start.13 = (bf16[320,1536]{1,0:T(8,128)(2,1)S(1)}, bf16[320,1536]{1,0:T(8,128)(2,1)S(1)}, u32[]{:S(2)}, u32[]{:S(2)}) collective-permute-start(bf16[320,1536]{1,0:T(8,128)(2,1)S(1)} %add_convert_fusion.2), channel_id=1, source_target_pairs={{24,16},{28,20},{16,8},{20,12},{25,17},{29,21},{17,9},{21,13},{26,... | collective-permute-start | bytes 2949128 | tf_op jit(solution)/shard_map/ppermute | solution.py:117
  128.1 38.8 %collective-permute-start.12 = (bf16[320,1536]{1,0:T(8,128)(2,1)S(1)}, bf16[320,1536]{1,0:T(8,128)(2,1)S(1)}, u32[]{:S(2)}, u32[]{:S(2)}) collective-permute-start(bf16[320,1536]{1,0:T(8,128)(2,1)S(1)} %add_convert_fusion.2), channel_id=1, source_target_pairs={{0,8},{4,12},{8,16},{12,20},{1,9},{5,13},{9,17},{13,21},{2,10},{6,... | collective-permute-start | bytes 2949128 | tf_op jit(solution)/shard_map/ppermute | solution.py:117
  146.9 38.2 %collective-permute-start.20 = (bf16[320,1536]{1,0:T(8,128)(2,1)S(1)}, bf16[320,1536]{1,0:T(8,128)(2,1)S(1)}, u32[]{:S(2)}, u32[]{:S(2)}) collective-permute-start(bf16[320,1536]{1,0:T(8,128)(2,1)S(1)} %fusion.15), channel_id=1, source_target_pairs={{24,16},{28,20},{16,8},{20,12},{8,0},{12,4},{25,17},{29,21},{17,9}... | collective-permute-start | bytes 2949128 | tf_op jit(solution)/shard_map/ppermute | solution.py:117
  150.4 38.7 %collective-permute-start.19 = (bf16[320,1536]{1,0:T(8,128)(2,1)}, bf16[320,1536]{1,0:T(8,128)(2,1)S(1)}, u32[]{:S(2)}, u32[]{:S(2)}) collective-permute-start(bf16[320,1536]{1,0:T(8,128)(2,1)} %fusion.13), channel_id=1, source_target_pairs={{0,8},{4,12},{8,16},{12,20},{16,24},{20,28},{1,9},{5,13},{9,17},{1... | collective-permute-start | bytes 2949128 | tf_op jit(solution)/shard_map/ppermute | solution.py:117
  169.2 35.2 %collective-permute-start.26 = (bf16[320,1536]{1,0:T(8,128)(2,1)S(1)}, bf16[320,1536]{1,0:T(8,128)(2,1)S(1)}, u32[]{:S(2)}, u32[]{:S(2)}) collective-permute-start(bf16[320,1536]{1,0:T(8,128)(2,1)S(1)} %add_convert_fusion), channel_id=1, source_target_pairs={{24,16},{28,20},{16,8},{20,12},{8,0},{12,4},{25,17},{29,21},{17,9}... | collective-permute-start | bytes 2949128 | tf_op jit(solution)/shard_map/ppermute | solution.py:117
  170.5 37.3 %collective-permute-start.25 = (bf16[320,1536]{1,0:T(8,128)(2,1)S(1)}, bf16[320,1536]{1,0:T(8,128)(2,1)S(1)}, u32[]{:S(2)}, u32[]{:S(2)}) collective-permute-start(bf16[320,1536]{1,0:T(8,128)(2,1)S(1)} %add_convert_fusion.1), channel_id=1, source_target_pairs={{0,8},{4,12},{8,16},{12,20},{16,24},{20,28},{1,9},{5,13},{9,17},{1... | collective-permute-start | bytes 2949128 | tf_op jit(solution)/shard_map/ppermute | solution.py:117
  190.6 2.1 collective-permute-start.21
  194.0 13.8 %collective-permute-start.24 = (bf16[80,2048]{1,0:T(8,128)(2,1)S(1)}, bf16[80,2048]{1,0:T(8,128)(2,1)S(1)}, u32[]{:S(2)}, u32[]{:S(2)}) collective-permute-start(bf16[80,2048]{1,0:T(8,128)(2,1)S(1)} %get-tuple-element.72), channel_id=1, source_target_pairs={{0,3},{1,2},{2,1},{3,0},{4,7},{5,6},{6,5},{7,4},{8,11},{9,10},{10,... | collective-permute-start | bytes 983048 | tf_op jit(solution)/shard_map/ppermute | solution.py:68
  197.1 14.9 %collective-permute-start.23 = (bf16[80,2048]{1,0:T(8,128)(2,1)S(1)}, bf16[80,2048]{1,0:T(8,128)(2,1)S(1)}, u32[]{:S(2)}, u32[]{:S(2)}) collective-permute-start(bf16[80,2048]{1,0:T(8,128)(2,1)S(1)} %get-tuple-element.73), channel_id=1, source_target_pairs={{0,2},{1,3},{2,0},{3,1},{4,6},{5,7},{6,4},{7,5},{8,10},{9,11},{10,... | collective-permute-start | bytes 983048 | tf_op jit(solution)/shard_map/ppermute | solution.py:68
  198.3 13.8 %collective-permute-start.22 = (bf16[80,2048]{1,0:T(8,128)(2,1)S(1)}, bf16[80,2048]{1,0:T(8,128)(2,1)S(1)}, u32[]{:S(2)}, u32[]{:S(2)}) collective-permute-start(bf16[80,2048]{1,0:T(8,128)(2,1)S(1)} %get-tuple-element.74), channel_id=1, source_target_pairs={{0,1},{1,0},{2,3},{3,2},{4,5},{5,4},{6,7},{7,6},{8,9},{9,8},{10,11... | collective-permute-start | bytes 983048 | tf_op jit(solution)/shard_map/ppermute | solution.py:68
  208.6 4.7 %collective-permute-start.27 = (bf16[320,768]{1,0:T(8,128)(2,1)S(1)}, bf16[320,768]{1,0:T(8,128)(2,1)S(1)}, u32[]{:S(2)}, u32[]{:S(2)}) collective-permute-start(bf16[320,768]{1,0:T(8,128)(2,1)S(1)} %fusion.21), channel_id=1, source_target_pairs={{0,4},{4,0},{8,12},{12,8},{16,20},{20,16},{24,28},{28,24},{1,5},{5... | collective-permute-start | bytes 1474568 | tf_op jit(solution)/shard_map/ppermute | solution.py:40
  214.8 11.6 %collective-permute-start.30 = (bf16[80,2048]{1,0:T(8,128)(2,1)S(1)}, bf16[80,2048]{1,0:T(8,128)(2,1)S(1)}, u32[]{:S(2)}, u32[]{:S(2)}) collective-permute-start(bf16[80,2048]{1,0:T(8,128)(2,1)S(1)} %get-tuple-element.76), channel_id=1, source_target_pairs={{0,3},{1,2},{2,1},{3,0},{4,7},{5,6},{6,5},{7,4},{8,11},{9,10},{10,... | collective-permute-start | bytes 983048 | tf_op jit(solution)/shard_map/ppermute | solution.py:68
  217.2 15.2 %collective-permute-start.29 = (bf16[80,2048]{1,0:T(8,128)(2,1)S(1)}, bf16[80,2048]{1,0:T(8,128)(2,1)S(1)}, u32[]{:S(2)}, u32[]{:S(2)}) collective-permute-start(bf16[80,2048]{1,0:T(8,128)(2,1)S(1)} %get-tuple-element.77), channel_id=1, source_target_pairs={{0,2},{1,3},{2,0},{3,1},{4,6},{5,7},{6,4},{7,5},{8,10},{9,11},{10,... | collective-permute-start | bytes 983048 | tf_op jit(solution)/shard_map/ppermute | solution.py:68
  218.3 14.1 %collective-permute-start.28 = (bf16[80,2048]{1,0:T(8,128)(2,1)S(1)}, bf16[80,2048]{1,0:T(8,128)(2,1)S(1)}, u32[]{:S(2)}, u32[]{:S(2)}) collective-permute-start(bf16[80,2048]{1,0:T(8,128)(2,1)S(1)} %get-tuple-element.78), channel_id=1, source_target_pairs={{0,1},{1,0},{2,3},{3,2},{4,5},{5,4},{6,7},{7,6},{8,9},{9,8},{10,11... | collective-permute-start | bytes 983048 | tf_op jit(solution)/shard_map/ppermute | solution.py:68
  233.2 2.0 collective-permute-start.31
  (4 other events, 14.2 us)

commit v5 on v4

--- a/solution.py
+++ b/solution.py
@@ -11,12 +11,12 @@
 
 
 def ranks_of(ids, groups):
-    flat = ids.reshape(-1)
-    count = flat.shape[0]
-    onehot = (flat[:, None] == jnp.arange(groups, dtype=jnp.int32)).astype(BF16)
-    before = (jnp.arange(count)[:, None] > jnp.arange(count)[None, :]).astype(BF16)
-    ranks = jnp.dot(before, onehot, preferred_element_type=F32)
-    return jnp.sum(ranks * onehot.astype(F32), axis=1).reshape(ids.shape)
+    flat = ids.T.reshape(-1)
+    places = jnp.arange(flat.shape[0])
+    onehot = (jnp.arange(groups, dtype=jnp.int32)[:, None] == flat[None, :]).astype(BF16)
+    before = (places[:, None] < places[None, :]).astype(BF16)
+    ranks = jnp.dot(onehot, before, preferred_element_type=F32)
+    return jnp.sum(ranks * onehot.astype(F32), axis=0).reshape(ids.shape[1], ids.shape[0])
 
 
 def take(array, index):
@@ -45,7 +45,7 @@
     def split(array):
         return [take(array, which) for which in range(array.shape[0])]
 
-    notes = jnp.concatenate([expert_ids.astype(F32).T, ranks_of(expert_ids, groups).T], axis=0)
+    notes = jnp.concatenate([expert_ids.astype(F32).T, ranks_of(expert_ids, groups)], axis=0)
     notes = jnp.pad(notes, ((0, NOTE_ROWS - 2 * top), (0, width - tok_count))).astype(BF16)
     sent = jnp.concatenate([tokens, jnp.tile(notes, (1, n_dp))], axis=0)
     arrived = lax.all_to_all(sent, "dp", split_axis=1, concat_axis=0, tiled=True)
@@ -136,7 +136,7 @@
 
     def outputs_of(part):
         below, above = sums[part]
-        total = product(part, plane) + below.astype(F32) + above.astype(F32)
+        total = lax.optimization_barrier(product(part, plane)) + below.astype(F32) + above.astype(F32)
         hidden = (jax.nn.silu(total[:, :half]) * total[:, half:]).astype(BF16)
         ours = jnp.dot(hidden, out_weight[0], preferred_element_type=F32)
         return (ours + jnp.dot(other(hidden), out_weight[1], preferred_element_type=F32)).astype(BF16)

time: 241 us -> 239 us (level)
  waiting for transfers between devices: 105 us -> 101 us
    ppermute x9, waiting for transfers between devices: 44.2 us -> 40.3 us  [across(): lax.ppermute(blocks[k], 'expert', [(i, i ^ k) for i in range(groups)])]
  transfers between devices with their start and end apart: 33 -> 33, of which waited for: 17 -> 20; matrix products, arithmetic and copies ran while one was open for 15% -> 15% of each run, Pallas kernels for 0% -> 0%
where the time goes in v5:
time: 239 us; the launch traced here: 235 us
  waiting for transfers between devices  101 us (42%)
  starting transfers between devices  87.9 us (37%)
  matrix products  22.5 us (9%)
  other arithmetic  16 us (7%)
  local copies, waits for them, and re-layouts  7.25 us (3%)
    ppermute x4, starting transfers between devices, send_on(): lax.ppermute(sending[0], 'dp', upward)  46.5 us
    ppermute x9, waiting for transfers between devices, across(): lax.ppermute(blocks[k], 'expert', [(i, i ^ k) for i in range(groups)])  40.3 us
    ppermute x2, waiting for transfers between devices, send_on(): both = lax.ppermute(sending[0], 'dp', upward + downward)  18.2 us
    all_to_all x1, waiting for transfers between devices, on_device(): lax.all_to_all(sent, 'dp', split_axis=1, concat_axis=0, tiled=True)  13.2 us
    dot_general x10, matrix products, product(): jnp.dot(take(rows[part], target % planes), in_weight, preferred_element_t...  11.9 us
    ppermute x9, starting transfers between devices, across(): lax.ppermute(blocks[k], 'expert', [(i, i ^ k) for i in range(groups)])  10.9 us
    ppermute x4, waiting for transfers between devices, send_on(): lax.ppermute(sending[1], 'dp', downward)  9.36 us
    ppermute x3, waiting for transfers between devices, pass_on(): lax.ppermute(above, 'dp', downward)  8.27 us
  transfers between devices with their start and end apart: 33, of which 20 were waited for; matrix products, arithmetic and copies ran while one was open for 15% of the time, Pallas kernels for 0%

profile of v5, /device:TPU:0, one launch (start us, length us, event | category | flops | bytes accessed | tf_op | source)
XLA Modules:
  0.0 235.3 jit_solution(9604358553936806494)
XLA Ops:
  1.6 1.6 copy.9
  5.0 6.3 %all-to-all-start = ((bf16[136,8,512]{2,0,1:T(8,128)(2,1)}), bf16[136,8,512]{2,0,1:T(8,128)(2,1)S(1)}, u32[]{:S(2)}, u32[]{:S(2)}) async-start(bf16[136,8,512]{2,0,1:T(8,128)(2,1)} %pad_maximum_fusion.6), calls=%async_computation | async-start | bytes 2228224 | tf_op jit(solution)/shard_map/all_to_all | solution.py:51
  11.3 2.0 dynamic-slice_bitcast_fusion.6
  16.4 5.7 %collective-permute-start.5 = (bf16[1536,512]{1,0:T(8,128)(2,1)}, bf16[1536,512]{1,0:T(8,128)(2,1)}, u32[]{:S(2)}, u32[]{:S(2)}) collective-permute-start(bf16[1536,512]{1,0:T(8,128)(2,1)} %bitcast.23), channel_id=1, source_target_pairs={{0,8},{4,12},{8,16},{12,20},{16,24},{20,28},{1,9},{5,13},{9,17},{1... | collective-permute-start | bytes 4718600 | tf_op jit(solution)/shard_map/ppermute | solution.py:74
  23.3 3.3 %pad_maximum_fusion.2 = bf16[1024,1536]{1,0:T(8,128)(2,1)} fusion(bf16[512,1536]{1,0:T(8,128)(2,1)} %collective-permute-done, bf16[512,768]{1,0:T(8,128)(2,1)S(1)} %get-tuple-element.69, bf16[512,768]{1,0:T(8,128)(2,1)S(1)} %get-tuple-element.128), kind=kLoop, calls=%fused_computation.12 | loop fusion | flops 9437184 | bytes 6291456 | tf_op jit(solution)/shard_map/concatenate | solution.py:57
  26.6 13.2 %all-to-all-done = bf16[136,8,512]{2,0,1:T(8,128)(2,1)S(1)} async-done(((bf16[136,8,512]{2,0,1:T(8,128)(2,1)}), bf16[136,8,512]{2,0,1:T(8,128)(2,1)S(1)}, u32[]{:S(2)}, u32[]{:S(2)}) %all-to-all-start) | async-done | bytes 1114144 | tf_op jit(solution)/shard_map/all_to_all | solution.py:51
  40.2 2.5 %collective-permute-start.4 = (bf16[8,80,512]{2,1,0:T(8,128)(2,1)S(1)}, bf16[8,80,512]{2,1,0:T(8,128)(2,1)S(1)}, u32[]{:S(2)}, u32[]{:S(2)}) collective-permute-start(bf16[8,80,512]{2,1,0:T(8,128)(2,1)S(1)} %convolution_convert_fusion.2), channel_id=1, source_target_pairs={{0,3},{1,2},{2,1},{3,0},{4,7},{5,6},{6,5},{7,4},{8,11},{9,10},{10,... | collective-permute-start | bytes 1966088 | tf_op jit(solution)/shard_map/ppermute | solution.py:68
  46.6 12.3 %collective-permute-done.4 = bf16[8,80,512]{2,1,0:T(8,128)(2,1)S(1)} collective-permute-done((bf16[8,80,512]{2,1,0:T(8,128)(2,1)S(1)}, bf16[8,80,512]{2,1,0:T(8,128)(2,1)S(1)}, u32[]{:S(2)}, u32[]{:S(2)}) %collective-permute-start.4) | collective-permute-done | bytes 655392 | tf_op jit(solution)/shard_map/ppermute | solution.py:68
  58.9 12.1 %collective-permute-done.3 = bf16[8,80,512]{2,1,0:T(8,128)(2,1)S(1)} collective-permute-done((bf16[8,80,512]{2,1,0:T(8,128)(2,1)}, bf16[8,80,512]{2,1,0:T(8,128)(2,1)S(1)}, u32[]{:S(2)}, u32[]{:S(2)}) %collective-permute-start.3) | collective-permute-done | bytes 655392 | tf_op jit(solution)/shard_map/ppermute | solution.py:68
  73.8 2.2 collective-permute-done.7
  77.1 3.2 %collective-permute-start.16 = (bf16[320,1536]{1,0:T(8,128)(2,1)S(1)}, bf16[320,1536]{1,0:T(8,128)(2,1)S(1)}, u32[]{:S(2)}, u32[]{:S(2)}) collective-permute-start(bf16[320,1536]{1,0:T(8,128)(2,1)S(1)} %convolution_convert_fusion), channel_id=1, source_target_pairs={{0,8},{4,12},{24,16},{28,20},{1,9},{5,13},{25,17},{29,21},{2,10},{... | collective-permute-start | bytes 2949128 | tf_op jit(solution)/shard_map/ppermute | solution.py:115
  81.1 1.3 collective-permute-start.11
  83.6 4.6 %collective-permute-start.9 = (bf16[320,1536]{1,0:T(8,128)(2,1)S(1)}, bf16[320,1536]{1,0:T(8,128)(2,1)S(1)}, u32[]{:S(2)}, u32[]{:S(2)}) collective-permute-start(bf16[320,1536]{1,0:T(8,128)(2,1)S(1)} %convolution_convert_fusion.1), channel_id=1, source_target_pairs={{0,8},{4,12},{24,16},{28,20},{1,9},{5,13},{25,17},{29,21},{2,10},{... | collective-permute-start | bytes 2949128 | tf_op jit(solution)/shard_map/ppermute | solution.py:115
  88.2 14.1 %collective-permute-done.16 = bf16[320,1536]{1,0:T(8,128)(2,1)S(1)} collective-permute-done((bf16[320,1536]{1,0:T(8,128)(2,1)S(1)}, bf16[320,1536]{1,0:T(8,128)(2,1)S(1)}, u32[]{:S(2)}, u32[]{:S(2)}) %collective-permute-start.16) | collective-permute-done | bytes 983072 | tf_op jit(solution)/shard_map/ppermute | solution.py:115
  106.1 5.0 %collective-permute-start.17 = (bf16[320,1536]{1,0:T(8,128)(2,1)S(1)}, bf16[320,1536]{1,0:T(8,128)(2,1)S(1)}, u32[]{:S(2)}, u32[]{:S(2)}) collective-permute-start(bf16[320,1536]{1,0:T(8,128)(2,1)S(1)} %fusion.13), channel_id=1, source_target_pairs={{0,8},{4,12},{8,16},{12,20},{1,9},{5,13},{9,17},{13,21},{2,10},{6,... | collective-permute-start | bytes 2949128 | tf_op jit(solution)/shard_map/ppermute | solution.py:117
  111.1 8.3 %collective-permute-done.11 = bf16[1536,512]{1,0:T(8,128)(2,1)S(1)} collective-permute-done((bf16[1536,512]{1,0:T(8,128)(2,1)}, bf16[1536,512]{1,0:T(8,128)(2,1)S(1)}, u32[]{:S(2)}, u32[]{:S(2)}) %collective-permute-start.11) | collective-permute-done | bytes 1572896 | tf_op jit(solution)/shard_map/ppermute | solution.py:74
  119.4 4.0 %collective-permute-done.9 = bf16[320,1536]{1,0:T(8,128)(2,1)S(1)} collective-permute-done((bf16[320,1536]{1,0:T(8,128)(2,1)S(1)}, bf16[320,1536]{1,0:T(8,128)(2,1)S(1)}, u32[]{:S(2)}, u32[]{:S(2)}) %collective-permute-start.9) | collective-permute-done | bytes 983072 | tf_op jit(solution)/shard_map/ppermute | solution.py:115
  124.2 1.3 collective-permute-start.15
  127.4 17.0 %collective-permute-start.12 = (bf16[320,1536]{1,0:T(8,128)(2,1)S(1)}, bf16[320,1536]{1,0:T(8,128)(2,1)S(1)}, u32[]{:S(2)}, u32[]{:S(2)}) collective-permute-start(bf16[320,1536]{1,0:T(8,128)(2,1)S(1)} %add_convert_fusion.2), channel_id=1, source_target_pairs={{0,8},{4,12},{8,16},{12,20},{1,9},{5,13},{9,17},{13,21},{2,10},{6,... | collective-permute-start | bytes 2949128 | tf_op jit(solution)/shard_map/ppermute | solution.py:117
  148.4 17.3 %collective-permute-start.19 = (bf16[320,1536]{1,0:T(8,128)(2,1)S(1)}, bf16[320,1536]{1,0:T(8,128)(2,1)S(1)}, u32[]{:S(2)}, u32[]{:S(2)}) collective-permute-start(bf16[320,1536]{1,0:T(8,128)(2,1)S(1)} %fusion.12), channel_id=1, source_target_pairs={{0,8},{4,12},{8,16},{12,20},{16,24},{20,28},{1,9},{5,13},{9,17},{1... | collective-permute-start | bytes 2949128 | tf_op jit(solution)/shard_map/ppermute | solution.py:117
  169.7 7.1 %collective-permute-start.25 = (bf16[320,1536]{1,0:T(8,128)(2,1)S(1)}, bf16[320,1536]{1,0:T(8,128)(2,1)S(1)}, u32[]{:S(2)}, u32[]{:S(2)}) collective-permute-start(bf16[320,1536]{1,0:T(8,128)(2,1)S(1)} %add_convert_fusion.1), channel_id=1, source_target_pairs={{0,8},{4,12},{8,16},{12,20},{16,24},{20,28},{1,9},{5,13},{9,17},{1... | collective-permute-start | bytes 2949128 | tf_op jit(solution)/shard_map/ppermute | solution.py:117
  176.8 1.6 select_bitcast_fusion
  178.6 2.6 %pad_maximum_fusion = bf16[4,1536,512]{2,1,0:T(8,128)(2,1)S(1)} fusion(bf16[1,1536,512]{2,1,0:T(8,128)(2,1)S(1)} %select_bitcast_fusion, bf16[1,1536,512]{2,1,0:T(8,128)(2,1)S(1)} %select_bitcast_fusion.1, bf16[1,1536,512]{2,1,0:T(8,128)(2,1)S(1)} %select_bitcast_fusion.2, bf16[1,1536,512]{2,1,0:T(8,128)(2,1)} %param.11), kind=kLoop, calls=%fused_computation | loop fusion | flops 9437184 | bytes 12582912 | tf_op jit(solution)/shard_map/stack | solution.py:133
  181.7 2.8 %collective-permute-done.20 = bf16[320,1536]{1,0:T(8,128)(2,1)S(1)} collective-permute-done((bf16[320,1536]{1,0:T(8,128)(2,1)S(1)}, bf16[320,1536]{1,0:T(8,128)(2,1)S(1)}, u32[]{:S(2)}, u32[]{:S(2)}) %collective-permute-start.20) | collective-permute-done | bytes 983072 | tf_op jit(solution)/shard_map/ppermute | solution.py:117
  184.5 3.2 %collective-permute-done.19 = bf16[320,1536]{1,0:T(8,128)(2,1)S(1)} collective-permute-done((bf16[320,1536]{1,0:T(8,128)(2,1)S(1)}, bf16[320,1536]{1,0:T(8,128)(2,1)S(1)}, u32[]{:S(2)}, u32[]{:S(2)}) %collective-permute-start.19) | collective-permute-done | bytes 983072 | tf_op jit(solution)/shard_map/ppermute | solution.py:117
  191.8 2.5 %collective-permute-start.24 = (bf16[80,2048]{1,0:T(8,128)(2,1)S(1)}, bf16[80,2048]{1,0:T(8,128)(2,1)S(1)}, u32[]{:S(2)}, u32[]{:S(2)}) collective-permute-start(bf16[80,2048]{1,0:T(8,128)(2,1)S(1)} %get-tuple-element.72), channel_id=1, source_target_pairs={{0,3},{1,2},{2,1},{3,0},{4,7},{5,6},{6,5},{7,4},{8,11},{9,10},{10,... | collective-permute-start | bytes 983048 | tf_op jit(solution)/shard_map/ppermute | solution.py:68
  196.6 6.5 %collective-permute-done.26 = bf16[320,1536]{1,0:T(8,128)(2,1)S(1)} collective-permute-done((bf16[320,1536]{1,0:T(8,128)(2,1)S(1)}, bf16[320,1536]{1,0:T(8,128)(2,1)S(1)}, u32[]{:S(2)}, u32[]{:S(2)}) %collective-permute-start.26) | collective-permute-done | bytes 983072 | tf_op jit(solution)/shard_map/ppermute | solution.py:117
  203.1 3.8 %collective-permute-done.25 = bf16[320,1536]{1,0:T(8,128)(2,1)S(1)} collective-permute-done((bf16[320,1536]{1,0:T(8,128)(2,1)S(1)}, bf16[320,1536]{1,0:T(8,128)(2,1)S(1)}, u32[]{:S(2)}, u32[]{:S(2)}) %collective-permute-start.25) | collective-permute-done | bytes 983072 | tf_op jit(solution)/shard_map/ppermute | solution.py:117
  207.8 2.1 collective-permute-done.23
  212.6 2.5 %collective-permute-start.30 = (bf16[80,2048]{1,0:T(8,128)(2,1)S(1)}, bf16[80,2048]{1,0:T(8,128)(2,1)S(1)}, u32[]{:S(2)}, u32[]{:S(2)}) collective-permute-start(bf16[80,2048]{1,0:T(8,128)(2,1)S(1)} %get-tuple-element.76), channel_id=1, source_target_pairs={{0,3},{1,2},{2,1},{3,0},{4,7},{5,6},{6,5},{7,4},{8,11},{9,10},{10,... | collective-permute-start | bytes 983048 | tf_op jit(solution)/shard_map/ppermute | solution.py:68
  216.7 7.4 %collective-permute-done.30 = bf16[80,2048]{1,0:T(8,128)(2,1)S(1)} collective-permute-done((bf16[80,2048]{1,0:T(8,128)(2,1)S(1)}, bf16[80,2048]{1,0:T(8,128)(2,1)S(1)}, u32[]{:S(2)}, u32[]{:S(2)}) %collective-permute-start.30) | collective-permute-done | bytes 327712 | tf_op jit(solution)/shard_map/ppermute | solution.py:68
  224.2 6.0 %collective-permute-done.29 = bf16[80,2048]{1,0:T(8,128)(2,1)S(1)} collective-permute-done((bf16[80,2048]{1,0:T(8,128)(2,1)S(1)}, bf16[80,2048]{1,0:T(8,128)(2,1)S(1)}, u32[]{:S(2)}, u32[]{:S(2)}) %collective-permute-start.29) | collective-permute-done | bytes 327712 | tf_op jit(solution)/shard_map/ppermute | solution.py:68
  (134 shorter events, 49.0 us)
Async XLA Ops:
  5.0 34.8 %all-to-all-start = ((bf16[136,8,512]{2,0,1:T(8,128)(2,1)}), bf16[136,8,512]{2,0,1:T(8,128)(2,1)S(1)}, u32[]{:S(2)}, u32[]{:S(2)}) async-start(bf16[136,8,512]{2,0,1:T(8,128)(2,1)} %pad_maximum_fusion.6), calls=%async_computation | async-start | bytes 2228224 | tf_op jit(solution)/shard_map/all_to_all | solution.py:51
  14.7 8.7 %collective-permute-start = (bf16[512,1536]{1,0:T(8,128)(2,1)}, bf16[512,1536]{1,0:T(8,128)(2,1)}, u32[]{:S(2)}, u32[]{:S(2)}) collective-permute-start(bf16[512,1536]{1,0:T(8,128)(2,1)} %pad_maximum_fusion.5), channel_id=1, source_target_pairs={{0,4},{4,0},{8,12},{12,8},{16,20},{20,16},{24,28},{28,24},{1,5},{5... | collective-permute-start | bytes 4718600 | tf_op jit(solution)/shard_map/ppermute | solution.py:40
  15.2 57.3 %collective-permute-start.6 = (bf16[1536,512]{1,0:T(8,128)(2,1)}, bf16[1536,512]{1,0:T(8,128)(2,1)}, u32[]{:S(2)}, u32[]{:S(2)}) collective-permute-start(bf16[1536,512]{1,0:T(8,128)(2,1)} %bitcast.23), channel_id=1, source_target_pairs={{8,0},{12,4},{16,8},{20,12},{24,16},{28,20},{9,1},{13,5},{17,9},{2... | collective-permute-start | bytes 4718600 | tf_op jit(solution)/shard_map/ppermute | solution.py:74
  16.4 56.0 %collective-permute-start.5 = (bf16[1536,512]{1,0:T(8,128)(2,1)}, bf16[1536,512]{1,0:T(8,128)(2,1)}, u32[]{:S(2)}, u32[]{:S(2)}) collective-permute-start(bf16[1536,512]{1,0:T(8,128)(2,1)} %bitcast.23), channel_id=1, source_target_pairs={{0,8},{4,12},{8,16},{12,20},{16,24},{20,28},{1,9},{5,13},{9,17},{1... | collective-permute-start | bytes 4718600 | tf_op jit(solution)/shard_map/ppermute | solution.py:74
  40.2 18.7 %collective-permute-start.4 = (bf16[8,80,512]{2,1,0:T(8,128)(2,1)S(1)}, bf16[8,80,512]{2,1,0:T(8,128)(2,1)S(1)}, u32[]{:S(2)}, u32[]{:S(2)}) collective-permute-start(bf16[8,80,512]{2,1,0:T(8,128)(2,1)S(1)} %convolution_convert_fusion.2), channel_id=1, source_target_pairs={{0,3},{1,2},{2,1},{3,0},{4,7},{5,6},{6,5},{7,4},{8,11},{9,10},{10,... | collective-permute-start | bytes 1966088 | tf_op jit(solution)/shard_map/ppermute | solution.py:68
  44.0 27.1 %collective-permute-start.3 = (bf16[8,80,512]{2,1,0:T(8,128)(2,1)}, bf16[8,80,512]{2,1,0:T(8,128)(2,1)S(1)}, u32[]{:S(2)}, u32[]{:S(2)}) collective-permute-start(bf16[8,80,512]{2,1,0:T(8,128)(2,1)} %convolution_convert_fusion.3), channel_id=1, source_target_pairs={{0,2},{1,3},{2,0},{3,1},{4,6},{5,7},{6,4},{7,5},{8,10},{9,11},{10,... | collective-permute-start | bytes 1966088 | tf_op jit(solution)/shard_map/ppermute | solution.py:68
  45.7 25.6 %collective-permute-start.2 = (bf16[8,80,512]{2,1,0:T(8,128)(2,1)}, bf16[8,80,512]{2,1,0:T(8,128)(2,1)}, u32[]{:S(2)}, u32[]{:S(2)}) collective-permute-start(bf16[8,80,512]{2,1,0:T(8,128)(2,1)} %convolution_convert_fusion.4), channel_id=1, source_target_pairs={{0,1},{1,0},{2,3},{3,2},{4,5},{5,4},{6,7},{7,6},{8,9},{9,8},{10,11... | collective-permute-start | bytes 1966088 | tf_op jit(solution)/shard_map/ppermute | solution.py:68
  72.8 3.1 %collective-permute-start.7 = (bf16[4,320,512]{2,1,0:T(8,128)(2,1)S(1)}, bf16[4,320,512]{2,1,0:T(8,128)(2,1)S(1)}, u32[]{:S(2)}, u32[]{:S(2)}) collective-permute-start(bf16[4,320,512]{2,1,0:T(8,128)(2,1)S(1)} %bitcast.142), channel_id=1, source_target_pairs={{0,4},{4,0},{8,12},{12,8},{16,20},{20,16},{24,28},{28,24},{1,5},{5... | collective-permute-start | bytes 3932168 | tf_op jit(solution)/shard_map/ppermute | solution.py:40
  73.2 9.2 %collective-permute-start.8 = (bf16[4,320,512]{2,1,0:T(8,128)(2,1)S(1)}, bf16[4,320,512]{2,1,0:T(8,128)(2,1)S(1)}, u32[]{:S(2)}, u32[]{:S(2)}) collective-permute-start(bf16[4,320,512]{2,1,0:T(8,128)(2,1)S(1)} %bitcast.139), channel_id=1, source_target_pairs={{0,4},{4,0},{8,12},{12,8},{16,20},{20,16},{24,28},{28,24},{1,5},{5... | collective-permute-start | bytes 3932168 | tf_op jit(solution)/shard_map/ppermute | solution.py:40
  77.1 25.2 %collective-permute-start.16 = (bf16[320,1536]{1,0:T(8,128)(2,1)S(1)}, bf16[320,1536]{1,0:T(8,128)(2,1)S(1)}, u32[]{:S(2)}, u32[]{:S(2)}) collective-permute-start(bf16[320,1536]{1,0:T(8,128)(2,1)S(1)} %convolution_convert_fusion), channel_id=1, source_target_pairs={{0,8},{4,12},{24,16},{28,20},{1,9},{5,13},{25,17},{29,21},{2,10},{... | collective-permute-start | bytes 2949128 | tf_op jit(solution)/shard_map/ppermute | solution.py:115
  80.4 30.8 %collective-permute-start.10 = (bf16[1536,512]{1,0:T(8,128)(2,1)}, bf16[1536,512]{1,0:T(8,128)(2,1)S(1)}, u32[]{:S(2)}, u32[]{:S(2)}) collective-permute-start(bf16[1536,512]{1,0:T(8,128)(2,1)} %collective-permute-done.5), channel_id=1, source_target_pairs={{8,16},{12,20},{16,24},{20,28},{9,17},{13,21},{17,25},{21,29},{10,... | collective-permute-start | bytes 4718600 | tf_op jit(solution)/shard_map/ppermute | solution.py:74
  81.1 38.3 %collective-permute-start.11 = (bf16[1536,512]{1,0:T(8,128)(2,1)}, bf16[1536,512]{1,0:T(8,128)(2,1)S(1)}, u32[]{:S(2)}, u32[]{:S(2)}) collective-permute-start(bf16[1536,512]{1,0:T(8,128)(2,1)} %collective-permute-done.6), channel_id=1, source_target_pairs={{8,0},{12,4},{16,8},{20,12},{9,1},{13,5},{17,9},{21,13},{10,2},{14... | collective-permute-start | bytes 4718600 | tf_op jit(solution)/shard_map/ppermute | solution.py:74
  83.6 39.8 %collective-permute-start.9 = (bf16[320,1536]{1,0:T(8,128)(2,1)S(1)}, bf16[320,1536]{1,0:T(8,128)(2,1)S(1)}, u32[]{:S(2)}, u32[]{:S(2)}) collective-permute-start(bf16[320,1536]{1,0:T(8,128)(2,1)S(1)} %convolution_convert_fusion.1), channel_id=1, source_target_pairs={{0,8},{4,12},{24,16},{28,20},{1,9},{5,13},{25,17},{29,21},{2,10},{... | collective-permute-start | bytes 2949128 | tf_op jit(solution)/shard_map/ppermute | solution.py:115
  103.6 23.9 %collective-permute-start.18 = (bf16[320,1536]{1,0:T(8,128)(2,1)S(1)}, bf16[320,1536]{1,0:T(8,128)(2,1)S(1)}, u32[]{:S(2)}, u32[]{:S(2)}) collective-permute-start(bf16[320,1536]{1,0:T(8,128)(2,1)S(1)} %fusion.13), channel_id=1, source_target_pairs={{24,16},{28,20},{16,8},{20,12},{25,17},{29,21},{17,9},{21,13},{26,... | collective-permute-start | bytes 2949128 | tf_op jit(solution)/shard_map/ppermute | solution.py:117
  106.1 38.6 %collective-permute-start.17 = (bf16[320,1536]{1,0:T(8,128)(2,1)S(1)}, bf16[320,1536]{1,0:T(8,128)(2,1)S(1)}, u32[]{:S(2)}, u32[]{:S(2)}) collective-permute-start(bf16[320,1536]{1,0:T(8,128)(2,1)S(1)} %fusion.13), channel_id=1, source_target_pairs={{0,8},{4,12},{8,16},{12,20},{1,9},{5,13},{9,17},{13,21},{2,10},{6,... | collective-permute-start | bytes 2949128 | tf_op jit(solution)/shard_map/ppermute | solution.py:117
  123.4 42.6 %collective-permute-start.14 = (bf16[1536,512]{1,0:T(8,128)(2,1)S(1)}, bf16[1536,512]{1,0:T(8,128)(2,1)S(1)}, u32[]{:S(2)}, u32[]{:S(2)}) collective-permute-start(bf16[1536,512]{1,0:T(8,128)(2,1)S(1)} %collective-permute-done.10), channel_id=1, source_target_pairs={{16,24},{20,28},{17,25},{21,29},{18,26},{22,30},{19,27},{23,31}} | collective-permute-start | bytes 4718600 | tf_op jit(solution)/shard_map/ppermute | solution.py:74
  124.2 41.8 %collective-permute-start.15 = (bf16[1536,512]{1,0:T(8,128)(2,1)S(1)}, bf16[1536,512]{1,0:T(8,128)(2,1)S(1)}, u32[]{:S(2)}, u32[]{:S(2)}) collective-permute-start(bf16[1536,512]{1,0:T(8,128)(2,1)S(1)} %collective-permute-done.11), channel_id=1, source_target_pairs={{8,0},{12,4},{9,1},{13,5},{10,2},{14,6},{11,3},{15,7}} | collective-permute-start | bytes 4718600 | tf_op jit(solution)/shard_map/ppermute | solution.py:74
  126.7 21.7 %collective-permute-start.13 = (bf16[320,1536]{1,0:T(8,128)(2,1)S(1)}, bf16[320,1536]{1,0:T(8,128)(2,1)S(1)}, u32[]{:S(2)}, u32[]{:S(2)}) collective-permute-start(bf16[320,1536]{1,0:T(8,128)(2,1)S(1)} %add_convert_fusion.2), channel_id=1, source_target_pairs={{24,16},{28,20},{16,8},{20,12},{25,17},{29,21},{17,9},{21,13},{26,... | collective-permute-start | bytes 2949128 | tf_op jit(solution)/shard_map/ppermute | solution.py:117
  127.4 38.6 %collective-permute-start.12 = (bf16[320,1536]{1,0:T(8,128)(2,1)S(1)}, bf16[320,1536]{1,0:T(8,128)(2,1)S(1)}, u32[]{:S(2)}, u32[]{:S(2)}) collective-permute-start(bf16[320,1536]{1,0:T(8,128)(2,1)S(1)} %add_convert_fusion.2), channel_id=1, source_target_pairs={{0,8},{4,12},{8,16},{12,20},{1,9},{5,13},{9,17},{13,21},{2,10},{6,... | collective-permute-start | bytes 2949128 | tf_op jit(solution)/shard_map/ppermute | solution.py:117
  145.9 38.6 %collective-permute-start.20 = (bf16[320,1536]{1,0:T(8,128)(2,1)S(1)}, bf16[320,1536]{1,0:T(8,128)(2,1)S(1)}, u32[]{:S(2)}, u32[]{:S(2)}) collective-permute-start(bf16[320,1536]{1,0:T(8,128)(2,1)S(1)} %fusion.14), channel_id=1, source_target_pairs={{24,16},{28,20},{16,8},{20,12},{8,0},{12,4},{25,17},{29,21},{17,9}... | collective-permute-start | bytes 2949128 | tf_op jit(solution)/shard_map/ppermute | solution.py:117
  148.4 39.3 %collective-permute-start.19 = (bf16[320,1536]{1,0:T(8,128)(2,1)S(1)}, bf16[320,1536]{1,0:T(8,128)(2,1)S(1)}, u32[]{:S(2)}, u32[]{:S(2)}) collective-permute-start(bf16[320,1536]{1,0:T(8,128)(2,1)S(1)} %fusion.12), channel_id=1, source_target_pairs={{0,8},{4,12},{8,16},{12,20},{16,24},{20,28},{1,9},{5,13},{9,17},{1... | collective-permute-start | bytes 2949128 | tf_op jit(solution)/shard_map/ppermute | solution.py:117
  168.4 34.7 %collective-permute-start.26 = (bf16[320,1536]{1,0:T(8,128)(2,1)S(1)}, bf16[320,1536]{1,0:T(8,128)(2,1)S(1)}, u32[]{:S(2)}, u32[]{:S(2)}) collective-permute-start(bf16[320,1536]{1,0:T(8,128)(2,1)S(1)} %add_convert_fusion), channel_id=1, source_target_pairs={{24,16},{28,20},{16,8},{20,12},{8,0},{12,4},{25,17},{29,21},{17,9}... | collective-permute-start | bytes 2949128 | tf_op jit(solution)/shard_map/ppermute | solution.py:117
  169.7 37.2 %collective-permute-start.25 = (bf16[320,1536]{1,0:T(8,128)(2,1)S(1)}, bf16[320,1536]{1,0:T(8,128)(2,1)S(1)}, u32[]{:S(2)}, u32[]{:S(2)}) collective-permute-start(bf16[320,1536]{1,0:T(8,128)(2,1)S(1)} %add_convert_fusion.1), channel_id=1, source_target_pairs={{0,8},{4,12},{8,16},{12,20},{16,24},{20,28},{1,9},{5,13},{9,17},{1... | collective-permute-start | bytes 2949128 | tf_op jit(solution)/shard_map/ppermute | solution.py:117
  188.3 2.1 collective-permute-start.21
  191.8 15.1 %collective-permute-start.24 = (bf16[80,2048]{1,0:T(8,128)(2,1)S(1)}, bf16[80,2048]{1,0:T(8,128)(2,1)S(1)}, u32[]{:S(2)}, u32[]{:S(2)}) collective-permute-start(bf16[80,2048]{1,0:T(8,128)(2,1)S(1)} %get-tuple-element.72), channel_id=1, source_target_pairs={{0,3},{1,2},{2,1},{3,0},{4,7},{5,6},{6,5},{7,4},{8,11},{9,10},{10,... | collective-permute-start | bytes 983048 | tf_op jit(solution)/shard_map/ppermute | solution.py:68
  195.5 14.4 %collective-permute-start.23 = (bf16[80,2048]{1,0:T(8,128)(2,1)S(1)}, bf16[80,2048]{1,0:T(8,128)(2,1)S(1)}, u32[]{:S(2)}, u32[]{:S(2)}) collective-permute-start(bf16[80,2048]{1,0:T(8,128)(2,1)S(1)} %get-tuple-element.73), channel_id=1, source_target_pairs={{0,2},{1,3},{2,0},{3,1},{4,6},{5,7},{6,4},{7,5},{8,10},{9,11},{10,... | collective-permute-start | bytes 983048 | tf_op jit(solution)/shard_map/ppermute | solution.py:68
  196.0 13.9 %collective-permute-start.22 = (bf16[80,2048]{1,0:T(8,128)(2,1)S(1)}, bf16[80,2048]{1,0:T(8,128)(2,1)S(1)}, u32[]{:S(2)}, u32[]{:S(2)}) collective-permute-start(bf16[80,2048]{1,0:T(8,128)(2,1)S(1)} %get-tuple-element.74), channel_id=1, source_target_pairs={{0,1},{1,0},{2,3},{3,2},{4,5},{5,4},{6,7},{7,6},{8,9},{9,8},{10,11... | collective-permute-start | bytes 983048 | tf_op jit(solution)/shard_map/ppermute | solution.py:68
  207.7 3.5 %collective-permute-start.27 = (bf16[320,768]{1,0:T(8,128)(2,1)S(1)}, bf16[320,768]{1,0:T(8,128)(2,1)S(1)}, u32[]{:S(2)}, u32[]{:S(2)}) collective-permute-start(bf16[320,768]{1,0:T(8,128)(2,1)S(1)} %fusion.20), channel_id=1, source_target_pairs={{0,4},{4,0},{8,12},{12,8},{16,20},{20,16},{24,28},{28,24},{1,5},{5... | collective-permute-start | bytes 1474568 | tf_op jit(solution)/shard_map/ppermute | solution.py:40
  212.6 11.6 %collective-permute-start.30 = (bf16[80,2048]{1,0:T(8,128)(2,1)S(1)}, bf16[80,2048]{1,0:T(8,128)(2,1)S(1)}, u32[]{:S(2)}, u32[]{:S(2)}) collective-permute-start(bf16[80,2048]{1,0:T(8,128)(2,1)S(1)} %get-tuple-element.76), channel_id=1, source_target_pairs={{0,3},{1,2},{2,1},{3,0},{4,7},{5,6},{6,5},{7,4},{8,11},{9,10},{10,... | collective-permute-start | bytes 983048 | tf_op jit(solution)/shard_map/ppermute | solution.py:68
  215.5 14.7 %collective-permute-start.29 = (bf16[80,2048]{1,0:T(8,128)(2,1)S(1)}, bf16[80,2048]{1,0:T(8,128)(2,1)S(1)}, u32[]{:S(2)}, u32[]{:S(2)}) collective-permute-start(bf16[80,2048]{1,0:T(8,128)(2,1)S(1)} %get-tuple-element.77), channel_id=1, source_target_pairs={{0,2},{1,3},{2,0},{3,1},{4,6},{5,7},{6,4},{7,5},{8,10},{9,11},{10,... | collective-permute-start | bytes 983048 | tf_op jit(solution)/shard_map/ppermute | solution.py:68
  216.1 14.2 %collective-permute-start.28 = (bf16[80,2048]{1,0:T(8,128)(2,1)S(1)}, bf16[80,2048]{1,0:T(8,128)(2,1)S(1)}, u32[]{:S(2)}, u32[]{:S(2)}) collective-permute-start(bf16[80,2048]{1,0:T(8,128)(2,1)S(1)} %get-tuple-element.78), channel_id=1, source_target_pairs={{0,1},{1,0},{2,3},{3,2},{4,5},{5,4},{6,7},{7,6},{8,9},{9,8},{10,11... | collective-permute-start | bytes 983048 | tf_op jit(solution)/shard_map/ppermute | solution.py:68
  231.1 2.0 collective-permute-start.31
  (4 other events, 14.2 us)
